TPU v7x, 32 devices: a whole 2x2x4 slice. The times are simulated.
32 devices in a mesh: dp: 4 (over y, x), fsdp: 8 (over z, core).
Axes of the slice: x: 2, y: 2, z: 4, core: 2. Of those that a mesh axis runs over, the one named last changes fastest.
Arguments:
- tokens: bfloat16 [65536, 512], P(('dp', 'fsdp')), may hold values from -6 to 6
- present: int32 [65536], P(('dp', 'fsdp')), may hold values 0 or 1
- lengths: int32 [32, 4], P(('dp', 'fsdp')), may hold values from 1 to 1024, 2048 in all within a row
- conv_w: bfloat16 [4608, 512], P(('dp', 'fsdp')), may hold values from -0.09375 to 0.09375
- conv_b: bfloat16 [512], P(('dp', 'fsdp')), may hold values from -3 to 3
- gain_one: bfloat16 [512], P(('dp', 'fsdp')), may hold values from 0.099609375 to 1.8984375
- shift_one: bfloat16 [512], P(('dp', 'fsdp')), may hold values from -2 to 2
- w_in: bfloat16 [512, 2048], P(('dp', 'fsdp')), may hold values from -0.25 to 0.25
- b_in: bfloat16 [2048], P(('dp', 'fsdp')), may hold values from -3 to 3
- w_out: bfloat16 [2048, 512], P(('dp', 'fsdp')), may hold values from -0.125 to 0.125
- b_out: bfloat16 [512], P(('dp', 'fsdp')), may hold values from -3 to 3
- gain_two: bfloat16 [512], P(('dp', 'fsdp')), may hold values from 0.099609375 to 1.8984375
- shift_two: bfloat16 [512], P(('dp', 'fsdp')), may hold values from -2 to 2
- cotangent: bfloat16 [65536, 512], P(('dp', 'fsdp')), may hold values from -6 to 6
Outputs:
- mixed: bfloat16 [65536, 512], P(('dp', 'fsdp'))
- d_tokens: float32 [65536, 512], P(('dp', 'fsdp'))
- d_conv_w: float32 [4608, 512], P(('dp', 'fsdp'))
- d_conv_b: float32 [512], P(('dp', 'fsdp'))
- d_gain_one: float32 [512], P(('dp', 'fsdp'))
- d_shift_one: float32 [512], P(('dp', 'fsdp'))
- d_w_in: float32 [512, 2048], P(('dp', 'fsdp'))
- d_b_in: float32 [2048], P(('dp', 'fsdp'))
- d_w_out: float32 [2048, 512], P(('dp', 'fsdp'))
- d_b_out: float32 [512], P(('dp', 'fsdp'))
- d_gain_two: float32 [512], P(('dp', 'fsdp'))
- d_shift_two: float32 [512], P(('dp', 'fsdp'))
Inputs may be any that keep to these rules, and one draw needn't show every extreme that they name: Each row gives the lengths of the 4 windows that fill one device's 2048 rows end to end, in order; they sum to 2048 and one of them is 1024.
All inputs are finite; a program needn't handle non-finite values. No bound on the sum of `present` on one device may be relied on, other than what follows from the above.
Results may differ from a plain program's by a relative error of at most 0.0064.
Values may be sent and summed in bfloat16 or wider, within the bound.
No kernel may reach another device: no remote copies, remote signals or barrier semaphores. Data moves between devices by JAX's collectives and lax.ppermute only.
A program may use at most 192 MiB of HBM per device.

v0:
```python
import jax
import jax.numpy as jnp
from jax import lax
from jax.sharding import PartitionSpec as P

KERNEL_TAPS = 9
DILATION_STEP = 8


EPSILON = 1e-05


def layer_norm(values, scales, offset):
    center = jnp.mean(values, axis=-1, keepdims=True)
    shifted = values - center
    second = jnp.mean(shifted * shifted, axis=-1, keepdims=True)
    return shifted * lax.rsqrt(second + EPSILON) * scales + offset


def gelu_exact(values):
    return jax.nn.gelu(values, approximate=False)


def tap_masks(length_row, row_count):
    window_ends = jnp.cumsum(length_row)
    window_starts = window_ends - length_row
    token_position = jnp.arange(row_count, dtype=jnp.int32)
    inside = (token_position[:, None] >= window_starts[None, :]) & (
        token_position[:, None] < window_ends[None, :]
    )
    first_row = jnp.sum(jnp.where(inside, window_starts[None, :], 0), axis=1)
    last_row = jnp.sum(jnp.where(inside, window_ends[None, :], 0), axis=1)
    tap_valid = []
    for kernel_tap_index in range(KERNEL_TAPS):
        target_position = token_position + (kernel_tap_index - KERNEL_TAPS // 2) * DILATION_STEP
        tap_valid.append((target_position >= first_row) & (target_position < last_row))
    return jnp.stack(tap_valid)


def shifted_stack(values, tap_valid):
    receptive_reach = KERNEL_TAPS // 2 * DILATION_STEP
    row_count = values.shape[0]
    padded = jnp.pad(values, ((receptive_reach, receptive_reach), (0, 0)))
    pieces = []
    for kernel_tap_index in range(KERNEL_TAPS):
        window_begin = kernel_tap_index * DILATION_STEP
        window = padded[window_begin : window_begin + row_count]
        pieces.append(
            jnp.where(tap_valid[kernel_tap_index][:, None], window, jnp.zeros_like(window))
        )
    return jnp.concatenate(pieces, axis=1)


def unshift_sum(grads, tap_valid, feature_count):
    receptive_reach = KERNEL_TAPS // 2 * DILATION_STEP
    row_count = grads.shape[0]
    total = jnp.zeros((row_count + 2 * receptive_reach, feature_count), jnp.float32)
    for kernel_tap_index in range(KERNEL_TAPS):
        block = grads[:, kernel_tap_index * feature_count : (kernel_tap_index + 1) * feature_count]
        block = jnp.where(tap_valid[kernel_tap_index][:, None], block, 0.0)
        window_begin = kernel_tap_index * DILATION_STEP
        total = total + jnp.pad(block, ((window_begin, 2 * receptive_reach - window_begin), (0, 0)))
    return total[receptive_reach : receptive_reach + row_count]


def contract_rows(left, right):
    return lax.dot_general(
        left, right, (((0,), (0,)), ((), ())), preferred_element_type=jnp.float32
    )


def contract_cols(left, right):
    return lax.dot_general(
        left, right, (((1,), (1,)), ((), ())), preferred_element_type=jnp.float32
    )


def on_device(
    tokens,
    present,
    lengths,
    conv_w,
    conv_b,
    gain_one,
    shift_one,
    w_in,
    b_in,
    w_out,
    b_out,
    gain_two,
    shift_two,
    cotangent,
):
    row_count = tokens.shape[0]
    feature_count = tokens.shape[1]
    tap_valid = tap_masks(lengths[0], row_count)
    keep_rows = present[:, None] > 0
    masked = jnp.where(keep_rows, tokens, jnp.zeros_like(tokens))
    stacked = shifted_stack(masked, tap_valid)
    inputs = tokens.astype(jnp.float32)
    gathered = (
        lax.all_gather(w_in, ("dp", "fsdp"), axis=0, tiled=True),
        lax.all_gather(w_out, ("dp", "fsdp"), axis=0, tiled=True),
        lax.all_gather(conv_b, ("dp", "fsdp"), axis=0, tiled=True),
        lax.all_gather(gain_one, ("dp", "fsdp"), axis=0, tiled=True),
        lax.all_gather(shift_one, ("dp", "fsdp"), axis=0, tiled=True),
        lax.all_gather(b_in, ("dp", "fsdp"), axis=0, tiled=True),
        lax.all_gather(b_out, ("dp", "fsdp"), axis=0, tiled=True),
        lax.all_gather(gain_two, ("dp", "fsdp"), axis=0, tiled=True),
        lax.all_gather(shift_two, ("dp", "fsdp"), axis=0, tiled=True),
    )
    (
        full_in,
        full_out,
        bias_conv,
        scale_one,
        offset_one,
        bias_in,
        bias_out,
        scale_two,
        offset_two,
    ) = gathered
    columns = stacked
    conv_sum = jnp.dot(
        columns,
        lax.all_gather(conv_w, ("dp", "fsdp"), axis=0, tiled=True),
        preferred_element_type=jnp.float32,
    )
    conv_pre = conv_sum + bias_conv.astype(jnp.float32)

    def first_piece(conv_values, scales, offset):
        return inputs + layer_norm(gelu_exact(conv_values), scales, offset)

    hidden_full, first_back = jax.vjp(
        first_piece, conv_pre, scale_one.astype(jnp.float32), offset_one.astype(jnp.float32)
    )
    hidden = hidden_full.astype(jnp.bfloat16)
    inner = jnp.dot(hidden, full_in, preferred_element_type=jnp.float32) + bias_in.astype(
        jnp.float32
    )
    active_full, active_back = jax.vjp(gelu_exact, inner)
    active = active_full.astype(jnp.bfloat16)
    outer = jnp.dot(active, full_out, preferred_element_type=jnp.float32) + bias_out.astype(
        jnp.float32
    )
    normed, second_back = jax.vjp(
        layer_norm, outer, scale_two.astype(jnp.float32), offset_two.astype(jnp.float32)
    )
    mixed = (hidden.astype(jnp.float32) + normed).astype(jnp.bfloat16)
    upstream = cotangent.astype(jnp.float32)
    d_outer, d_scale_two, d_offset_two = second_back(upstream)
    d_outer_low = d_outer.astype(jnp.bfloat16)
    back_in, back_out = (
        lax.all_gather(w_in, ("dp", "fsdp"), axis=0, tiled=True),
        lax.all_gather(w_out, ("dp", "fsdp"), axis=0, tiled=True),
    )
    d_bias_out = jnp.sum(d_outer_low.astype(jnp.float32), axis=0)
    d_weight_out = contract_rows(active, d_outer_low)
    d_active = contract_cols(d_outer_low, back_out)
    (d_inner,) = active_back(d_active)
    d_inner_low = d_inner.astype(jnp.bfloat16)
    d_bias_in = jnp.sum(d_inner_low.astype(jnp.float32), axis=0)
    d_weight_in = contract_rows(hidden, d_inner_low)
    d_hidden = contract_cols(d_inner_low, back_in) + upstream
    d_conv, d_scale_one, d_offset_one = first_back(d_hidden)
    d_conv_low = d_conv.astype(jnp.bfloat16)
    d_bias_conv = jnp.sum(d_conv_low.astype(jnp.float32), axis=0)
    d_stacked = contract_cols(
        d_conv_low, lax.all_gather(conv_w, ("dp", "fsdp"), axis=0, tiled=True)
    )
    d_masked = unshift_sum(d_stacked, tap_valid, feature_count)
    d_tokens = d_hidden + jnp.where(keep_rows, d_masked, 0.0)
    columns = stacked
    d_conv_w = lax.psum_scatter(
        contract_rows(columns, d_conv_low), ("dp", "fsdp"), scatter_dimension=0, tiled=True
    )
    shares = (
        lax.psum_scatter(d_weight_in, ("dp", "fsdp"), scatter_dimension=0, tiled=True),
        lax.psum_scatter(d_weight_out, ("dp", "fsdp"), scatter_dimension=0, tiled=True),
        lax.psum_scatter(d_bias_conv, ("dp", "fsdp"), scatter_dimension=0, tiled=True),
        lax.psum_scatter(d_scale_one, ("dp", "fsdp"), scatter_dimension=0, tiled=True),
        lax.psum_scatter(d_offset_one, ("dp", "fsdp"), scatter_dimension=0, tiled=True),
        lax.psum_scatter(d_bias_in, ("dp", "fsdp"), scatter_dimension=0, tiled=True),
        lax.psum_scatter(d_bias_out, ("dp", "fsdp"), scatter_dimension=0, tiled=True),
        lax.psum_scatter(d_scale_two, ("dp", "fsdp"), scatter_dimension=0, tiled=True),
        lax.psum_scatter(d_offset_two, ("dp", "fsdp"), scatter_dimension=0, tiled=True),
    )
    (
        share_in,
        share_out,
        share_conv_b,
        share_scale_one,
        share_offset_one,
        share_bias_in,
        share_bias_out,
        share_scale_two,
        share_offset_two,
    ) = shares
    return (
        mixed,
        d_tokens,
        d_conv_w,
        share_conv_b,
        share_scale_one,
        share_offset_one,
        share_in,
        share_bias_in,
        share_out,
        share_bias_out,
        share_scale_two,
        share_offset_two,
    )


def solution(mesh):
    in_specs = (
        P(("dp", "fsdp"), None),
        P(("dp", "fsdp")),
        P(("dp", "fsdp"), None),
        P(("dp", "fsdp"), None),
        P(("dp", "fsdp")),
        P(("dp", "fsdp")),
        P(("dp", "fsdp")),
        P(("dp", "fsdp"), None),
        P(("dp", "fsdp")),
        P(("dp", "fsdp"), None),
        P(("dp", "fsdp")),
        P(("dp", "fsdp")),
        P(("dp", "fsdp")),
        P(("dp", "fsdp"), None),
    )
    out_specs = (
        P(("dp", "fsdp"), None),
        P(("dp", "fsdp"), None),
        P(("dp", "fsdp"), None),
        P(("dp", "fsdp")),
        P(("dp", "fsdp")),
        P(("dp", "fsdp")),
        P(("dp", "fsdp"), None),
        P(("dp", "fsdp")),
        P(("dp", "fsdp"), None),
        P(("dp", "fsdp")),
        P(("dp", "fsdp")),
        P(("dp", "fsdp")),
    )
    return jax.shard_map(
        on_device, mesh=mesh, in_specs=in_specs, out_specs=out_specs, check_vma=False
    )
```

profile of v0, /device:TPU:0, one launch (start us, length us, event | category | flops | bytes accessed | tf_op | source)
XLA Modules:
  0.0 650.0 jit_solution(15095893262174370278)
XLA Ops:
  11.0 2.9 copy.56
  15.8 42.4 %all-reduce.25 = (bf16[512]{0:T(512)(128)(2,1)S(1)}, bf16[512]{0:T(512)(128)(2,1)S(1)}, bf16[512]{0:T(512)(128)(2,1)S(1)}, bf16[2048]{0:T(1024)(128)(2,1)S(1)}, ...) all-reduce(bf16[512]{0:T(512)(128)(2,1)S(1)} %dynamic-update-slice,, ...), channel_id=1, replica_groups=mesh['dp'=4,'fsdp'=8] {'dp','fsdp'}, use_global_device_ids=true, to_apply=%add.10 | all-reduce | flops 5120 | bytes 20480
  59.4 3.9 copy.58
  86.7 26.1 %fusion.51 = (f32[2048]{0:T(1024)S(1)}, f32[2048,512]{0,1:T(8,128)S(1)}, f32[2048,512]{0,1:T(8,128)}, f32[2048,512]{0,1:T(8,128)}) fusion(f32[512]{0:T(512)S(1)} %convert_element_type.78, bf16[2048,4608]{0,1:T(8,128)(2,1)} %select_dynamic-update-slice_fusion, bf16[4608,512]{1,0:T(8,128)(2,1)} %all-gather.4.cloned.1.call-done), kind=kOutput, calls=%fused_computation.140 | convolution fusion | flops 9732880384 | bytes 36186112 | tf_op jit(solution)/shard_map/dot_general | solution.py:124
  117.7 18.2 %all-gather.6.cloned.1.call-done = bf16[512,2048]{1,0:T(8,128)(2,1)} async-done(((bf16[16,2048]{1,0:T(8,128)(2,1)}), bf16[512,2048]{1,0:T(8,128)(2,1)}) %all-gather.6.cloned.1.call-update) | async-done | bytes 2097168 | tf_op jit(solution)/shard_map/all_gather | solution.py:102
  135.9 44.2 %multiply_convert_fusion = (bf16[2048,2048]{1,0:T(8,128)(2,1)}, f32[2048,2048]{1,0:T(8,128)}, f32[2048,2048]{1,0:T(8,128)}) fusion(f32[2048]{0:T(1024)S(1)} %convert_element_type.83, bf16[2048,512]{0,1:T(8,128)(2,1)} %add_convert_fusion.4, bf16[512,2048]{1,0:T(8,128)(2,1)} %all-gather.6.cloned.1.call-done), kind=kOutput, calls=%fused_computation.4 | convolution fusion | flops 4571791360 | bytes 46145536 | tf_op jit(solution)/shard_map/dot_general | solution.py:138
  180.2 14.1 %all-gather.8.cloned.1.call-done = bf16[2048,512]{1,0:T(8,128)(2,1)} async-done(((bf16[64,512]{1,0:T(8,128)(2,1)}), bf16[2048,512]{1,0:T(8,128)(2,1)}) %all-gather.8.cloned.1.call-update) | async-done | bytes 2097168 | tf_op jit(solution)/shard_map/all_gather | solution.py:103
  194.3 7.8 %add_reduce_fusion = (f32[2048]{0:T(1024)S(1)}, f32[2048,512]{0,1:T(8,128)S(1)}) fusion(f32[512]{0:T(512)S(1)} %copy-done.18, bf16[2048,2048]{1,0:T(8,128)(2,1)} %get-tuple-element.77, bf16[2048,512]{1,0:T(8,128)(2,1)} %all-gather.8.cloned.1.call-done), kind=kOutput, calls=%fused_computation.72 | convolution fusion | flops 4297062400 | bytes 14690304 | tf_op jit(solution)/shard_map/dot_general | solution.py:143
  203.8 3.4 fusion.10
  207.2 4.2 convert_reduce_fusion.2
  212.8 6.9 %fusion.55 = f32[2048,512]{1,0:T(8,128)} fusion(bf16[2048,2048]{1,0:T(8,128)(2,1)S(1)} %bitcast.29, bf16[2048,512]{0,1:T(8,128)(2,1)S(1)} %get-tuple-element.74), kind=kOutput, calls=%fused_computation.143 | convolution fusion | flops 4294967296 | bytes 14680064 | tf_op jit(solution)/shard_map/dot_general | solution.py:67
  219.8 21.8 %convert_reduce_fusion = (f32[2048]{0:T(1024)S(1)}, bf16[2048,2048]{1,0:T(8,128)(2,1)}) fusion(f32[2048,2048]{1,0:T(8,128)} %get-tuple-element.78, bf16[2048,512]{0,1:T(8,128)(2,1)} %copy-done.9, bf16[2048,512]{1,0:T(8,128)(2,1)} %all-gather.8.cloned.1.call-done, f32[2048,2048]{1,0:T(8,128)} %get-tuple-element.104, f32[2048]{0:T(1024)S(1)} %convert_element_type.83), kind=kOutput, calls=%fused_computation.2 | convolution fusion | flops 4366268416 | bytes 46153728 | tf_op jit(solution)/shard_map/dot_general | solution.py:73
  241.6 10.5 %fusion.54 = f32[512,2048]{1,0:T(8,128)} fusion(bf16[2048,512]{0,1:T(8,128)(2,1)} %add_convert_fusion.4, bf16[2048,2048]{1,0:T(8,128)(2,1)} %get-tuple-element.109), kind=kOutput, calls=%fused_computation.142 | convolution fusion | flops 4294967296 | bytes 14680064 | tf_op jit(solution)/shard_map/dot_general | solution.py:67
  252.8 10.4 %fusion.49 = (f32[512]{0:T(512)S(1)}, f32[2048]{0:T(1024)S(1)}, f32[2048,512]{0,1:T(8,128)S(1)}) fusion(f32[512]{0:T(512)S(1)} %copy-done.21, f32[2048,512]{0,1:T(8,128)} %copy-done, f32[2048]{0:T(1024)S(1)} %copy-done.11, bf16[2048,512]{0,1:T(8,128)(2,1)S(1)} %copy-done.4, bf16[2048,2048]{1,0:T(8,128)(2,1)} %get-tuple-element.109, ...), kind=kOutput, calls=%fused_computation.139 | convolution fusion | flops 4302304768 | bytes 20992000 | tf_op jit(solution)/shard_map/dot_general | solution.py:73
  268.2 4.2 convert_reduce_fusion.3
  272.4 16.2 %fusion.53 = f32[4608,512]{1,0:T(8,128)} fusion(bf16[2048,4608]{0,1:T(8,128)(2,1)} %select_dynamic-update-slice_fusion, bf16[2048,512]{0,1:T(8,128)(2,1)S(1)} %get-tuple-element.76), kind=kOutput, calls=%fused_computation.141 | convolution fusion | flops 9663676416 | bytes 30408704 | tf_op jit(solution)/shard_map/dot_general | solution.py:67
  288.6 39.3 %all-reduce.24 = (f32[512]{0:T(512)S(1)}, f32[512]{0:T(512)S(1)}, f32[512]{0:T(512)S(1)}, f32[2048]{0:T(1024)S(1)}, f32[512]{0:T(512)S(1)}, /*index=5*/f32[512]{0:T(512)S(1)}, f32[512]{0:T(512)S(1)}) all-reduce(f32[512]{0:T(512)S(1)} %get-tuple-element.75, ...), channel_id=3, replica_groups=mesh['dp'=4,'fsdp'=8] {'dp','fsdp'}, use_global_device_ids=true, to_apply=%region_13.14.clone | all-reduce | flops 5120 | bytes 40960
  331.4 18.0 %fusion.56 = f32[2048,4608]{0,1:T(8,128)} fusion(bf16[4608,512]{1,0:T(8,128)(2,1)} %all-gather.4.cloned.1.call-done, bf16[2048,512]{0,1:T(8,128)(2,1)S(1)} %get-tuple-element.76), kind=kOutput, calls=%fused_computation.144 | convolution fusion | flops 9663676416 | bytes 44564480 | tf_op jit(solution)/shard_map/dot_general | solution.py:73
  349.5 23.0 %slice_select_fusion.8 = (f32[2048,512]{0,1:T(8,128)}, f32[2048,512]{0,1:T(8,128)S(1)}, f32[2048,512]{0,1:T(8,128)S(1)}, f32[2048,512]{0,1:T(8,128)}, f32[2048,5...) fusion(f32[2048,4608]{0,1:T(8,128)} %fusion.56, ...), kind=kLoop, calls=%fused_computation.47 | loop fusion | flops 9437184 | bytes 75515904 | tf_op jit(solution)/shard_map/jit(_where)/select_n | solution.py:60
  372.5 7.2 %pad_add_fusion = f32[2112,512]{0,1:T(8,128)S(1)} fusion(f32[2048,512]{0,1:T(8,128)} %get-tuple-element.88, f32[2048,512]{0,1:T(8,128)} %get-tuple-element.89, f32[2048,512]{0,1:T(8,128)} %get-tuple-element.82), kind=kLoop, calls=%fused_computation.27 | loop fusion | flops 2162688 | bytes 16908288 | tf_op jit(solution)/shard_map/add | solution.py:62
  379.8 11.8 %fusion.12 = f32[2048,512]{0,1:T(8,128)} fusion(f32[2048,512]{0,1:T(8,128)S(1)} %copy-done.3, f32[2048,512]{0,1:T(8,128)} %get-tuple-element.90, f32[2048,512]{0,1:T(8,128)S(1)} %get-tuple-element.83, f32[2048,512]{0,1:T(8,128)S(1)} %get-tuple-element.84, f32[2048,512]{0,1:T(8,128)} %get-tuple-element.85, f32[2048,512]{0,1:T(8,128)} %get-tuple-element.86, ...), kind=kLoop, calls=%fused_computation.33 | loop fusion | flops 8388608 | bytes 37750784 | tf_op jit(solution)/shard_map/add | solution.py:172
  391.6 5.5 copy.70
  400.2 103.7 %reduce-scatter.6.cloned.1.call-done = f32[16,2048]{1,0:T(8,128)} async-done(((f32[512,2048]{1,0:T(8,128)}), f32[16,2048]{1,0:T(8,128)}) %reduce-scatter.6.cloned.1.call-update) | async-done | bytes 131088 | tf_op jit(solution)/shard_map/reduce_scatter | solution.py:178
  503.9 139.1 %reduce-scatter.4.cloned.1.call-done = f32[144,512]{1,0:T(8,128)} async-done(((f32[4608,512]{1,0:T(8,128)}), f32[144,512]{1,0:T(8,128)}) %reduce-scatter.4.cloned.1.call-update) | async-done | bytes 294928 | tf_op jit(solution)/shard_map/reduce_scatter | solution.py:174
  (176 shorter events, 50.2 us)
Async XLA Ops:
  7.3 79.4 %all-gather.4.cloned.1.call-start = ((), (), s32[]{:S(2)}) async-start(), calls=%async_computation.3 | async-start | bytes 4866048 | tf_op jit(solution)/shard_map/all_gather | solution.py:126
  8.0 127.9 %all-gather.6.cloned.1.call-start = ((), (), s32[]{:S(2)}) async-start(), calls=%async_computation.4 | async-start | bytes 2162688 | tf_op jit(solution)/shard_map/all_gather | solution.py:102
  8.7 185.6 %all-gather.8.cloned.1.call-start = ((), (), s32[]{:S(2)}) async-start(), calls=%async_computation.5 | async-start | bytes 2162688 | tf_op jit(solution)/shard_map/all_gather | solution.py:103
  9.5 390.7 %reduce-scatter.8.cloned.1.call-start = ((), (), s32[]{:S(2)}) async-start(), calls=%async_computation.8 | async-start | bytes 4325376 | tf_op jit(solution)/shard_map/reduce_scatter | solution.py:179
  14.0 60.5 %copy-start.16 = (pred[2048]{0:T(1024)(128)(4,1)}, pred[2048]{0:T(1024)(128)(4,1)S(1)}, u32[]{:S(2)}) copy-start(pred[2048]{0:T(1024)(128)(4,1)S(1)} %broadcast_compare_fusion) | copy-start | bytes 6148
  58.2 28.5 %copy-start.40 = (f32[512]{0:T(512)}, f32[512]{0:T(512)S(1)}, u32[]{:S(2)}) copy-start(f32[512]{0:T(512)S(1)} %convert_element_type.78) | copy-start | bytes 6148
  58.2 56.2 %copy-start.20 = (f32[512]{0:T(512)}, f32[512]{0:T(512)S(1)}, u32[]{:S(2)}) copy-start(f32[512]{0:T(512)S(1)} %convert_element_type.79) | copy-start | bytes 6148
  64.1 12.3 %copy-start.30 = (pred[2048]{0:T(1024)(128)(4,1)}, pred[2048]{0:T(1024)(128)(4,1)S(1)}, u32[]{:S(2)}) copy-start(pred[2048]{0:T(1024)(128)(4,1)S(1)} %get-tuple-element.95) | copy-start | bytes 6148
  64.1 14.9 %copy-start.28 = (pred[2048]{0:T(1024)(128)(4,1)}, pred[2048]{0:T(1024)(128)(4,1)S(1)}, u32[]{:S(2)}) copy-start(pred[2048]{0:T(1024)(128)(4,1)S(1)} %get-tuple-element.94) | copy-start | bytes 6148
  64.1 17.4 %copy-start.26 = (pred[2048]{0:T(1024)(128)(4,1)}, pred[2048]{0:T(1024)(128)(4,1)S(1)}, u32[]{:S(2)}) copy-start(pred[2048]{0:T(1024)(128)(4,1)S(1)} %get-tuple-element.93) | copy-start | bytes 6148
  64.1 20.0 %copy-start.24 = (pred[2048]{0:T(1024)(128)(4,1)}, pred[2048]{0:T(1024)(128)(4,1)S(1)}, u32[]{:S(2)}) copy-start(pred[2048]{0:T(1024)(128)(4,1)S(1)} %get-tuple-element.92) | copy-start | bytes 6148
  117.7 76.6 %copy-start.18 = (f32[512]{0:T(512)S(1)}, f32[512]{0:T(512)}, u32[]{:S(2)}) copy-start(f32[512]{0:T(512)} %convert_element_type.85) | copy-start | bytes 6148
  219.7 284.2 %reduce-scatter.6.cloned.1.call-start = ((), (), s32[]{:S(2)}) async-start(), calls=%async_computation.7 | async-start | bytes 4325376 | tf_op jit(solution)/shard_map/reduce_scatter | solution.py:178
  252.1 11.1 %copy-start.13 = (f32[2048]{0:T(1024)S(1)}, f32[2048]{0:T(1024)}, u32[]{:S(2)}) copy-start(f32[2048]{0:T(1024)} %copy-done.12) | copy-start | bytes 24580
  252.1 390.8 %reduce-scatter.4.cloned.1.call-start = ((), (), s32[]{:S(2)}) async-start(), calls=%async_computation.6 | async-start | bytes 9732096 | tf_op jit(solution)/shard_map/reduce_scatter | solution.py:174
  331.3 18.1 %copy-start.23 = (pred[2048]{0:T(1024)(128)(4,1)S(1)}, pred[2048]{0:T(1024)(128)(4,1)}, u32[]{:S(2)}) copy-start(pred[2048]{0:T(1024)(128)(4,1)} %copy-done.22) | copy-start | bytes 6148
  331.3 18.1 %copy-start.25 = (pred[2048]{0:T(1024)(128)(4,1)S(1)}, pred[2048]{0:T(1024)(128)(4,1)}, u32[]{:S(2)}) copy-start(pred[2048]{0:T(1024)(128)(4,1)} %copy-done.24) | copy-start | bytes 6148
  331.3 18.1 %copy-start.27 = (pred[2048]{0:T(1024)(128)(4,1)S(1)}, pred[2048]{0:T(1024)(128)(4,1)}, u32[]{:S(2)}) copy-start(pred[2048]{0:T(1024)(128)(4,1)} %copy-done.26) | copy-start | bytes 6148
  331.3 18.1 %copy-start.29 = (pred[2048]{0:T(1024)(128)(4,1)S(1)}, pred[2048]{0:T(1024)(128)(4,1)}, u32[]{:S(2)}) copy-start(pred[2048]{0:T(1024)(128)(4,1)} %copy-done.28) | copy-start | bytes 6148
  331.3 18.1 %copy-start.31 = (pred[2048]{0:T(1024)(128)(4,1)S(1)}, pred[2048]{0:T(1024)(128)(4,1)}, u32[]{:S(2)}) copy-start(pred[2048]{0:T(1024)(128)(4,1)} %copy-done.30) | copy-start | bytes 6148
  331.4 18.1 %copy-start.33 = (pred[2048]{0:T(1024)(128)(4,1)S(1)}, pred[2048]{0:T(1024)(128)(4,1)}, u32[]{:S(2)}) copy-start(pred[2048]{0:T(1024)(128)(4,1)} %copy-done.32) | copy-start | bytes 6148
  331.4 18.1 %copy-start.35 = (pred[2048]{0:T(1024)(128)(4,1)S(1)}, pred[2048]{0:T(1024)(128)(4,1)}, u32[]{:S(2)}) copy-start(pred[2048]{0:T(1024)(128)(4,1)} %copy-done.34) | copy-start | bytes 6148
  331.4 18.1 %copy-start.37 = (pred[2048]{0:T(1024)(128)(4,1)S(1)}, pred[2048]{0:T(1024)(128)(4,1)}, u32[]{:S(2)}) copy-start(pred[2048]{0:T(1024)(128)(4,1)} %copy-done.36) | copy-start | bytes 6148
  331.4 18.1 %copy-start.39 = (pred[2048]{0:T(1024)(128)(4,1)S(1)}, pred[2048]{0:T(1024)(128)(4,1)}, u32[]{:S(2)}) copy-start(pred[2048]{0:T(1024)(128)(4,1)} %copy-done.38) | copy-start | bytes 6148
  (35 other events, 190.7 us)
Sparse Core Ops, SparseCore 0:
  11.1 66.4 all-gather.3
  80.6 55.2 all-gather.5
  138.9 55.3 all-gather.7
  219.8 141.6 reduce-scatter.7
  364.2 139.6 reduce-scatter.5
  510.2 132.6 reduce-scatter.3
where the time goes:
time: 653 us; the launch traced here: 650 us
  waiting for transfers between devices  277 us (42%)
  matrix products  162 us (25%)
  other arithmetic  86 us (13%)
  blocking collectives  81.7 us (13%)
  local copies, waits for them, and re-layouts  27.9 us (4%)
  between operations  14.9 us (2%)
    reduce_scatter x1, waiting for transfers between devices, on_device(): lax.psum_scatter(contract_rows(columns, d_conv_low), ('dp', 'fsdp'), scat...  139 us
    reduce_scatter x1, waiting for transfers between devices, on_device(): lax.psum_scatter(d_weight_in, ('dp', 'fsdp'), scatter_dimension=0, tiled=...  104 us
    unnamed x2, blocking collectives  81.7 us
    dot_general x3, matrix products, contract_cols(): lax.dot_general(left, right, (((1,), (1,)), ((), ())), preferred_element_...  50.2 us
    dot_general x1, matrix products, on_device(): jnp.dot(hidden, full_in, preferred_element_type=jnp.float32)  44.2 us
    dot_general x3, matrix products, contract_rows(): lax.dot_general(left, right, (((0,), (0,)), ((), ())), preferred_element_...  33.5 us
    unnamed x131, local copies, waits for them, and re-layouts  27.9 us
    dot_general x1, matrix products, on_device(): jnp.dot(columns, lax.all_gather(conv_w, ('dp', 'fsdp'), axis=0, tiled=Tru...  26.1 us
  transfers between devices with their start and end apart: 6, of which 4 were waited for; matrix products, arithmetic and copies ran while one was open for 38% of the time, Pallas kernels for 0%

commit v1 on v0

v1 whole, which is shorter than its diff:
```python
import functools
import jax
import jax.numpy as jnp
from jax import lax
from jax.experimental import pallas as pl
from jax.experimental.pallas import tpu as pltpu
from jax.sharding import PartitionSpec as P

TAPS = 9
STEP = 8
REACH = (TAPS // 2) * STEP
EPSILON = 1e-05
AXES = ("dp", "fsdp")
f32 = jnp.float32
bf16 = jnp.bfloat16
ANY = pl.BlockSpec(memory_space=pl.ANY)
SMEM = pl.BlockSpec(memory_space=pltpu.SMEM)


def dot(a, b):
    return jnp.dot(a, b, preferred_element_type=f32)


def dot_t(a, b):
    return lax.dot_general(a, b, (((1,), (1,)), ((), ())), preferred_element_type=f32)


def dot_rows(a, b):
    return lax.dot_general(a, b, (((0,), (0,)), ((), ())), preferred_element_type=f32)


def gelu_pair(v):
    t = pl.reciprocal(1.0 + 0.23164190 * jnp.abs(v))
    e = jnp.exp(-0.5 * v * v)
    poly = t * (0.127414796 + t * (-0.142248368 + t * (0.7107068705 + t * (-0.7265760135 + t * 0.5307027145))))
    tail = poly * e
    phi = jnp.where(v >= 0.0, 1.0 - tail, tail)
    return v * phi, phi + v * (e * 0.3989422804014327)


def mean(v):
    return jnp.mean(v, axis=-1, keepdims=True)


def colsum(v):
    return jnp.sum(v, axis=0, keepdims=True)


def vmem(mib):
    return pltpu.CompilerParams(vmem_limit_bytes=mib << 20)


def cost(macs, nbytes):
    return pl.CostEstimate(flops=2 * macs, bytes_accessed=nbytes, transcendentals=0)


def whole(shape):
    return pl.BlockSpec(shape, lambda *_: (0,) * len(shape), pipeline_mode=pl.Buffered(1))


def rows_of(tile, width):
    return pl.BlockSpec((tile, width), lambda i: (i, 0))


def window_bounds(len_ref, position, wins, total):
    first = jnp.zeros_like(position)
    last = jnp.full_like(position, total)
    edge = jnp.int32(0)
    edges = []
    for w in range(wins - 1):
        edge = edge + len_ref[0, w]
        edges.append(edge)
    for edge in edges:
        first = jnp.where(position >= edge, edge, first)
    for edge in reversed(edges):
        last = jnp.where(position < edge, edge, last)
    return first, last


def wide(mask, width):
    return jnp.concatenate([mask] * (width // 128), axis=1)


def prep_kernel(len_ref, tokens_ref, keep_ref, stacked_ref, masked_ref, padded, *, tile, wins):
    step = pl.program_id(0)
    rows, width = tokens_ref.shape

    @pl.when(step == 0)
    def _():
        padded[:REACH] = jnp.zeros((REACH, width), f32)
        padded[rows + REACH :] = jnp.zeros((REACH, width), f32)
        for r in range(0, rows, tile):
            padded[REACH + r : REACH + r + tile] = tokens_ref[r : r + tile].astype(f32) * wide(keep_ref[r : r + tile], width)

    start = pl.multiple_of(step * tile, tile)
    masked_ref[...] = padded[pl.ds(start + REACH, tile)].astype(bf16)
    position = lax.broadcasted_iota(jnp.int32, (tile, 128), 0) + start
    first, last = window_bounds(len_ref, position, wins, rows)
    for tap in range(TAPS):
        other = position + (tap - TAPS // 2) * STEP
        valid = ((other >= first) & (other < last)).astype(f32)
        block = padded[pl.ds(pl.multiple_of(start + tap * STEP, STEP), tile)] * wide(valid, width)
        stacked_ref[:, tap * width : (tap + 1) * width] = block.astype(bf16)


def prep(lengths, tokens, keep):
    rows, width = tokens.shape
    tile = 256
    return pl.pallas_call(
        functools.partial(prep_kernel, tile=tile, wins=lengths.shape[1]),
        grid=(rows // tile,),
        in_specs=[SMEM, whole((rows, width)), whole((rows, 128))],
        out_specs=[rows_of(tile, TAPS * width), rows_of(tile, width)],
        out_shape=[
            jax.ShapeDtypeStruct((rows, TAPS * width), bf16),
            jax.ShapeDtypeStruct((rows, width), bf16),
        ],
        scratch_shapes=[pltpu.VMEM((rows + 2 * REACH, width), f32)],
        compiler_params=vmem(60),
        cost_estimate=cost(0, 24 * rows * width),
        name="prep",
    )(lengths, tokens, keep)


def place_halves(mine, other, core, blocks, body, store, sems):
    copies = []
    for source, which in ((mine, core), (other, 1 - core)):
        for block in range(blocks):
            start = pl.multiple_of((2 * block + which) * body, 16)
            copies.append(
                pltpu.make_async_copy(
                    source.at[block, pl.ds(0, body)], store.at[pl.ds(start, body)], sems.at[len(copies)]
                )
            )
    return copies


def conv_kernel(
    core_ref, mine, other, stacked_ref, tokens_ref, hidden_ref, normed_ref, slope_ref, small_ref, store, small, sems, *, blocks, body, extra
):
    core = core_ref[0]

    @pl.when(pl.program_id(0) == 0)
    def _():
        copies = place_halves(mine, other, core, blocks, body, store, sems)
        for n, source in enumerate((mine, other)):
            copies.append(
                pltpu.make_async_copy(source.at[:, pl.ds(body, extra)], small.at[n], sems.at[2 * blocks + n])
            )
        for copy in copies:
            copy.start()
        for copy in copies:
            copy.wait()
        small_ref[...] = jnp.sum(small[...].astype(f32), axis=(0, 1))

    conv = dot(stacked_ref[...], store[...]) + small_ref[0:1]
    bent, bend = gelu_pair(conv)
    center = mean(bent)
    shifted = bent - center
    root = lax.rsqrt(mean(shifted * shifted) + EPSILON)
    normed = shifted * root
    hidden_ref[...] = (tokens_ref[...].astype(f32) + normed * small_ref[1:2] + small_ref[2:3]).astype(bf16)
    normed_ref[...] = normed
    slope_ref[...] = bend * root


def conv_forward(core, mine, other, stacked, tokens, body, extra):
    rows, width = tokens.shape
    blocks = mine.shape[0]
    tile = 512
    tall = rows_of(tile, width)
    return pl.pallas_call(
        functools.partial(conv_kernel, blocks=blocks, body=body, extra=extra),
        grid=(rows // tile,),
        in_specs=[SMEM, ANY, ANY, rows_of(tile, TAPS * width), tall],
        out_specs=[tall, tall, tall, pl.BlockSpec((extra, width), lambda i: (0, 0))],
        out_shape=[
            jax.ShapeDtypeStruct((rows, width), bf16),
            jax.ShapeDtypeStruct((rows, width), f32),
            jax.ShapeDtypeStruct((rows, width), f32),
            jax.ShapeDtypeStruct((extra, width), f32),
        ],
        scratch_shapes=[
            pltpu.VMEM((TAPS * width, width), bf16),
            pltpu.VMEM((2, blocks, extra, width), bf16),
            pltpu.SemaphoreType.DMA((2 * blocks + 2,)),
        ],
        compiler_params=vmem(60),
        cost_estimate=cost(TAPS * rows * width * width, 24 * rows * width),
        name="conv_forward",
    )(core, mine, other, stacked, tokens)


def chain_kernel(
    ff, small_ref, hidden_ref, normed_ref, slope_ref, cot_ref,
    mixed_ref, active_ref, d_outer_ref, d_inner_ref, d_hidden_ref, d_conv_ref, sums_ref,
    w_in, w_out, bend, sems, *, cols, chunk,
):
    step = pl.program_id(0)
    blocks, inner_rows, _ = w_in.shape
    width = hidden_ref.shape[1]

    @pl.when(step == 0)
    def _():
        copies = [
            pltpu.make_async_copy(
                ff.at[:, pl.ds(j * inner_rows, inner_rows)], w_in.at[:, :, pl.ds(j * width, width)], sems.at[j]
            )
            for j in range(cols)
        ]
        copies.append(
            pltpu.make_async_copy(ff.at[:, pl.ds(cols * inner_rows, w_out.shape[1])], w_out, sems.at[cols])
        )
        for copy in copies:
            copy.start()
        for copy in copies:
            copy.wait()
        sums_ref[...] = jnp.zeros_like(sums_ref)

    full_in = w_in.reshape(blocks * inner_rows, w_in.shape[2])
    full_out = w_out.reshape(blocks * w_out.shape[1], width)
    hidden = hidden_ref[...]
    total = full_in.shape[1]
    for j in range(total // chunk):
        part = slice(j * chunk, (j + 1) * chunk)
        bias = small_ref[6 + j * chunk // width : 7 + j * chunk // width, j * chunk % width : j * chunk % width + chunk]
        inner = dot(hidden, full_in[:, part]) + bias
        act, slope = gelu_pair(inner)
        active_ref[:, part] = act.astype(bf16)
        bend[:, part] = slope
    outer = dot(active_ref[...], full_out[...]) + small_ref[3:4]
    center = mean(outer)
    shifted = outer - center
    root = lax.rsqrt(mean(shifted * shifted) + EPSILON)
    normal = shifted * root
    gain_two = small_ref[4:5]
    mixed_ref[...] = (hidden.astype(f32) + normal * gain_two + small_ref[5:6]).astype(bf16)
    cot = cot_ref[...].astype(f32)
    q = cot * gain_two
    d_outer = (root * (q - mean(q) - normal * mean(q * normal))).astype(bf16)
    d_outer_ref[...] = d_outer
    sums_ref[3:4] += colsum(d_outer.astype(f32))
    sums_ref[4:5] += colsum(cot * normal)
    sums_ref[5:6] += colsum(cot)
    for j in range(total // chunk):
        part = slice(j * chunk, (j + 1) * chunk)
        d_active = dot_t(d_outer, full_out[part])
        d_inner = (d_active * bend[:, part]).astype(bf16)
        d_inner_ref[:, part] = d_inner
        row, col = 6 + j * chunk // width, j * chunk % width
        sums_ref[row : row + 1, col : col + chunk] += colsum(d_inner.astype(f32))
    d_hidden = dot_t(d_inner_ref[...], full_in[...]) + cot
    d_hidden_ref[...] = d_hidden
    first = normed_ref[...]
    sums_ref[1:2] += colsum(d_hidden * first)
    sums_ref[2:3] += colsum(d_hidden)
    p = d_hidden * small_ref[1:2]
    d_conv = (slope_ref[...] * (p - mean(p) - first * mean(p * first))).astype(bf16)
    d_conv_ref[...] = d_conv
    sums_ref[0:1] += colsum(d_conv.astype(f32))


def chain(ff, small, hidden, normed, slope, cotangent, inner_rows, outer_rows, total):
    rows, width = hidden.shape
    blocks = ff.shape[0]
    tile = 512
    tall = rows_of(tile, width)
    broad = rows_of(tile, total)
    return pl.pallas_call(
        functools.partial(chain_kernel, cols=total // width, chunk=512),
        grid=(rows // tile,),
        in_specs=[ANY, whole(small.shape), tall, tall, tall, tall],
        out_specs=[tall, broad, tall, broad, tall, tall, pl.BlockSpec((16, width), lambda i: (0, 0))],
        out_shape=[
            jax.ShapeDtypeStruct((rows, width), bf16),
            jax.ShapeDtypeStruct((rows, total), bf16),
            jax.ShapeDtypeStruct((rows, width), bf16),
            jax.ShapeDtypeStruct((rows, total), bf16),
            jax.ShapeDtypeStruct((rows, width), f32),
            jax.ShapeDtypeStruct((rows, width), bf16),
            jax.ShapeDtypeStruct((16, width), f32),
        ],
        scratch_shapes=[
            pltpu.VMEM((blocks, inner_rows, total), bf16),
            pltpu.VMEM((blocks, outer_rows, width), bf16),
            pltpu.VMEM((tile, total), f32),
            pltpu.SemaphoreType.DMA((total // width + 1,)),
        ],
        compiler_params=vmem(60),
        cost_estimate=cost(4 * rows * width * total, 40 * rows * width),
        name="chain",
    )(ff, small, hidden, normed, slope, cotangent)


def ff_grads_kernel(core_ref, hidden_ref, d_outer_ref, active_ref, d_inner_ref, keep_ref, send_ref, store, sems, *, blocks, inner_rows, outer_rows):
    step = pl.program_id(0)
    width = hidden_ref.shape[1]
    cols = pl.num_programs(0)
    d_in = dot_rows(hidden_ref[...], d_inner_ref[...]).astype(bf16)
    store[:, pl.ds(pl.multiple_of(step * inner_rows, inner_rows), inner_rows)] = d_in.reshape(2 * blocks, inner_rows, width)
    d_out = dot_rows(active_ref[...], d_outer_ref[...]).astype(bf16)
    first = store.shape[1] - outer_rows
    if outer_rows <= width:
        many = width // outer_rows
        store[pl.ds(step * many, many), pl.ds(first, outer_rows)] = d_out.reshape(many, outer_rows, width)
    else:
        per = outer_rows // width
        start = pl.multiple_of(first + (step % per) * width, 16)
        store[pl.ds(step // per, 1), pl.ds(start, width)] = d_out.reshape(1, width, width)

    @pl.when(step == cols - 1)
    def _():
        core = core_ref[0]
        copies = []
        for block in range(blocks):
            copies.append(pltpu.make_async_copy(store.at[2 * block + core], keep_ref.at[block], sems.at[0, block]))
            copies.append(pltpu.make_async_copy(store.at[2 * block + 1 - core], send_ref.at[block], sems.at[1, block]))
        for copy in copies:
            copy.start()
        for copy in copies:
            copy.wait()


def ff_grads(core, hidden, d_outer, active, d_inner, blocks, inner_rows, outer_rows):
    rows, width = hidden.shape
    total = active.shape[1]
    cols = total // width
    share = cols * inner_rows + outer_rows
    part = pl.BlockSpec((rows, width), lambda j: (0, j))
    return pl.pallas_call(
        functools.partial(ff_grads_kernel, blocks=blocks, inner_rows=inner_rows, outer_rows=outer_rows),
        grid=(cols,),
        in_specs=[SMEM, whole((rows, width)), whole((rows, width)), part, part],
        out_specs=[ANY, ANY],
        out_shape=[jax.ShapeDtypeStruct((blocks, share, width), bf16)] * 2,
        scratch_shapes=[pltpu.VMEM((2 * blocks, share, width), bf16), pltpu.SemaphoreType.DMA((2, blocks))],
        compiler_params=vmem(60),
        cost_estimate=cost(2 * rows * width * total, 20 * rows * width),
        name="ff_grads",
    )(core, hidden, d_outer, active, d_inner)


def lay_shifted(values_ref, even, odd, tile):
    rows, width = values_ref.shape
    zeros = jnp.zeros((REACH, width), bf16)
    even[:REACH] = zeros
    even[rows + REACH :] = zeros
    odd[: REACH] = zeros
    odd[rows :] = jnp.zeros((2 * REACH, width), bf16)
    for r in range(0, rows, tile):
        block = values_ref[r : r + tile]
        even[REACH + r : REACH + r + tile] = block
        odd[REACH - STEP + r : REACH - STEP + r + tile] = block


def conv_grad_kernel(len_ref, core_ref, masked_ref, d_conv_ref, keep_ref, send_ref, even, odd, store, sems, *, wins, blocks, body):
    rows, width = d_conv_ref.shape
    channels = masked_ref.shape[1]
    lay_shifted(d_conv_ref, even, odd, 256)
    position = lax.broadcasted_iota(jnp.int32, (rows, 128), 0)
    first, last = window_bounds(len_ref, position, wins, rows)
    for tap in range(TAPS):
        mirror = TAPS - 1 - tap
        other = position + (mirror - TAPS // 2) * STEP
        valid = ((other >= first) & (other < last)).astype(bf16)
        source = (odd if mirror % 2 else even)[mirror // 2 * 2 * STEP : mirror // 2 * 2 * STEP + rows]
        block = source * wide(valid, width)
        store[tap * channels : (tap + 1) * channels] = dot_rows(masked_ref[...], block).astype(bf16)
    core = core_ref[0]
    copies = []
    for block in range(blocks):
        for n, (target, which) in enumerate(((keep_ref, core), (send_ref, 1 - core))):
            start = pl.multiple_of((2 * block + which) * body, 16)
            copies.append(pltpu.make_async_copy(store.at[pl.ds(start, body)], target.at[block], sems.at[n, block]))
    for copy in copies:
        copy.start()
    for copy in copies:
        copy.wait()


def conv_grad(lengths, core, masked, d_conv, part, parts, blocks, body):
    rows, channels = masked.shape
    width = d_conv.shape[1] // parts
    return pl.pallas_call(
        functools.partial(conv_grad_kernel, wins=lengths.shape[1], blocks=blocks, body=body),
        grid=(1,),
        in_specs=[SMEM, SMEM, whole((rows, channels)), pl.BlockSpec((rows, width), lambda i: (0, part))],
        out_specs=[ANY, ANY],
        out_shape=[jax.ShapeDtypeStruct((blocks, body, width), bf16)] * 2,
        scratch_shapes=[
            pltpu.VMEM((rows + 2 * REACH, width), bf16),
            pltpu.VMEM((rows + 2 * REACH, width), bf16),
            pltpu.VMEM((TAPS * channels, width), bf16),
            pltpu.SemaphoreType.DMA((2, blocks)),
        ],
        compiler_params=vmem(60),
        cost_estimate=cost(TAPS * rows * width * channels, 12 * rows * width),
        name="conv_grad",
    )(lengths, core, masked, d_conv)


def token_grad_kernel(
    len_ref, core_ref, mine, other, d_conv_ref, d_hidden_ref, keep_ref, d_tokens_ref, even, odd, store, sems, *, wins, blocks, body, tile
):
    step = pl.program_id(0)
    rows, width = d_conv_ref.shape

    @pl.when(step == 0)
    def _():
        copies = place_halves(mine, other, core_ref[0], blocks, body, store, sems)
        for copy in copies:
            copy.start()
        lay_shifted(d_conv_ref, even, odd, 256)
        for copy in copies:
            copy.wait()

    start = pl.multiple_of(step * tile, tile)
    position = lax.broadcasted_iota(jnp.int32, (tile, 128), 0) + start
    first, last = window_bounds(len_ref, position, wins, rows)
    total = None
    for tap in range(TAPS):
        mirror = TAPS - 1 - tap
        other_row = position + (mirror - TAPS // 2) * STEP
        valid = ((other_row >= first) & (other_row < last)).astype(bf16)
        offset = pl.multiple_of(start + mirror // 2 * 2 * STEP, 2 * STEP)
        block = (odd if mirror % 2 else even)[pl.ds(offset, tile)] * wide(valid, width)
        term = dot_t(block, store[tap * width : (tap + 1) * width])
        total = term if total is None else total + term
    d_tokens_ref[...] = d_hidden_ref[...] + total * wide(keep_ref[...], width)


def token_grad(lengths, core, mine, other, d_conv, d_hidden, keep, body):
    rows, width = d_conv.shape
    blocks = mine.shape[0]
    tile = 512
    return pl.pallas_call(
        functools.partial(token_grad_kernel, wins=lengths.shape[1], blocks=blocks, body=body, tile=tile),
        grid=(rows // tile,),
        in_specs=[SMEM, SMEM, ANY, ANY, whole((rows, width)), rows_of(tile, width), rows_of(tile, 128)],
        out_specs=rows_of(tile, width),
        out_shape=jax.ShapeDtypeStruct((rows, width), f32),
        scratch_shapes=[
            pltpu.VMEM((rows + 2 * REACH, width), bf16),
            pltpu.VMEM((rows + 2 * REACH, width), bf16),
            pltpu.VMEM((TAPS * width, width), bf16),
            pltpu.SemaphoreType.DMA((2 * blocks,)),
        ],
        compiler_params=vmem(60),
        cost_estimate=cost(TAPS * rows * width * width, 12 * rows * width),
        name="token_grad",
    )(lengths, core, mine, other, d_conv, d_hidden, keep)


def on_device(
    n_dp, n_fsdp, tokens, present, lengths, conv_w, conv_b, gain_one, shift_one, w_in, b_in, w_out, b_out, gain_two, shift_two, cotangent
):
    rows, width = tokens.shape
    total = w_in.shape[1]
    cols = total // width
    devices = n_dp * n_fsdp
    place = lax.axis_index("dp") * n_fsdp + lax.axis_index("fsdp")
    fast = conv_w.shape[0] % 16 == 0 and w_in.shape[0] % 16 == 0
    extra = 16
    keep = jnp.broadcast_to((present > 0).astype(f32)[:, None], (rows, 128))
    swap = [(i, i ^ 1) for i in range(n_fsdp)]
    columns = [list(range(c, n_fsdp, 2)) for c in range(2)]
    n_z = n_fsdp // 2
    vectors = (conv_b, gain_one, shift_one, b_out, gain_two, shift_two)
    if fast:
        core = lax.rem(lax.axis_index("fsdp"), 2).astype(jnp.int32).reshape(1)
        body = conv_w.shape[0]
        inner_rows, outer_rows = w_in.shape[0], w_out.shape[0]
        blocks = devices // 2
        lane = jnp.arange(width)
        lines = []
        for vector in vectors:
            n = vector.shape[0]
            lines.append(jnp.where(lane // n == place, jnp.tile(vector, width // n), 0))
        n = b_in.shape[0]
        for j in range(cols):
            lines.append(jnp.where((lane + j * width) // n == place, jnp.tile(b_in, width // n), 0))
        lines += [jnp.zeros_like(lines[0])] * (extra - len(lines))
        pack = jnp.concatenate([conv_w, jnp.stack(lines)], axis=0)
        mine = lax.all_to_all(
            jnp.broadcast_to(pack, (n_z,) + pack.shape), "fsdp", 0, 0, tiled=True, axis_index_groups=columns
        )
        mine = lax.all_to_all(jnp.broadcast_to(mine, (n_dp,) + mine.shape), "dp", 0, 0, tiled=True)
        mine = mine.reshape((blocks,) + pack.shape)
        other = lax.ppermute(mine, "fsdp", swap)
        ff_own = jnp.concatenate([w_in[:, j * width : (j + 1) * width] for j in range(cols)] + [w_out], axis=0)
        ff = lax.all_gather(ff_own, AXES, axis=0, tiled=False)
    else:
        core = jnp.zeros((1,), jnp.int32)
        gather = functools.partial(lax.all_gather, axis_name=AXES, axis=0, tiled=True)
        full = gather(conv_w).reshape(2, 1, -1, width)
        body = full.shape[2]
        lines = [gather(vector) for vector in vectors] + list(gather(b_in).reshape(cols, width))
        lines += [jnp.zeros_like(lines[0])] * (extra - len(lines))
        tails = jnp.stack([jnp.stack(lines), jnp.zeros((extra, width), bf16)])[:, None]
        halves = jnp.concatenate([full, tails], axis=2)
        mine, other = halves[0], halves[1]
        full_in, full_out = gather(w_in), gather(w_out)
        inner_rows, outer_rows = full_in.shape[0] // 2, full_out.shape[0] // 2
        blocks = 1
        ff = jnp.concatenate(
            [full_in[:, j * width : (j + 1) * width].reshape(2, inner_rows, width) for j in range(cols)]
            + [full_out.reshape(2, outer_rows, width)],
            axis=1,
        )

    stacked, masked = prep(lengths, tokens, keep)
    hidden, normed, slope, small = conv_forward(core, mine, other, stacked, tokens, body, extra)
    mixed, active, d_outer, d_inner, d_hidden, d_conv, sums = chain(
        ff, small, hidden, normed, slope, cotangent, inner_rows, outer_rows, total
    )
    ff_pair = ff_grads(core, hidden, d_outer, active, d_inner, blocks, inner_rows, outer_rows)
    parts = 2
    conv_pairs = [conv_grad(lengths, core, masked, d_conv, part, parts, blocks, body) for part in range(parts)]
    d_conv_late, conv_pairs[-1] = lax.optimization_barrier((d_conv, conv_pairs[-1]))
    d_tokens = token_grad(lengths, core, mine, other, d_conv_late, d_hidden, keep, body)

    shares = sums[:6].reshape(6, devices, -1).transpose(1, 0, 2).reshape(devices, -1)
    shares = jnp.concatenate([shares, sums[6 : 6 + cols].reshape(devices, -1)], axis=1)
    shares = jnp.sum(lax.all_to_all(shares, AXES, 0, 0, tiled=True), axis=0)
    n = width // devices
    vector_grads = [shares[i * n : (i + 1) * n] for i in range(6)] + [shares[6 * n :]]

    def reduced(pair):
        kept, sent = pair
        if not fast:
            both = jnp.concatenate([kept, sent], axis=0)
            return both
        came = lax.ppermute(sent, "fsdp", swap)
        chip = (kept.astype(f32) + came.astype(f32)).astype(bf16)
        chip = chip.reshape((n_dp, n_z) + chip.shape[1:])
        chip = lax.all_to_all(chip, "dp", 0, 0, tiled=True)
        chip = jnp.sum(chip.astype(f32), axis=0).astype(bf16)
        chip = lax.all_to_all(chip, "fsdp", 0, 0, tiled=True, axis_index_groups=columns)
        return jnp.sum(chip.astype(f32), axis=0)

    ff_share = reduced(ff_pair)
    conv_shares = [reduced(pair) for pair in conv_pairs]
    if fast:
        d_w_in = jnp.concatenate([ff_share[j * inner_rows : (j + 1) * inner_rows] for j in range(cols)], axis=1)
        d_w_out = ff_share[cols * inner_rows :]
        d_conv_w = jnp.concatenate(conv_shares, axis=1)
    else:
        scatter = functools.partial(lax.psum_scatter, axis_name=AXES, scatter_dimension=0, tiled=True)
        d_in_full = jnp.concatenate(
            [ff_share[:, j * inner_rows : (j + 1) * inner_rows].reshape(-1, width) for j in range(cols)], axis=1
        )
        d_w_in = scatter(d_in_full.astype(f32))
        d_w_out = scatter(ff_share[:, cols * inner_rows :].reshape(-1, width).astype(f32))
        conv_full = jnp.concatenate([share.reshape(-1, width // parts) for share in conv_shares], axis=1)
        d_conv_w = scatter(conv_full.astype(f32))
    d_conv_b, d_gain_one, d_shift_one, d_b_out, d_gain_two, d_shift_two, d_b_in = vector_grads
    return (
        mixed, d_tokens, d_conv_w, d_conv_b, d_gain_one, d_shift_one, d_w_in, d_b_in, d_w_out, d_b_out, d_gain_two, d_shift_two
    )


def solution(mesh):
    both = P(AXES)
    flat = P(AXES, None)
    in_specs = (flat, both, flat, flat, both, both, both, flat, both, flat, both, both, both, flat)
    out_specs = (flat, flat, flat, both, both, both, flat, both, flat, both, both, both)
    return jax.shard_map(
        functools.partial(on_device, mesh.shape["dp"], mesh.shape["fsdp"]),
        mesh=mesh,
        in_specs=in_specs,
        out_specs=out_specs,
        check_vma=False,
    )
```

time: 653 us -> 326 us (0.50)
  waiting for transfers between devices: 277 us -> 60.5 us
  matrix products: 162 us -> 0 us
  Pallas kernels: 0 us -> 123 us
  other arithmetic: 86 us -> 13.8 us
  starting transfers between devices: 0.45 us -> 28.9 us
  blocking collectives: 81.7 us -> 67.5 us
  local copies, waits for them, and re-layouts: 27.9 us -> 17.6 us
    reduce_scatter x3 -> x0, waiting for transfers between devices: 243 us -> none  [the longest x1 139 us: on_device(): lax.psum_scatter(contract_rows(columns, d_conv_low), ('dp', 'fsdp'), scat...]
    dot_general x9 -> x0, matrix products: 162 us -> none  [the longest x3 50.2 us: contract_cols(): lax.dot_general(left, right, (((1,), (1,)), ((), ())), preferred_element_...]
    pallas_call x0 -> x7, Pallas kernels: none -> 123 us  [the longest x1 38.8 us: chain(): pl.pallas_call(functools.partial(chain_kernel, cols=total // width, chunk...]
    unnamed x2 -> x0, blocking collectives: 81.7 us -> none
    all_to_all x0 -> x2, blocking collectives: none -> 67.5 us  [the longest x1 41.4 us: on_device(): lax.all_to_all(jnp.broadcast_to(mine, (n_dp,) + mine.shape), 'dp', 0, 0,...]
    all_to_all x0 -> x7, waiting for transfers between devices: none -> 60.5 us  [the longest x3 48.5 us: reduced(): chip = lax.all_to_all(chip, 'dp', 0, 0, tiled=True)]
    all_gather x3 -> x1, waiting for transfers between devices: 32.3 us -> 0.02 us  [on_device(): ff = lax.all_gather(ff_own, AXES, axis=0, tiled=False)]
    all_to_all x0 -> x7, starting transfers between devices: none -> 27.8 us  [the longest x3 13.7 us: reduced(): lax.all_to_all(chip, 'fsdp', 0, 0, tiled=True, axis_index_groups=columns)]
  transfers between devices with their start and end apart: 6 -> 12, of which waited for: 4 -> 5; matrix products, arithmetic and copies ran while one was open for 38% -> 7% of each run, Pallas kernels for 0% -> 26%
where the time goes in v1:
time: 326 us; the launch traced here: 325 us
  Pallas kernels  123 us (38%)
  blocking collectives  67.5 us (21%)
  waiting for transfers between devices  60.5 us (19%)
  starting transfers between devices  28.9 us (9%)
  local copies, waits for them, and re-layouts  17.6 us (5%)
  between operations  14.3 us (4%)
  other arithmetic  13.8 us (4%)
    all_to_all x3, waiting for transfers between devices, reduced(): chip = lax.all_to_all(chip, 'dp', 0, 0, tiled=True)  48.5 us
    all_to_all x1, blocking collectives, on_device(): lax.all_to_all(jnp.broadcast_to(mine, (n_dp,) + mine.shape), 'dp', 0, 0,...  41.4 us
    pallas_call x1, Pallas kernels, chain(): pl.pallas_call(functools.partial(chain_kernel, cols=total // width, chunk...  38.8 us
    all_to_all x1, blocking collectives, on_device(): lax.all_to_all(jnp.broadcast_to(pack, (n_z,) + pack.shape), 'fsdp', 0, 0,...  26.1 us
    pallas_call x1, Pallas kernels, conv_forward(): pl.pallas_call(functools.partial(conv_kernel, blocks=blocks, body=body, e...  22.7 us
    pallas_call x2, Pallas kernels, conv_grad(): pl.pallas_call(functools.partial(conv_grad_kernel, wins=lengths.shape[1],...  18.4 us
    pallas_call x1, Pallas kernels, token_grad(): pl.pallas_call(functools.partial(token_grad_kernel, wins=lengths.shape[1]...  16.4 us
    pallas_call x1, Pallas kernels, ff_grads(): pl.pallas_call(functools.partial(ff_grads_kernel, blocks=blocks, inner_ro...  15.3 us
  transfers between devices with their start and end apart: 12, of which 5 were waited for; matrix products, arithmetic and copies ran while one was open for 7% of the time, Pallas kernels for 26%

profile of v1, /device:TPU:0, one launch (start us, length us, event | category | flops | bytes accessed | tf_op | source)
XLA Modules:
  0.0 325.2 jit_solution(236482816416594997)
XLA Ops:
  18.0 26.1 %all_to_all.49 = bf16[4,160,512]{2,1,0:T(8,128)(2,1)S(1)} all-to-all(bf16[4,160,512]{2,1,0:T(8,128)(2,1)S(1)} %broadcast_in_dim.26), channel_id=1, replica_groups={{0,2,4,6},{1,3,5,7},{8,10,12,14},{9,11,13,15},{16,18,20,22},{17,19,21,2..., dimensions={0} | all-to-all | bytes 1310720 | tf_op jit(solution)/shard_map/all_to_all | solution.py:484
  44.4 41.4 %all_to_all.50 = bf16[4,4,160,512]{3,2,1,0:T(8,128)(2,1)S(1)} all-to-all(bf16[4,4,160,512]{3,2,1,0:T(8,128)(2,1)S(1)} %broadcast_in_dim.27), channel_id=1, replica_groups=mesh['dp'=4,'fsdp'=8] {'dp'}, dimensions={0} | all-to-all | bytes 5242880 | tf_op jit(solution)/shard_map/all_to_all | solution.py:487
  85.8 1.7 broadcast_in_dim.28.keep_ref
  87.5 10.9 %prep.1 = (bf16[2048,4608]{1,0:T(8,128)(2,1)}, bf16[2048,512]{1,0:T(8,128)(2,1)}) custom-call(s32[1,4]{1,0:T(1,128)} %len_ref.7, bf16[2048,512]{1,0:T(8,128)(2,1)} %tokens_ref.3, f32[2048,128]{1,0:T(8,128)} %broadcast_in_dim.28.keep_ref), custom_call_target="tpu_custom_call" | custom-call | bytes 25165824 | tf_op jit(solution)/shard_map/prep/pallas_call | solution.py:109
  98.4 22.7 %conv_forward.1 = (bf16[2048,512]{1,0:T(8,128)(2,1)}, f32[2048,512]{1,0:T(8,128)}, f32[2048,512]{1,0:T(8,128)}, f32[16,512]{1,0:T(8,128)}) custom-call(s32[1]{0:T(128)} %bitcast.1.core_ref, bf16[16,160,512]{2,1,0:T(8,128)(2,1)} %bitcast.9, bf16[16,160,512]{2,1,0:T(8,128)(2,1)} %collective-permute-done.other, ...), custom_call_target="tpu_custom_call" | custom-call | flops 9663676416 | bytes 25165824 | tf_op jit(solution)/shard_map/conv_forward/pallas_call | solution.py:172
  121.2 38.8 %chain.1 = (bf16[2048,512]{1,0:T(8,128)(2,1)}, bf16[2048,2048]{1,0:T(8,128)(2,1)}, bf16[2048,512]{1,0:T(8,128)(2,1)}, bf16[2048,2048]{1,0:T(8,128)(2,1)}, f32[20...) custom-call(bf16[32,128,512]{2,1,0:T(8,128)(2,1)} %bitcast.13, ...), custom_call_target="tpu_custom_call" | custom-call | flops 17179869184 | bytes 41943040 | tf_op jit(solution)/shard_map/chain/pallas_call | solution.py:269
  162.5 3.4 %all-to-all-start.6 = ((f32[32,1,160]{2,1,0:T(1,128)}), f32[32,1,160]{2,1,0:T(1,128)}, u32[]{:S(2)}, u32[]{:S(2)}) async-start(f32[32,1,160]{2,1,0:T(1,128)} %all_to_all.36), calls=%async_computation.6 | async-start | bytes 65536 | tf_op jit(solution)/shard_map/all_to_all | solution.py:524
  165.9 9.2 %conv_grad.2 = (bf16[16,144,256]{2,1,0:T(8,128)(2,1)}, bf16[16,144,256]{2,1,0:T(8,128)(2,1)}) custom-call(s32[1,4]{1,0:T(1,128)} %len_ref.7, s32[1]{0:T(128)} %bitcast.1.core_ref, bf16[2048,512]{1,0:T(8,128)(2,1)} %get-tuple-element.41.masked_ref, bf16[2048,512]{1,0:T(8,128)(2,1)} %get-tuple-element.44.d_conv_ref), custom_call_target="tpu_custom_call" | custom-call | flops 4831838208 | bytes 6291456 | tf_op jit(solution)/shard_map/conv_grad/pallas_call | solution.py:384
  175.2 9.3 %conv_grad.3 = (bf16[16,144,256]{2,1,0:T(8,128)(2,1)}, bf16[16,144,256]{2,1,0:T(8,128)(2,1)}) custom-call(s32[1,4]{1,0:T(1,128)} %len_ref.7, s32[1]{0:T(128)} %bitcast.1.core_ref, bf16[2048,512]{1,0:T(8,128)(2,1)} %get-tuple-element.41.masked_ref, bf16[2048,512]{1,0:T(8,128)(2,1)} %get-tuple-element.44.d_conv_ref), custom_call_target="tpu_custom_call" | custom-call | flops 4831838208 | bytes 6291456 | tf_op jit(solution)/shard_map/conv_grad/pallas_call | solution.py:384
  185.0 15.3 %ff_grads.1 = (bf16[16,128,512]{2,1,0:T(8,128)(2,1)}, bf16[16,128,512]{2,1,0:T(8,128)(2,1)}) custom-call(s32[1]{0:T(128)} %bitcast.1.core_ref, bf16[2048,512]{1,0:T(8,128)(2,1)} %get-tuple-element.36.hidden_ref, bf16[2048,512]{1,0:T(8,128)(2,1)} %get-tuple-element.51.d_outer_ref, bf16[2048,2048]{1,0:T(8,128)(2,1)} %get-tuple-element.52.active_ref, ...), custom_call_target="tpu_custom_call" | custom-call | flops 8589934592 | bytes 20971520 | tf_op jit(solution)/shard_map/ff_grads/pallas_call | solution.py:330
  200.7 2.6 add_convert_fusion.1
  203.3 3.6 %all-to-all-start.4 = ((bf16[4,4,144,256]{3,2,1,0:T(8,128)(2,1)}), bf16[4,4,144,256]{3,2,1,0:T(8,128)(2,1)S(1)}, u32[]{:S(2)}, u32[]{:S(2)}) async-start(bf16[4,4,144,256]{3,2,1,0:T(8,128)(2,1)} %bitcast.4), calls=%async_computation.4 | async-start | bytes 2359296 | tf_op jit(solution)/shard_map/all_to_all | solution.py:536
  208.2 14.3 %all-to-all-done.4 = bf16[4,4,144,256]{3,2,1,0:T(8,128)(2,1)S(1)} async-done(((bf16[4,4,144,256]{3,2,1,0:T(8,128)(2,1)}), bf16[4,4,144,256]{3,2,1,0:T(8,128)(2,1)S(1)}, u32[]{:S(2)}, u32[]{:S(2)}) %all-to-all-start.4) | async-done | bytes 1179680 | tf_op jit(solution)/shard_map/all_to_all | solution.py:536
  222.5 3.5 %all-to-all-start.2 = ((bf16[4,4,144,256]{3,2,1,0:T(8,128)(2,1)}), bf16[4,4,144,256]{3,2,1,0:T(8,128)(2,1)S(1)}, u32[]{:S(2)}, u32[]{:S(2)}) async-start(bf16[4,4,144,256]{3,2,1,0:T(8,128)(2,1)} %bitcast.3), calls=%async_computation.2 | async-start | bytes 2359296 | tf_op jit(solution)/shard_map/all_to_all | solution.py:536
  227.0 13.8 %all-to-all-done.2 = bf16[4,4,144,256]{3,2,1,0:T(8,128)(2,1)S(1)} async-done(((bf16[4,4,144,256]{3,2,1,0:T(8,128)(2,1)}), bf16[4,4,144,256]{3,2,1,0:T(8,128)(2,1)S(1)}, u32[]{:S(2)}, u32[]{:S(2)}) %all-to-all-start.2) | async-done | bytes 1179680 | tf_op jit(solution)/shard_map/all_to_all | solution.py:536
  240.9 4.5 %all-to-all-start.5 = ((bf16[4,144,256]{2,1,0:T(8,128)(2,1)}), bf16[4,144,256]{2,1,0:T(8,128)(2,1)S(1)}, u32[]{:S(2)}, u32[]{:S(2)}) async-start(bf16[4,144,256]{2,1,0:T(8,128)(2,1)} %reduce_sum.74), calls=%async_computation.5 | async-start | bytes 589824 | tf_op jit(solution)/shard_map/all_to_all | solution.py:538
  245.4 4.2 %add_convert_fusion = bf16[16,128,512]{2,1,0:T(8,128)(2,1)} fusion(bf16[16,128,512]{2,1,0:T(8,128)(2,1)} %collective-permute-done.3, bf16[16,128,512]{2,1,0:T(8,128)(2,1)} %get-tuple-element.54), kind=kLoop, calls=%fused_computation | loop fusion | flops 4194304 | bytes 6291456 | tf_op jit(solution)/shard_map/convert_element_type | solution.py:534
  249.6 4.5 %all-to-all-done.5 = bf16[4,144,256]{2,1,0:T(8,128)(2,1)S(1)} async-done(((bf16[4,144,256]{2,1,0:T(8,128)(2,1)}), bf16[4,144,256]{2,1,0:T(8,128)(2,1)S(1)}, u32[]{:S(2)}, u32[]{:S(2)}) %all-to-all-start.5) | async-done | bytes 294944 | tf_op jit(solution)/shard_map/all_to_all | solution.py:538
  254.8 3.6 %all-to-all-start.7 = ((bf16[4,4,128,512]{3,2,1,0:T(8,128)(2,1)}), bf16[4,4,128,512]{3,2,1,0:T(8,128)(2,1)S(1)}, u32[]{:S(2)}, u32[]{:S(2)}) async-start(bf16[4,4,128,512]{3,2,1,0:T(8,128)(2,1)} %bitcast.7), calls=%async_computation.7 | async-start | bytes 4194304 | tf_op jit(solution)/shard_map/all_to_all | solution.py:536
  259.4 20.3 %all-to-all-done.7 = bf16[4,4,128,512]{3,2,1,0:T(8,128)(2,1)S(1)} async-done(((bf16[4,4,128,512]{3,2,1,0:T(8,128)(2,1)}), bf16[4,4,128,512]{3,2,1,0:T(8,128)(2,1)S(1)}, u32[]{:S(2)}, u32[]{:S(2)}) %all-to-all-start.7) | async-done | bytes 2097184 | tf_op jit(solution)/shard_map/all_to_all | solution.py:536
  279.7 5.7 %all-to-all-start.3 = ((bf16[4,144,256]{2,1,0:T(8,128)(2,1)}), bf16[4,144,256]{2,1,0:T(8,128)(2,1)S(1)}, u32[]{:S(2)}, u32[]{:S(2)}) async-start(bf16[4,144,256]{2,1,0:T(8,128)(2,1)} %reduce_sum.72), calls=%async_computation.3 | async-start | bytes 589824 | tf_op jit(solution)/shard_map/all_to_all | solution.py:538
  286.7 7.5 %all-to-all-done.3 = bf16[4,144,256]{2,1,0:T(8,128)(2,1)S(1)} async-done(((bf16[4,144,256]{2,1,0:T(8,128)(2,1)}), bf16[4,144,256]{2,1,0:T(8,128)(2,1)S(1)}, u32[]{:S(2)}, u32[]{:S(2)}) %all-to-all-start.3) | async-done | bytes 294944 | tf_op jit(solution)/shard_map/all_to_all | solution.py:538
  294.2 3.5 %all-to-all-start.8 = ((bf16[4,128,512]{2,1,0:T(8,128)(2,1)}), bf16[4,128,512]{2,1,0:T(8,128)(2,1)S(1)}, u32[]{:S(2)}, u32[]{:S(2)}) async-start(bf16[4,128,512]{2,1,0:T(8,128)(2,1)} %reduce_sum.77), calls=%async_computation.8 | async-start | bytes 1048576 | tf_op jit(solution)/shard_map/all_to_all | solution.py:538
  297.7 16.4 %token_grad.1 = f32[2048,512]{1,0:T(8,128)} custom-call(s32[1,4]{1,0:T(1,128)} %len_ref.7, s32[1]{0:T(128)} %bitcast.1.core_ref, bf16[16,160,512]{2,1,0:T(8,128)(2,1)} %bitcast.10, bf16[16,160,512]{2,1,0:T(8,128)(2,1)} %collective-permute-done.other, bf16[2048,512]{1,0:T(8,128)(2,1)} %get-tuple-element.44.d_conv_ref, ...), custom_call_target="tpu_custom_call" | custom-call | flops 9663676416 | bytes 12582912 | tf_op jit(solution)/shard_map/token_grad/pallas_call | solution.py:436
  (78 shorter events, 24.0 us)
Async XLA Ops:
  7.2 114.0 %all-gather.3.cloned.1.call-start = ((), (), s32[]{:S(2)}) async-start(), calls=%async_computation.9 | async-start | bytes 4325376 | tf_op jit(solution)/shard_map/all_gather | solution.py:491
  10.9 0.7 copy-start.5
  44.4 41.5 %copy-start.6 = (s32[2048]{0:T(1024)S(1)}, s32[2048]{0:T(1024)}, u32[]{:S(2)}) copy-start(s32[2048]{0:T(1024)} %param.15) | copy-start | bytes 24580
  85.8 12.6 %copy-start = (bf16[4,4,160,512]{3,2,1,0:T(8,128)(2,1)}, bf16[4,4,160,512]{3,2,1,0:T(8,128)(2,1)S(1)}, u32[]{:S(2)}) copy-start(bf16[4,4,160,512]{3,2,1,0:T(8,128)(2,1)S(1)} %all_to_all.50) | copy-start | bytes 7864324
  85.8 12.6 %collective-permute-start = (bf16[16,160,512]{2,1,0:T(8,128)(2,1)S(1)}, bf16[16,160,512]{2,1,0:T(8,128)(2,1)}, u32[]{:S(2)}, u32[]{:S(2)}) collective-permute-start(bf16[16,160,512]{2,1,0:T(8,128)(2,1)S(1)} %bitcast.8), channel_id=1, source_target_pairs={{0,1},{1,0},{2,3},{3,2},{4,5},{5,4},{6,7},{7,6},{8,9},{9,8},{10,11... | collective-permute-start | bytes 7864328 | tf_op jit(solution)/shard_map/ppermute | solution.py:489
  162.5 40.8 %all-to-all-start.6 = ((f32[32,1,160]{2,1,0:T(1,128)}), f32[32,1,160]{2,1,0:T(1,128)}, u32[]{:S(2)}, u32[]{:S(2)}) async-start(f32[32,1,160]{2,1,0:T(1,128)} %all_to_all.36), calls=%async_computation.6 | async-start | bytes 65536 | tf_op jit(solution)/shard_map/all_to_all | solution.py:524
  175.1 25.6 %collective-permute-start.2 = (bf16[16,144,256]{2,1,0:T(8,128)(2,1)}, bf16[16,144,256]{2,1,0:T(8,128)(2,1)}, u32[]{:S(2)}, u32[]{:S(2)}) collective-permute-start(bf16[16,144,256]{2,1,0:T(8,128)(2,1)} %get-tuple-element.49), channel_id=1, source_target_pairs={{0,1},{1,0},{2,3},{3,2},{4,5},{5,4},{6,7},{7,6},{8,9},{9,8},{10,11... | collective-permute-start | bytes 3538952 | tf_op jit(solution)/shard_map/ppermute | solution.py:533
  184.5 22.4 %collective-permute-start.1 = (bf16[16,144,256]{2,1,0:T(8,128)(2,1)}, bf16[16,144,256]{2,1,0:T(8,128)(2,1)S(1)}, u32[]{:S(2)}, u32[]{:S(2)}) collective-permute-start(bf16[16,144,256]{2,1,0:T(8,128)(2,1)} %get-tuple-element.47), channel_id=1, source_target_pairs={{0,1},{1,0},{2,3},{3,2},{4,5},{5,4},{6,7},{7,6},{8,9},{9,8},{10,11... | collective-permute-start | bytes 3538952 | tf_op jit(solution)/shard_map/ppermute | solution.py:533
  185.0 15.7 %copy-start.2 = (bf16[16,144,256]{2,1,0:T(8,128)(2,1)S(1)}, bf16[16,144,256]{2,1,0:T(8,128)(2,1)}, u32[]{:S(2)}) copy-start(bf16[16,144,256]{2,1,0:T(8,128)(2,1)} %get-tuple-element.48) | copy-start | bytes 3538948
  200.3 6.6 %copy-start.1 = (bf16[16,144,256]{2,1,0:T(8,128)(2,1)S(1)}, bf16[16,144,256]{2,1,0:T(8,128)(2,1)}, u32[]{:S(2)}) copy-start(bf16[16,144,256]{2,1,0:T(8,128)(2,1)} %get-tuple-element.46) | copy-start | bytes 3538948
  200.3 45.1 %collective-permute-start.3 = (bf16[16,128,512]{2,1,0:T(8,128)(2,1)}, bf16[16,128,512]{2,1,0:T(8,128)(2,1)}, u32[]{:S(2)}, u32[]{:S(2)}) collective-permute-start(bf16[16,128,512]{2,1,0:T(8,128)(2,1)} %get-tuple-element.55), channel_id=1, source_target_pairs={{0,1},{1,0},{2,3},{3,2},{4,5},{5,4},{6,7},{7,6},{8,9},{9,8},{10,11... | collective-permute-start | bytes 6291464 | tf_op jit(solution)/shard_map/ppermute | solution.py:533
  203.3 19.3 %all-to-all-start.4 = ((bf16[4,4,144,256]{3,2,1,0:T(8,128)(2,1)}), bf16[4,4,144,256]{3,2,1,0:T(8,128)(2,1)S(1)}, u32[]{:S(2)}, u32[]{:S(2)}) async-start(bf16[4,4,144,256]{3,2,1,0:T(8,128)(2,1)} %bitcast.4), calls=%async_computation.4 | async-start | bytes 2359296 | tf_op jit(solution)/shard_map/all_to_all | solution.py:536
  222.5 18.3 %all-to-all-start.2 = ((bf16[4,4,144,256]{3,2,1,0:T(8,128)(2,1)}), bf16[4,4,144,256]{3,2,1,0:T(8,128)(2,1)S(1)}, u32[]{:S(2)}, u32[]{:S(2)}) async-start(bf16[4,4,144,256]{3,2,1,0:T(8,128)(2,1)} %bitcast.3), calls=%async_computation.2 | async-start | bytes 2359296 | tf_op jit(solution)/shard_map/all_to_all | solution.py:536
  240.9 13.3 %all-to-all-start.5 = ((bf16[4,144,256]{2,1,0:T(8,128)(2,1)}), bf16[4,144,256]{2,1,0:T(8,128)(2,1)S(1)}, u32[]{:S(2)}, u32[]{:S(2)}) async-start(bf16[4,144,256]{2,1,0:T(8,128)(2,1)} %reduce_sum.74), calls=%async_computation.5 | async-start | bytes 589824 | tf_op jit(solution)/shard_map/all_to_all | solution.py:538
  254.1 0.7 copy-start.3
  254.8 24.9 %all-to-all-start.7 = ((bf16[4,4,128,512]{3,2,1,0:T(8,128)(2,1)}), bf16[4,4,128,512]{3,2,1,0:T(8,128)(2,1)S(1)}, u32[]{:S(2)}, u32[]{:S(2)}) async-start(bf16[4,4,128,512]{3,2,1,0:T(8,128)(2,1)} %bitcast.7), calls=%async_computation.7 | async-start | bytes 4194304 | tf_op jit(solution)/shard_map/all_to_all | solution.py:536
  279.7 14.5 %all-to-all-start.3 = ((bf16[4,144,256]{2,1,0:T(8,128)(2,1)}), bf16[4,144,256]{2,1,0:T(8,128)(2,1)S(1)}, u32[]{:S(2)}, u32[]{:S(2)}) async-start(bf16[4,144,256]{2,1,0:T(8,128)(2,1)} %reduce_sum.72), calls=%async_computation.3 | async-start | bytes 589824 | tf_op jit(solution)/shard_map/all_to_all | solution.py:538
  294.2 22.7 %all-to-all-start.8 = ((bf16[4,128,512]{2,1,0:T(8,128)(2,1)}), bf16[4,128,512]{2,1,0:T(8,128)(2,1)S(1)}, u32[]{:S(2)}, u32[]{:S(2)}) async-start(bf16[4,128,512]{2,1,0:T(8,128)(2,1)} %reduce_sum.77), calls=%async_computation.8 | async-start | bytes 1048576 | tf_op jit(solution)/shard_map/all_to_all | solution.py:538
  297.6 18.4 %copy-start.4 = (bf16[4,144,256]{2,1,0:T(8,128)(2,1)S(1)}, bf16[4,144,256]{2,1,0:T(8,128)(2,1)}, u32[]{:S(2)}) copy-start(bf16[4,144,256]{2,1,0:T(8,128)(2,1)} %copy-done.3) | copy-start | bytes 884740
Sparse Core Ops, SparseCore 0:
  11.7 80.3 all-gather.2

commit v2 on v1

v2 whole, which is shorter than its diff:
```python
import functools
import jax
import jax.numpy as jnp
from jax import lax
from jax.experimental import pallas as pl
from jax.experimental.pallas import tpu as pltpu
from jax.sharding import PartitionSpec as P

TAPS = 9
STEP = 8
REACH = (TAPS // 2) * STEP
EPSILON = 1e-05
SPLIT = 80
SLAB = 512
QUARTERS = 4
AXES = ("dp", "fsdp")
f32 = jnp.float32
bf16 = jnp.bfloat16
ANY = pl.BlockSpec(memory_space=pl.ANY)
SMEM = pl.BlockSpec(memory_space=pltpu.SMEM)


def dot(a, b):
    return jnp.dot(a, b, preferred_element_type=f32)


def dot_t(a, b):
    return lax.dot_general(a, b, (((1,), (1,)), ((), ())), preferred_element_type=f32)


def dot_rows(a, b):
    return lax.dot_general(a, b, (((0,), (0,)), ((), ())), preferred_element_type=f32)


def gelu_pair(v):
    phi = 0.5 + 0.5 * lax.erf(v * 0.7071067811865476)
    return v * phi, phi + v * (0.3989422804014327 * jnp.exp2(v * v * -0.7213475204444817))


def mean(v):
    return jnp.sum(v, axis=-1, keepdims=True) * (1.0 / v.shape[-1])


def fold(v):
    return sum(v[r : r + 8] for r in range(0, v.shape[0], 8))


def slabs(total, size):
    return [pl.ds(r, size) for r in range(0, total, size)]


def colsum(v):
    return jnp.sum(v, axis=0, keepdims=True)


def vmem(mib):
    return pltpu.CompilerParams(vmem_limit_bytes=mib << 20)


def cost(macs, nbytes):
    return pl.CostEstimate(flops=macs // 32, bytes_accessed=nbytes // 32, transcendentals=0)


def whole(shape):
    return pl.BlockSpec(shape, lambda *_: (0,) * len(shape), pipeline_mode=pl.Buffered(1))


def rows_of(tile, width):
    return pl.BlockSpec((tile, width), lambda i: (i, 0))


def window_bounds(len_ref, position, wins, total):
    first = jnp.zeros_like(position)
    last = jnp.full_like(position, total)
    edge = jnp.int32(0)
    edges = []
    for w in range(wins - 1):
        edge = edge + len_ref[0, w]
        edges.append(edge)
    for edge in edges:
        first = jnp.where(position >= edge, edge, first)
    for edge in reversed(edges):
        last = jnp.where(position < edge, edge, last)
    return first, last


def wide(mask, width):
    return jnp.concatenate([mask] * (width // 128), axis=1)


def prep_kernel(len_ref, place_ref, tokens_ref, present_ref, stacked_ref, masked_ref, keep_ref, even, odd, *, tile, wins):
    step = pl.program_id(0)
    rows, width = tokens_ref.shape
    start = pl.multiple_of(step * tile, tile)

    @pl.when(step == 0)
    def _():
        edge = jnp.zeros((REACH, width), bf16)
        even[:REACH] = edge
        even[rows + REACH :] = edge
        odd[:REACH] = edge
        odd[rows : rows + REACH] = edge
        odd[rows + REACH :] = edge
        for r in range(0, rows, 128):
            line = jnp.broadcast_to((present_ref[r // 128 : r // 128 + 1] > 0).astype(f32), (128, 128))
            kept = line.T
            keep_ref[r : r + 128] = kept
            block = tokens_ref[r : r + 128] * wide(kept.astype(bf16), width)
            even[REACH + r : REACH + r + 128] = block
            odd[REACH - STEP + r : REACH - STEP + r + 128] = block

    masked_ref[...] = even[pl.ds(start + REACH, tile)].T
    position = lax.broadcasted_iota(jnp.int32, (tile, 128), 0) + start
    first, last = window_bounds(len_ref, position, wins, rows)
    per = TAPS * width // 128 // QUARTERS
    for tap in range(TAPS):
        other = position + (tap - TAPS // 2) * STEP
        valid = ((other >= first) & (other < last)).astype(bf16)
        offset = pl.multiple_of(start + tap // 2 * 2 * STEP, 2 * STEP)
        block = (odd if tap % 2 else even)[pl.ds(offset, tile)] * wide(valid, width)
        for lane in range(0, width, 128):
            chunk = (tap * width + lane) // 128
            seat = ((chunk // per) ^ place_ref[2]) * per + chunk % per
            stacked_ref[:, pl.ds(pl.multiple_of(seat * 128, 128), 128)] = block[:, lane : lane + 128]


def prep(lengths, place, tokens, present):
    rows, width = tokens.shape
    tile = 256
    return pl.pallas_call(
        functools.partial(prep_kernel, tile=tile, wins=lengths.shape[1]),
        grid=(rows // tile,),
        in_specs=[SMEM, SMEM, whole((rows, width)), whole((rows // 128, 128))],
        out_specs=[
            rows_of(tile, TAPS * width), pl.BlockSpec((width, tile), lambda i: (0, i)), pl.BlockSpec((rows, 128), lambda i: (0, 0))
        ],
        out_shape=[
            jax.ShapeDtypeStruct((rows, TAPS * width), bf16),
            jax.ShapeDtypeStruct((width, rows), bf16),
            jax.ShapeDtypeStruct((rows, 128), f32),
        ],
        scratch_shapes=[pltpu.VMEM((rows + 2 * REACH, width), bf16), pltpu.VMEM((rows + 2 * REACH, width), bf16)],
        compiler_params=vmem(60),
        cost_estimate=cost(0, 24 * rows * width),
        name="prep",
    )(lengths, place, tokens, present.reshape(rows // 128, 128))


def conv_sites(pieces, first, place, fast, body):
    if not fast:
        return [(piece.at[0], first, 0) for piece in pieces]
    core, z, _ = place
    sites = []
    per = len(pieces) // 2
    for n, piece in enumerate(pieces):
        which = core if n < per else 1 - core
        kind = first + n % per
        for hop in range(piece.shape[0]):
            row = (((z - hop) & 3) * 2 + which) * body + (SPLIT if kind == 4 else 0)
            sites.append((piece.at[hop], min(kind, 3), row))
    return sites


def conv_copies(sites, base, store, sems):
    copies = []
    for n, (source, kind, row) in enumerate(sites):
        start = pl.multiple_of(base(kind) + row, 16)
        copies.append(pltpu.make_async_copy(source, store.at[pl.ds(start, source.shape[0])], sems.at[n]))
    return copies


def conv_kernel(place_ref, *refs, fast, body):
    *pieces, stacked_ref, conv_ref, near_ref, store, sems, out_sem = refs
    depth = store.shape[0] // (QUARTERS - 1)
    back = pltpu.make_async_copy(store, near_ref, out_sem)

    @pl.when(pl.program_id(0) == 0)
    def _():
        sites = conv_sites(pieces, 0, tuple(place_ref[i] for i in range(3)), fast, body)
        copies = conv_copies(sites, lambda kind: kind * depth, store, sems)
        for copy in copies:
            copy.start()
        for copy in copies:
            copy.wait()
        back.start()

    conv_ref[...] = dot(stacked_ref[...], store[...])

    @pl.when(pl.program_id(0) == pl.num_programs(0) - 1)
    def _():
        back.wait()


def conv_forward(place, pieces, stacked, fast, body):
    rows, depth = stacked.shape
    width = pieces[0].shape[2]
    depth = depth // QUARTERS * (QUARTERS - 1)
    tile = 512
    return pl.pallas_call(
        functools.partial(conv_kernel, fast=fast, body=body),
        grid=(rows // tile,),
        in_specs=[SMEM] + [ANY] * len(pieces) + [rows_of(tile, depth)],
        out_specs=[rows_of(tile, width), ANY],
        out_shape=[jax.ShapeDtypeStruct((rows, width), f32), jax.ShapeDtypeStruct((depth, width), bf16)],
        scratch_shapes=[
            pltpu.VMEM((depth, width), bf16),
            pltpu.SemaphoreType.DMA((sum(piece.shape[0] for piece in pieces),)),
            pltpu.SemaphoreType.DMA,
        ],
        compiler_params=vmem(60),
        cost_estimate=cost(depth * rows * width, 24 * rows * width),
        name="conv_forward",
    )(place, *pieces, stacked)


def ff_copies(pieces, place, fast, store, sems):
    if not fast:
        return [pltpu.make_async_copy(pieces[0], store, sems.at[0])]
    core, z, _ = place
    copies = []
    for piece, which in zip(pieces, (core, 1 - core)):
        for seat in range(piece.shape[0]):
            block = (seat // 4 * 4 + ((z - seat) & 3)) * 2 + which
            copies.append(pltpu.make_async_copy(piece.at[seat], store.at[block], sems.at[len(copies)]))
    return copies


def feed_kernel(place_ref, *refs, far, count, tiles, chunk, inner_rows, outer_rows, extra, fast, body):
    far_pieces, ff_pieces = refs[:far], refs[far : far + count]
    refs = refs[far + count :]
    stacked_ref, partial_ref, tokens_ref, cot_ref = refs[:4]
    mixed_ref, d_hidden_ref, d_conv_ref, keep_ref, send_ref, sums_ref, far_ref = refs[4:11]
    packed, w_in, w_far, small_ref, bend, slope_ref, normed_ref, hiddens, actives, d_outers, d_inners = refs[11:22]
    tallies, ff_sems, far_sems, grad_sems, last_sems, out_sem = refs[22:]
    slab = SLAB
    store = packed
    step = pl.program_id(0)
    tile, width = tokens_ref.shape
    total = w_in.shape[1]
    blocks = packed.shape[0]
    cols = total // width
    place = tuple(place_ref[i] for i in range(3))
    core = place[0]
    depth = w_far.shape[0]
    top = cols * inner_rows
    back = pltpu.make_async_copy(w_far, far_ref, out_sem)

    @pl.when(step == 0)
    def _():
        copies = ff_copies(ff_pieces, place, fast, packed, ff_sems)
        far_sites = conv_sites(far_pieces, QUARTERS - 1, place, fast, body)
        copies += conv_copies(far_sites, lambda kind: 0, w_far, far_sems)
        for copy in copies:
            copy.start()
        tallies[...] = jnp.zeros_like(tallies)
        for copy in copies:
            copy.wait()
        back.start()
        for j in range(cols):
            part = packed[:, j * inner_rows : (j + 1) * inner_rows].reshape(blocks * inner_rows, width)
            w_in[:, j * width : (j + 1) * width] = part
        small_ref[...] = jnp.sum(packed[:, top : top + extra].astype(f32), axis=0)

    base = pl.multiple_of(jnp.minimum(step, tiles - 1) * tile, tile)

    def at(part):
        return pl.ds(pl.multiple_of(base + part.start, part.size), part.size)

    def add_tally(row, col, term):
        tallies[8 * row : 8 * row + 8, col : col + term.shape[1]] += fold(term)

    def out_rows(j):
        if outer_rows > chunk:
            per = outer_rows // chunk
            first = top + extra + j % per * chunk
            return packed[j // per, first : first + chunk]
        count = chunk // outer_rows
        return packed[j * count : (j + 1) * count, top + extra :].reshape(chunk, width)

    in_rows = step < tiles

    @pl.when(in_rows)
    def _():
        for part in slabs(tile, slab):
            conv = partial_ref[part] + dot(stacked_ref[part], w_far[...]) + small_ref[0:1]
            bent, slope = gelu_pair(conv)
            shifted = bent - mean(bent)
            root = lax.rsqrt(mean(shifted * shifted) + EPSILON)
            normed = shifted * root
            normed_ref[part] = normed
            slope_ref[part] = slope * root
            hiddens[at(part)] = (
                tokens_ref[part].astype(f32) + normed * small_ref[1:2] + small_ref[2:3]
            ).astype(bf16)

    for j in range(total // chunk):
        cut = slice(j * chunk, (j + 1) * chunk)

        @pl.when(in_rows)
        def _(j=j, cut=cut):
            for part in slabs(tile, slab):
                inner = dot(hiddens[at(part)], w_in[:, cut]) + small_ref[6 + j : 7 + j]
                act, slope = gelu_pair(inner)
                actives[at(part), cut] = act.astype(bf16)
                bend[part, cut] = slope

    @pl.when(in_rows)
    def _():
        gain_two = small_ref[4:5]
        for part in slabs(tile, slab):
            full = packed[:, top + extra :].reshape(blocks * outer_rows, width)
            outer = dot(actives[at(part)], full) + small_ref[3:4]
            shifted = outer - mean(outer)
            root = lax.rsqrt(mean(shifted * shifted) + EPSILON)
            normal = shifted * root
            mixed_ref[part] = (hiddens[at(part)].astype(f32) + normal * gain_two + small_ref[5:6]).astype(bf16)
            cot = cot_ref[part].astype(f32)
            q = cot * gain_two
            d_outer = (root * (q - mean(q) - normal * mean(q * normal))).astype(bf16)
            d_outers[at(part)] = d_outer
            add_tally(3, 0, d_outer.astype(f32))
            add_tally(4, 0, cot * normal)
            add_tally(5, 0, cot)

    for j in range(total // chunk):
        cut = slice(j * chunk, (j + 1) * chunk)

        @pl.when(in_rows)
        def _(j=j, cut=cut):
            for part in slabs(tile, slab):
                d_inner = (dot_t(d_outers[at(part)], out_rows(j)) * bend[part, cut]).astype(bf16)
                d_inners[at(part), cut] = d_inner
                add_tally(6 + j, 0, d_inner.astype(f32))

    @pl.when(in_rows)
    def _():
        for part in slabs(tile, slab):
            d_hidden = dot_t(d_inners[at(part)], w_in[...]) + cot_ref[part].astype(f32)
            d_hidden_ref[part] = d_hidden
            first = normed_ref[part]
            p = d_hidden * small_ref[1:2]
            d_conv = (slope_ref[part] * (p - mean(p) - first * mean(p * first))).astype(bf16)
            d_conv_ref[part] = d_conv
            add_tally(0, 0, d_conv.astype(f32))
            add_tally(1, 0, d_hidden * first)
            add_tally(2, 0, d_hidden)

    def grad_copies(j):
        copies = []
        if fast:
            z = place[1]
            below = pl.ds(top + extra, outer_rows)
            for n, (target, which) in enumerate(((keep_ref, core), (send_ref, 1 - core))):
                for k in range(4):
                    seat = j * 4 + ((k - z) & 3)
                    copies.append(
                        pltpu.make_async_copy(
                            store.at[2 * (4 * j + k) + which, below], target.at[seat, below], grad_sems.at[j, 4 * n + k]
                        )
                    )
        return copies

    def last_copies():
        copies = []
        if fast:
            z = place[1]
            above = pl.ds(0, top + extra)
            for block in range(blocks // 2):
                seat = block // 4 * 4 + ((block % 4 - z) & 3)
                for n, (target, which) in enumerate(((keep_ref, core), (send_ref, 1 - core))):
                    copies.append(
                        pltpu.make_async_copy(
                            store.at[2 * block + which, above], target.at[seat, above], last_sems.at[n, block]
                        )
                    )
        return copies

    @pl.when(step >= tiles)
    def _():
        j = step - tiles
        part = pl.ds(pl.multiple_of(j * width, width), width)
        d_out = dot_rows(actives[:, part], d_outers[...]).astype(bf16)
        first = top + extra
        if fast:
            many = width // outer_rows
            store[pl.ds(j * many, many), first : first + outer_rows] = d_out.reshape(many, outer_rows, width)
        else:
            per = outer_rows // width
            start = pl.multiple_of(first + (j % per) * width, 16)
            store[pl.ds(j // per, 1), pl.ds(start, width)] = d_out.reshape(1, width, width)
        d_in = dot_rows(hiddens[...], d_inners[:, part]).astype(bf16)
        above = pl.ds(pl.multiple_of(j * inner_rows, inner_rows), inner_rows)
        store[:, above] = d_in.reshape(blocks, inner_rows, width)
        for copy in grad_copies(j):
            copy.start()

    @pl.when(step == pl.num_programs(0) - 1)
    def _():
        back.wait()
        for row in range(sums_ref.shape[0]):
            sums_ref[row : row + 1] = colsum(tallies[8 * row : 8 * row + 8])
        if fast:
            head = sums_ref[:6].astype(bf16)
            rest = jnp.zeros((extra - 7, width), bf16)
            for dp in range(blocks // 8):
                line = jnp.concatenate([head, sums_ref[6 + dp : 7 + dp].astype(bf16), rest])
                store[8 * dp : 8 * dp + 8, top : top + extra] = jnp.broadcast_to(line, (8, extra, width))
            copies = last_copies()
            for copy in copies:
                copy.start()
            for j in range(cols):
                copies += grad_copies(j)
            for copy in copies:
                copy.wait()
        else:
            for n, target in enumerate((keep_ref, send_ref)):
                copy = pltpu.make_async_copy(store.at[pl.ds(n, 1)], target, grad_sems.at[0, n])
                copy.start()
                copy.wait()


def feed(place, far, pieces, stacked, partial, tokens, cotangent, inner_rows, outer_rows, extra, total, fast, body):
    rows, width = tokens.shape
    blocks = width // inner_rows
    tile = 512
    tiles, cols = rows // tile, total // width
    share = cols * inner_rows + extra + outer_rows
    depth = stacked.shape[1] // QUARTERS
    tall = pl.BlockSpec((tile, width), lambda i: (jnp.minimum(i, tiles - 1), 0))
    last = pl.BlockSpec((tile, depth), lambda i: (jnp.minimum(i, tiles - 1), QUARTERS - 1))
    return pl.pallas_call(
        functools.partial(
            feed_kernel, far=len(far), count=len(pieces), tiles=tiles, chunk=512, inner_rows=inner_rows,
            outer_rows=outer_rows, extra=extra, fast=fast, body=body,
        ),
        grid=(tiles + cols,),
        in_specs=[SMEM] + [ANY] * (len(far) + len(pieces)) + [last, tall, tall, tall],
        out_specs=[tall, tall, tall, ANY, ANY, pl.BlockSpec((16, width), lambda i: (0, 0)), ANY],
        out_shape=[
            jax.ShapeDtypeStruct((rows, width), bf16),
            jax.ShapeDtypeStruct((rows, width), f32),
            jax.ShapeDtypeStruct((rows, width), bf16),
            jax.ShapeDtypeStruct((blocks // 2, share, width), bf16),
            jax.ShapeDtypeStruct((blocks // 2, share, width), bf16),
            jax.ShapeDtypeStruct((16, width), f32),
            jax.ShapeDtypeStruct((depth, width), bf16),
        ],
        scratch_shapes=[
            pltpu.VMEM((blocks, share, width), bf16),
            pltpu.VMEM((width, total), bf16),
            pltpu.VMEM((depth, width), bf16),
            pltpu.VMEM((extra, width), f32),
            pltpu.VMEM((tile, total), f32),
            pltpu.VMEM((tile, width), f32),
            pltpu.VMEM((tile, width), f32),
            pltpu.VMEM((rows, width), bf16),
            pltpu.VMEM((rows, total), bf16),
            pltpu.VMEM((rows, width), bf16),
            pltpu.VMEM((rows, total), bf16),
            pltpu.VMEM((8 * extra, width), f32),
            pltpu.SemaphoreType.DMA((blocks,)),
            pltpu.SemaphoreType.DMA((sum(piece.shape[0] for piece in far),)),
            pltpu.SemaphoreType.DMA((cols, 8)),
            pltpu.SemaphoreType.DMA((2, max(blocks // 2, 1))),
            pltpu.SemaphoreType.DMA,
        ],
        compiler_params=vmem(60),
        cost_estimate=cost(6 * rows * width * total, 40 * rows * width),
        name="feed",
    )(place, *far, *pieces, stacked, partial, tokens, cotangent)


def lay_shifted(values_ref, even, odd, tile):
    rows, width = values_ref.shape
    zeros = jnp.zeros((REACH, width), bf16)
    even[:REACH] = zeros
    even[rows + REACH :] = zeros
    odd[:REACH] = zeros
    odd[rows:] = jnp.zeros((2 * REACH, width), bf16)
    for r in range(0, rows, tile):
        block = values_ref[r : r + tile]
        even[REACH + r : REACH + r + tile] = block
        odd[REACH - STEP + r : REACH - STEP + r + tile] = block


def tap_products(len_ref, place, masked_ref, even, odd, part, targets, store, sems, *, wins, blocks, body, turn):
    channels, rows = masked_ref.shape
    width = part.stop - part.start
    core = place[0]
    position = lax.broadcasted_iota(jnp.int32, (rows, 128), 0)
    first, last = window_bounds(len_ref, position, wins, rows)
    copies = []
    for tap in range(TAPS):
        mirror = TAPS - 1 - tap
        other = position + (mirror - TAPS // 2) * STEP
        valid = ((other >= first) & (other < last)).astype(bf16)
        source = (odd if mirror % 2 else even)[mirror // 2 * 2 * STEP : mirror // 2 * 2 * STEP + rows, part]
        store[tap * channels : (tap + 1) * channels] = dot(masked_ref[...], source * wide(valid, width)).astype(bf16)
        while len(copies) // 2 < blocks and (len(copies) // 2 + 1) * 2 * body <= (tap + 1) * channels:
            block = len(copies) // 2
            seat = ((block // 4) ^ turn) * 4 + ((block % 4 - place[1]) & 3) if blocks == 16 else block
            for n, (target, which) in enumerate(zip(targets, (core, 1 - core))):
                start = pl.multiple_of((2 * block + which) * body, 16)
                copies.append(pltpu.make_async_copy(store.at[pl.ds(start, body)], target.at[seat], sems.at[n, block]))
                copies[-1].start()
    for copy in copies:
        copy.wait()


def conv_grad_kernel(len_ref, place_ref, masked_ref, d_conv_ref, keep_ref, send_ref, even, odd, store, sems, *, wins, blocks, body):
    lay_shifted(d_conv_ref, even, odd, 256)
    tap_products(
        len_ref, tuple(place_ref[i] for i in range(3)), masked_ref, even, odd, slice(0, d_conv_ref.shape[1]),
        (keep_ref, send_ref), store, sems, wins=wins, blocks=blocks, body=body, turn=0,
    )


def conv_grad(lengths, place, masked, d_conv, blocks, body):
    channels, rows = masked.shape
    width = d_conv.shape[1]
    return pl.pallas_call(
        functools.partial(conv_grad_kernel, wins=lengths.shape[1], blocks=blocks, body=body),
        grid=(1,),
        in_specs=[SMEM, SMEM, whole(masked.shape), whole((rows, width))],
        out_specs=[ANY, ANY],
        out_shape=[jax.ShapeDtypeStruct((blocks, body, width), bf16)] * 2,
        scratch_shapes=[
            pltpu.VMEM((rows + 2 * REACH, width), bf16),
            pltpu.VMEM((rows + 2 * REACH, width), bf16),
            pltpu.VMEM((TAPS * channels, width), bf16),
            pltpu.SemaphoreType.DMA((2, blocks)),
        ],
        compiler_params=vmem(60),
        cost_estimate=cost(TAPS * rows * width * channels, 12 * rows * width),
        name="conv_grad",
    )(lengths, place, masked, d_conv)


def token_grad_kernel(
    len_ref, place_ref, near_ref, far_ref, d_conv_ref, d_hidden_ref, keep_ref, d_tokens_ref, even, odd, store, sems, *, wins, tile
):
    step = pl.program_id(0)
    rows, width = d_conv_ref.shape
    depth = far_ref.shape[0]

    @pl.when(step == 0)
    def _():
        copies = []
        for kind in range(QUARTERS):
            source = far_ref if kind == QUARTERS - 1 else near_ref.at[pl.ds(kind * depth, depth)]
            start = pl.multiple_of((place_ref[2] ^ kind) * depth, 128)
            copies.append(pltpu.make_async_copy(source, store.at[pl.ds(start, depth)], sems.at[kind]))
        for copy in copies:
            copy.start()
        lay_shifted(d_conv_ref, even, odd, 256)
        for copy in copies:
            copy.wait()

    start = pl.multiple_of(step * tile, tile)
    position = lax.broadcasted_iota(jnp.int32, (tile, 128), 0) + start
    first, last = window_bounds(len_ref, position, wins, rows)
    total = None
    for tap in range(TAPS):
        mirror = TAPS - 1 - tap
        other_row = position + (mirror - TAPS // 2) * STEP
        valid = ((other_row >= first) & (other_row < last)).astype(bf16)
        offset = pl.multiple_of(start + mirror // 2 * 2 * STEP, 2 * STEP)
        block = (odd if mirror % 2 else even)[pl.ds(offset, tile)] * wide(valid, width)
        term = dot_t(block, store[tap * width : (tap + 1) * width])
        total = term if total is None else total + term
    d_tokens_ref[...] = d_hidden_ref[...] + total * wide(keep_ref[...], width)


def token_grad(lengths, place, near, far, d_conv, d_hidden, keep):
    rows, width = d_conv.shape
    tile = 512
    return pl.pallas_call(
        functools.partial(token_grad_kernel, wins=lengths.shape[1], tile=tile),
        grid=(rows // tile,),
        in_specs=[SMEM, SMEM, ANY, ANY, whole((rows, width)), rows_of(tile, width), rows_of(tile, 128)],
        out_specs=rows_of(tile, width),
        out_shape=jax.ShapeDtypeStruct((rows, width), f32),
        scratch_shapes=[
            pltpu.VMEM((rows + 2 * REACH, width), bf16),
            pltpu.VMEM((rows + 2 * REACH, width), bf16),
            pltpu.VMEM((TAPS * width, width), bf16),
            pltpu.SemaphoreType.DMA((QUARTERS,)),
        ],
        compiler_params=vmem(60),
        cost_estimate=cost(TAPS * rows * width * width, 12 * rows * width),
        name="token_grad",
    )(lengths, place, near, far, d_conv, d_hidden, keep)


def on_device(
    n_dp, n_fsdp, tokens, present, lengths, conv_w, conv_b, gain_one, shift_one, w_in, b_in, w_out, b_out, gain_two, shift_two, cotangent
):
    rows, width = tokens.shape
    total = w_in.shape[1]
    cols = total // width
    devices = n_dp * n_fsdp
    fast = n_dp == 4 and n_fsdp == 8 and conv_w.shape[0] % 16 == 0 and w_in.shape[0] % 16 == 0
    bar = lax.optimization_barrier
    extra = 16
    n = width // devices
    swap = [(i, i ^ 1) for i in range(n_fsdp)]
    across = {r: [(i, i ^ r) for i in range(n_dp)] for r in (1, 2, 3)}
    along = {k: [(i, (i + 2 * k) % n_fsdp) for i in range(n_fsdp)] for k in (1, 2, 3)}
    vectors = (conv_b, gain_one, shift_one, b_out, gain_two, shift_two)
    if fast:
        fsdp = lax.axis_index("fsdp").astype(jnp.int32)
        dp = lax.axis_index("dp").astype(jnp.int32)
        place = jnp.stack([fsdp & 1, fsdp >> 1, dp])
        body = conv_w.shape[0]
        inner_rows, outer_rows = w_in.shape[0], w_out.shape[0]
        blocks = devices // 2

        def from_column(shard):
            return [shard] + [lax.ppermute(shard, "fsdp", along[k]) for k in (1, 2, 3)]

        column = jnp.stack(from_column(conv_w))
        seat = dp * n_fsdp + fsdp
        lane = jnp.arange(width, dtype=jnp.int32)
        line = jnp.arange(extra, dtype=jnp.int32)[:, None]
        lines = jnp.concatenate(
            [jnp.tile(jnp.stack(vectors), (1, devices))]
            + [jnp.tile(b_in, width // b_in.shape[0])[None]] * cols
            + [jnp.zeros((extra - 6 - cols, width), bf16)]
        )
        few = b_in.shape[0]
        own_line = ((line < 6) & (lane // n == seat)) | ((line == 6 + dp) & (lane // few == fsdp))
        lines = jnp.where(own_line, lines, 0)
        ff_own = jnp.concatenate([w_in[:, j * width : (j + 1) * width] for j in range(cols)] + [lines, w_out], axis=0)
        stacked, masked, keep = prep(lengths, place, tokens, present)
        column, ff_own, stacked, masked, keep = bar((column, ff_own, stacked, masked, keep))
        beside_x = lax.ppermute(column, "dp", across[1])
        beside_y = lax.ppermute(column, "dp", across[2])
        ff_column = jnp.stack(from_column(ff_own))
        column, beside_x, beside_y, ff_column = bar((column, beside_x, beside_y, ff_column))
        ff = lax.all_to_all(jnp.broadcast_to(ff_column, (n_dp,) + ff_column.shape), "dp", 0, 0, tiled=True)
        ff = (ff.reshape((blocks,) + ff_own.shape),)
        near = (column, beside_x, beside_y)
        near = near + tuple(lax.ppermute(piece, "fsdp", swap) for piece in near)
        far = (
            lax.ppermute(beside_x[:, :SPLIT], "dp", across[2]),
            lax.ppermute(beside_y[:, SPLIT:], "dp", across[1]),
        )
    else:
        place = jnp.zeros((3,), jnp.int32)
        gather = functools.partial(lax.all_gather, axis_name=AXES, axis=0, tiled=True)
        full = gather(conv_w)
        body = full.shape[0] // 2
        depth = full.shape[0] // QUARTERS * (QUARTERS - 1)
        near, far = (full[None, :depth],), (full[None, depth:],)
        lines = [gather(vector) for vector in vectors] + list(gather(b_in).reshape(cols, width))
        lines = jnp.stack(lines + [jnp.zeros_like(lines[0])] * (extra - len(lines)))
        full_in, full_out = gather(w_in), gather(w_out)
        inner_rows, outer_rows = full_in.shape[0] // 2, full_out.shape[0] // 2
        blocks = 1
        ff = [full_in[:, j * width : (j + 1) * width].reshape(2, inner_rows, width) for j in range(cols)]
        ff.append(jnp.stack([lines, jnp.zeros_like(lines)]))
        ff = (jnp.concatenate(ff + [full_out.reshape(2, outer_rows, width)], axis=1),)
        stacked, masked, keep = prep(lengths, place, tokens, present)

    partial, w_near = conv_forward(place, near, stacked, fast, body)
    if fast:
        far, ff, partial = lax.optimization_barrier((far, ff, partial))
        far = far + tuple(lax.ppermute(piece, "fsdp", swap) for piece in far)
        ff = ff + tuple(lax.ppermute(piece, "fsdp", swap) for piece in ff)
    mixed, d_hidden, d_conv, ff_keep, ff_send, sums, w_far = feed(
        place, far, ff, stacked, partial, tokens, cotangent, inner_rows, outer_rows, extra, total, fast, body
    )
    def added(terms):
        return sum(term.astype(f32) for term in terms)

    def chip_sum(kept, came):
        chip = added((kept, came)).astype(bf16)
        return chip.reshape((n_dp, blocks // n_dp) + chip.shape[1:])

    def plane_swap(chip):
        plane = lax.all_to_all(chip, "dp", 0, 0, tiled=True)
        return [plane[r] for r in range(n_dp)]

    def line_swap(plane):
        line = [added(part[k] for part in plane).astype(bf16) for k in range(4)]
        return [line[0]] + [lax.ppermute(line[k], "fsdp", along[k]) for k in (1, 2, 3)]

    if fast:
        ff_came = lax.ppermute(ff_send, "fsdp", swap)
        ff_plane = plane_swap(chip_sum(ff_keep, ff_came))
        conv_keep, conv_send = conv_grad(lengths, place, masked, d_conv, blocks, body)
        conv_came = lax.ppermute(conv_send, "fsdp", swap)
        conv_chip, ff_plane, d_conv = bar((chip_sum(conv_keep, conv_came), ff_plane, d_conv))
        conv_plane = plane_swap(conv_chip)
        ff_line = line_swap(ff_plane)
        d_tokens = token_grad(lengths, place, w_near, w_far, d_conv, d_hidden, keep)
        d_tokens, ff_line, conv_plane = bar((d_tokens, ff_line, conv_plane))
        conv_line = line_swap(conv_plane)
        ff_share = added(ff_line)
        d_conv_w = added(conv_line)
        top = cols * inner_rows
        d_w_in = jnp.concatenate([ff_share[j * inner_rows : (j + 1) * inner_rows] for j in range(cols)], axis=1)
        d_w_out = ff_share[top + extra :]
        seat = dp * n_fsdp + fsdp
        own = lax.dynamic_slice(ff_share[top : top + 6], (0, seat * n), (6, n))
        vector_grads = list(own)
        vector_grads.append(lax.dynamic_slice(ff_share[top + 6], (fsdp * few,), (few,)))
    else:
        conv_pair = conv_grad(lengths, place, masked, d_conv, blocks, body)
        d_tokens = token_grad(lengths, place, w_near, w_far, d_conv, d_hidden, keep)
        ff_share = jnp.concatenate((ff_keep, ff_send), axis=0)
        scatter = functools.partial(lax.psum_scatter, axis_name=AXES, scatter_dimension=0, tiled=True)
        d_in_full = jnp.concatenate(
            [ff_share[:, j * inner_rows : (j + 1) * inner_rows].reshape(-1, width) for j in range(cols)], axis=1
        )
        d_w_in = scatter(d_in_full.astype(f32))
        d_w_out = scatter(ff_share[:, cols * inner_rows + extra :].reshape(-1, width).astype(f32))
        d_conv_w = scatter(jnp.concatenate(conv_pair, axis=0).reshape(-1, width).astype(f32))
        vector_grads = [scatter(line) for line in sums[:6]] + [scatter(sums[6 : 6 + cols].reshape(-1))]
    d_conv_b, d_gain_one, d_shift_one, d_b_out, d_gain_two, d_shift_two, d_b_in = vector_grads
    return (
        mixed, d_tokens, d_conv_w, d_conv_b, d_gain_one, d_shift_one, d_w_in, d_b_in, d_w_out, d_b_out, d_gain_two, d_shift_two
    )


def solution(mesh):
    both = P(AXES)
    flat = P(AXES, None)
    in_specs = (flat, both, flat, flat, both, both, both, flat, both, flat, both, both, both, flat)
    out_specs = (flat, flat, flat, both, both, both, flat, both, flat, both, both, both)
    return jax.shard_map(
        functools.partial(on_device, mesh.shape["dp"], mesh.shape["fsdp"]),
        mesh=mesh,
        in_specs=in_specs,
        out_specs=out_specs,
        check_vma=False,
    )
```

time: 326 us -> 239 us (0.73)
  blocking collectives: 67.5 us -> 0 us
  Pallas kernels: 123 us -> 107 us
  between operations: 14.3 us -> 0.97 us
  starting transfers between devices: 28.9 us -> 40.7 us
  local copies, waits for them, and re-layouts: 17.6 us -> 13.5 us
    all_to_all x2 -> x0, blocking collectives: 67.5 us -> none  [the longest x1 41.4 us: on_device(): lax.all_to_all(jnp.broadcast_to(mine, (n_dp,) + mine.shape), 'dp', 0, 0,...]
    ppermute x4 -> x24, waiting for transfers between devices: 0.01 us -> 34.7 us  [the longest x6 10.5 us: from_column(): return [shard] + [lax.ppermute(shard, 'fsdp', along[k]) for k in (1, 2, 3)]]
    all_to_all x7 -> x3, waiting for transfers between devices: 60.5 us -> 27.6 us  [the longest x2 27.6 us: plane_swap(): plane = lax.all_to_all(chip, 'dp', 0, 0, tiled=True)]
    ppermute x4 -> x24, starting transfers between devices: 0.97 us -> 29.6 us  [the longest x6 11.3 us: line_swap(): lax.ppermute(line[k], 'fsdp', along[k])]
    all_to_all x7 -> x3, starting transfers between devices: 27.8 us -> 11.1 us  [the longest x2 7.26 us: plane_swap(): plane = lax.all_to_all(chip, 'dp', 0, 0, tiled=True)]
    pallas_call x3 -> x2, Pallas kernels: 76.8 us -> 65.3 us  [the longest x1 51.2 us: feed(): pl.pallas_call(functools.partial(feed_kernel, far=len(far), count=len(pie...]
    pallas_call x2 -> x1, Pallas kernels: 18.4 us -> 13.6 us  [conv_grad(): pl.pallas_call(functools.partial(conv_grad_kernel, wins=lengths.shape[1],...]
    reduce_sum x7 -> x0, other arithmetic: 4.13 us -> none  [the longest x3 3.18 us: reduced(): chip = jnp.sum(chip.astype(f32), axis=0).astype(bf16)]
  transfers between devices with their start and end apart: 12 -> 27, of which waited for: 5 -> 11; matrix products, arithmetic and copies ran while one was open for 7% -> 9% of each run, Pallas kernels for 26% -> 24%
where the time goes in v2:
time: 239 us; the launch traced here: 238 us
  Pallas kernels  107 us (45%)
  waiting for transfers between devices  62.3 us (26%)
  starting transfers between devices  40.7 us (17%)
  local copies, waits for them, and re-layouts  13.5 us (6%)
  other arithmetic  13.4 us (6%)
    pallas_call x1, Pallas kernels, feed(): pl.pallas_call(functools.partial(feed_kernel, far=len(far), count=len(pie...  51.2 us
    all_to_all x2, waiting for transfers between devices, plane_swap(): plane = lax.all_to_all(chip, 'dp', 0, 0, tiled=True)  27.6 us
    pallas_call x1, Pallas kernels, token_grad(): pl.pallas_call(functools.partial(token_grad_kernel, wins=lengths.shape[1]...  16.2 us
    pallas_call x1, Pallas kernels, conv_forward(): pl.pallas_call(functools.partial(conv_kernel, fast=fast, body=body), grid...  14.1 us
    pallas_call x1, Pallas kernels, conv_grad(): pl.pallas_call(functools.partial(conv_grad_kernel, wins=lengths.shape[1],...  13.6 us
    pallas_call x1, Pallas kernels, prep(): pl.pallas_call(functools.partial(prep_kernel, tile=tile, wins=lengths.sha...  12.3 us
    ppermute x6, starting transfers between devices, line_swap(): lax.ppermute(line[k], 'fsdp', along[k])  11.3 us
    ppermute x6, waiting for transfers between devices, from_column(): return [shard] + [lax.ppermute(shard, 'fsdp', along[k]) for k in (1, 2, 3)]  10.5 us
  transfers between devices with their start and end apart: 27, of which 11 were waited for; matrix products, arithmetic and copies ran while one was open for 9% of the time, Pallas kernels for 24%

profile of v2, /device:TPU:0, one launch (start us, length us, event | category | flops | bytes accessed | tf_op | source)
XLA Modules:
  0.0 238.2 jit_solution(10606953147808335169)
XLA Ops:
  0.7 3.1 %collective-permute-start = (bf16[144,512]{1,0:T(8,128)(2,1)}, bf16[144,512]{1,0:T(8,128)(2,1)S(1)}, u32[]{:S(2)}, u32[]{:S(2)}) collective-permute-start(bf16[144,512]{1,0:T(8,128)(2,1)} %param.17), channel_id=1, source_target_pairs={{0,2},{1,3},{2,4},{3,5},{4,6},{5,7},{6,0},{7,1},{8,10},{9,11},{10,... | collective-permute-start | bytes 442376 | tf_op jit(solution)/shard_map/ppermute | solution.py:619
  3.7 2.1 collective-permute-start.2
  12.0 12.3 %prep.1 = (bf16[2048,4608]{1,0:T(8,128)(2,1)}, bf16[512,2048]{1,0:T(8,128)(2,1)}, f32[2048,128]{1,0:T(8,128)}) custom-call(s32[1,4]{1,0:T(1,128)} %len_ref.5, s32[3]{0:T(128)} %pad_add_fusion.place_ref, bf16[2048,512]{1,0:T(8,128)(2,1)} %refs_8_.1, s32[16,128]{1,0:T(8,128)} %bitcast.80), custom_call_target="tpu_custom_call" | custom-call | bytes 786432 | tf_op jit(solution)/shard_map/prep/pallas_call | solution.py:130
  31.7 2.0 collective-permute-done.7
  33.7 8.5 %collective-permute-done.6 = bf16[144,512]{1,0:T(8,128)(2,1)S(1)} collective-permute-done((bf16[144,512]{1,0:T(8,128)(2,1)S(1)}, bf16[144,512]{1,0:T(8,128)(2,1)S(1)}, u32[]{:S(2)}, u32[]{:S(2)}) %collective-permute-start.6) | collective-permute-done | bytes 147488 | tf_op jit(solution)/shard_map/ppermute | solution.py:619
  44.1 3.8 %all-to-all-start = ((bf16[4,4,144,512]{3,2,1,0:T(8,128)(2,1)}), bf16[4,4,144,512]{3,2,1,0:T(8,128)(2,1)S(1)}, u32[]{:S(2)}, u32[]{:S(2)}) async-start(bf16[4,4,144,512]{3,2,1,0:T(8,128)(2,1)} %broadcast_in_dim.15), calls=%async_computation | async-start | bytes 4718592 | tf_op jit(solution)/shard_map/all_to_all | solution.py:640
  55.1 14.1 %conv_forward.1 = (f32[2048,512]{1,0:T(8,128)}, bf16[3456,512]{1,0:T(8,128)(2,1)}) custom-call(s32[3]{0:T(128)} %pad_add_fusion.place_ref, bf16[4,144,512]{2,1,0:T(8,128)(2,1)} %copy-done.1, bf16[4,144,512]{2,1,0:T(8,128)(2,1)} %copy-done.3, bf16[4,144,512]{2,1,0:T(8,128)(2,1)} %copy-done.4, bf16[4,144,512]{2,1,0:T(8,128)(2,1)} %copy-done.5, ...), custom_call_target="tpu_custom_call" | custom-call | flops 113246208 | bytes 786432 | tf_op jit(solution)/shard_map/conv_forward/pallas_call | solution.py:199
  69.2 10.0 %collective-permute-done.9.refs_1_ = bf16[4,64,512]{2,1,0:T(8,128)(2,1)} collective-permute-done((bf16[4,64,512]{2,1,0:T(8,128)(2,1)}, bf16[4,64,512]{2,1,0:T(8,128)(2,1)}, u32[]{:S(2)}, u32[]{:S(2)}) %collective-permute-start.9) | collective-permute-done | bytes 262176 | tf_op jit(solution)/shard_map/ppermute | solution.py:646
  81.1 4.6 %collective-permute-done.14.refs_3_ = bf16[4,64,512]{2,1,0:T(8,128)(2,1)S(1)} collective-permute-done((bf16[4,64,512]{2,1,0:T(8,128)(2,1)}, bf16[4,64,512]{2,1,0:T(8,128)(2,1)S(1)}, u32[]{:S(2)}, u32[]{:S(2)}) %collective-permute-start.14) | collective-permute-done | bytes 262176 | tf_op jit(solution)/shard_map/ppermute | solution.py:668
  86.6 51.2 %feed.1 = (bf16[2048,512]{1,0:T(8,128)(2,1)}, f32[2048,512]{1,0:T(8,128)}, bf16[2048,512]{1,0:T(8,128)(2,1)}, bf16[16,144,512]{2,1,0:T(8,128)(2,1)}, bf16[16,144...) custom-call(s32[3]{0:T(128)} %pad_add_fusion.place_ref, ...), custom_call_target="tpu_custom_call" | custom-call | flops 402653184 | bytes 1310720 | tf_op jit(solution)/shard_map/feed/pallas_call | solution.py:431
  138.3 13.6 %conv_grad.1 = (bf16[16,144,512]{2,1,0:T(8,128)(2,1)}, bf16[16,144,512]{2,1,0:T(8,128)(2,1)}) custom-call(s32[1,4]{1,0:T(1,128)} %len_ref.5, s32[3]{0:T(128)} %pad_add_fusion.place_ref, bf16[512,2048]{1,0:T(8,128)(2,1)} %get-tuple-element.71.masked_ref, bf16[2048,512]{1,0:T(8,128)(2,1)} %get-tuple-element.77.d_conv_ref), custom_call_target="tpu_custom_call" | custom-call | flops 150994944 | bytes 393216 | tf_op jit(solution)/shard_map/conv_grad/pallas_call | solution.py:521
  152.0 3.9 %add_convert_fusion = bf16[16,144,512]{2,1,0:T(8,128)(2,1)} fusion(bf16[16,144,512]{2,1,0:T(8,128)(2,1)} %collective-permute-done.17, bf16[16,144,512]{2,1,0:T(8,128)(2,1)S(1)} %copy-done.2), kind=kLoop, calls=%fused_computation | loop fusion | flops 4718592 | bytes 7077888 | tf_op jit(solution)/shard_map/convert_element_type | solution.py:677
  155.9 3.6 %all-to-all-start.1 = ((bf16[4,4,144,512]{3,2,1,0:T(8,128)(2,1)}), bf16[4,4,144,512]{3,2,1,0:T(8,128)(2,1)S(1)}, u32[]{:S(2)}, u32[]{:S(2)}) async-start(bf16[4,4,144,512]{3,2,1,0:T(8,128)(2,1)} %bitcast.20), calls=%async_computation.1 | async-start | bytes 4718592 | tf_op jit(solution)/shard_map/all_to_all | solution.py:681
  159.5 4.5 %add_convert_fusion.1 = bf16[16,144,512]{2,1,0:T(8,128)(2,1)} fusion(bf16[16,144,512]{2,1,0:T(8,128)(2,1)} %collective-permute-done.16, bf16[16,144,512]{2,1,0:T(8,128)(2,1)} %get-tuple-element.73), kind=kLoop, calls=%fused_computation.1 | loop fusion | flops 4718592 | bytes 7077888 | tf_op jit(solution)/shard_map/convert_element_type | solution.py:677
  164.0 24.0 %all-to-all-done.1 = bf16[4,4,144,512]{3,2,1,0:T(8,128)(2,1)S(1)} async-done(((bf16[4,4,144,512]{3,2,1,0:T(8,128)(2,1)}), bf16[4,4,144,512]{3,2,1,0:T(8,128)(2,1)S(1)}, u32[]{:S(2)}, u32[]{:S(2)}) %all-to-all-start.1) | async-done | bytes 2359328 | tf_op jit(solution)/shard_map/all_to_all | solution.py:681
  189.2 3.6 %all-to-all-start.2 = ((bf16[4,4,144,512]{3,2,1,0:T(8,128)(2,1)}), bf16[4,4,144,512]{3,2,1,0:T(8,128)(2,1)S(1)}, u32[]{:S(2)}, u32[]{:S(2)}) async-start(bf16[4,4,144,512]{3,2,1,0:T(8,128)(2,1)} %bitcast.19), calls=%async_computation.2 | async-start | bytes 4718592 | tf_op jit(solution)/shard_map/all_to_all | solution.py:681
  192.9 2.4 %fusion.5 = (bf16[144,512]{1,0:T(8,128)(2,1)}, bf16[144,512]{1,0:T(8,128)(2,1)}, bf16[144,512]{1,0:T(8,128)(2,1)}, bf16[144,512]{1,0:T(8,128)(2,1)}) fusion(bf16[4,144,512]{2,1,0:T(8,128)(2,1)S(1)} %get-tuple-element.83, bf16[4,144,512]{2,1,0:T(8,128)(2,1)S(1)} %get-tuple-element.82, bf16[4,144,512]{2,1,0:T(8,128)(2,1)} %get-tuple-element.81, ...), kind=kLoop, calls=%fused_computation.27 | loop fusion | flops 2359296 | bytes 2949120 | tf_op jit(solution)/shard_map/add | solution.py:674
  196.5 2.4 %collective-permute-start.19 = (bf16[144,512]{1,0:T(8,128)(2,1)}, bf16[144,512]{1,0:T(8,128)(2,1)S(1)}, u32[]{:S(2)}, u32[]{:S(2)}) collective-permute-start(bf16[144,512]{1,0:T(8,128)(2,1)} %get-tuple-element.102), channel_id=1, source_target_pairs={{0,4},{1,5},{2,6},{3,7},{4,0},{5,1},{6,2},{7,3},{8,12},{9,13},{10,... | collective-permute-start | bytes 442376 | tf_op jit(solution)/shard_map/ppermute | solution.py:686
  198.9 2.0 collective-permute-start.18
  200.9 16.2 %token_grad.1 = f32[2048,512]{1,0:T(8,128)} custom-call(s32[1,4]{1,0:T(1,128)} %len_ref.5, s32[3]{0:T(128)} %pad_add_fusion.place_ref, bf16[3456,512]{1,0:T(8,128)(2,1)} %get-tuple-element.69.near_ref, bf16[1152,512]{1,0:T(8,128)(2,1)} %get-tuple-element.70.far_ref, bf16[2048,512]{1,0:T(8,128)(2,1)} %get-tuple-element.77.d_conv_ref, ...), custom_call_target="tpu_custom_call" | custom-call | flops 150994944 | bytes 393216 | tf_op jit(solution)/shard_map/token_grad/pallas_call | solution.py:577
  217.1 3.6 %all-to-all-done.2 = bf16[4,4,144,512]{3,2,1,0:T(8,128)(2,1)S(1)} async-done(((bf16[4,4,144,512]{3,2,1,0:T(8,128)(2,1)}), bf16[4,4,144,512]{3,2,1,0:T(8,128)(2,1)S(1)}, u32[]{:S(2)}, u32[]{:S(2)}) %all-to-all-start.2) | async-done | bytes 2359328 | tf_op jit(solution)/shard_map/all_to_all | solution.py:681
  223.1 2.1 collective-permute-start.23
  225.2 1.8 collective-permute-start.22
  231.3 6.1 %collective-permute-done.22 = bf16[144,512]{1,0:T(8,128)(2,1)S(1)} collective-permute-done((bf16[144,512]{1,0:T(8,128)(2,1)S(1)}, bf16[144,512]{1,0:T(8,128)(2,1)S(1)}, u32[]{:S(2)}, u32[]{:S(2)}) %collective-permute-start.22) | collective-permute-done | bytes 147488 | tf_op jit(solution)/shard_map/ppermute | solution.py:686
  (96 shorter events, 35.9 us)
Async XLA Ops:
  0.7 23.6 %collective-permute-start = (bf16[144,512]{1,0:T(8,128)(2,1)}, bf16[144,512]{1,0:T(8,128)(2,1)S(1)}, u32[]{:S(2)}, u32[]{:S(2)}) collective-permute-start(bf16[144,512]{1,0:T(8,128)(2,1)} %param.17), channel_id=1, source_target_pairs={{0,2},{1,3},{2,4},{3,5},{4,6},{5,7},{6,0},{7,1},{8,10},{9,11},{10,... | collective-permute-start | bytes 442376 | tf_op jit(solution)/shard_map/ppermute | solution.py:619
  3.7 20.6 %collective-permute-start.2 = (bf16[144,512]{1,0:T(8,128)(2,1)}, bf16[144,512]{1,0:T(8,128)(2,1)S(1)}, u32[]{:S(2)}, u32[]{:S(2)}) collective-permute-start(bf16[144,512]{1,0:T(8,128)(2,1)} %param.17), channel_id=1, source_target_pairs={{0,6},{1,7},{2,0},{3,1},{4,2},{5,3},{6,4},{7,5},{8,14},{9,15},{10,... | collective-permute-start | bytes 442376 | tf_op jit(solution)/shard_map/ppermute | solution.py:619
  5.8 18.5 %collective-permute-start.1 = (bf16[144,512]{1,0:T(8,128)(2,1)}, bf16[144,512]{1,0:T(8,128)(2,1)S(1)}, u32[]{:S(2)}, u32[]{:S(2)}) collective-permute-start(bf16[144,512]{1,0:T(8,128)(2,1)} %param.17), channel_id=1, source_target_pairs={{0,4},{1,5},{2,6},{3,7},{4,0},{5,1},{6,2},{7,3},{8,12},{9,13},{10,... | collective-permute-start | bytes 442376 | tf_op jit(solution)/shard_map/ppermute | solution.py:619
  24.4 17.8 %collective-permute-start.4 = (bf16[4,144,512]{2,1,0:T(8,128)(2,1)S(1)}, bf16[4,144,512]{2,1,0:T(8,128)(2,1)S(1)}, u32[]{:S(2)}, u32[]{:S(2)}) collective-permute-start(bf16[4,144,512]{2,1,0:T(8,128)(2,1)S(1)} %pad_maximum_fusion.refs_0_), channel_id=1, source_target_pairs={{0,16},{8,24},{16,0},{24,8},{1,17},{9,25},{17,1},{25,9},{2,18},{10... | collective-permute-start | bytes 1769480 | tf_op jit(solution)/shard_map/ppermute | solution.py:637
  26.0 16.3 %collective-permute-start.3 = (bf16[4,144,512]{2,1,0:T(8,128)(2,1)S(1)}, bf16[4,144,512]{2,1,0:T(8,128)(2,1)S(1)}, u32[]{:S(2)}, u32[]{:S(2)}) collective-permute-start(bf16[4,144,512]{2,1,0:T(8,128)(2,1)S(1)} %pad_maximum_fusion.refs_0_), channel_id=1, source_target_pairs={{0,8},{8,0},{16,24},{24,16},{1,9},{9,1},{17,25},{25,17},{2,10},{10... | collective-permute-start | bytes 1769480 | tf_op jit(solution)/shard_map/ppermute | solution.py:636
  27.5 6.1 %collective-permute-start.7 = (bf16[144,512]{1,0:T(8,128)(2,1)S(1)}, bf16[144,512]{1,0:T(8,128)(2,1)S(1)}, u32[]{:S(2)}, u32[]{:S(2)}) collective-permute-start(bf16[144,512]{1,0:T(8,128)(2,1)S(1)} %constant_dynamic-update-slice_fusion), channel_id=1, source_target_pairs={{0,6},{1,7},{2,0},{3,1},{4,2},{5,3},{6,4},{7,5},{8,14},{9,15},{10,... | collective-permute-start | bytes 442376 | tf_op jit(solution)/shard_map/ppermute | solution.py:619
  28.9 13.3 %collective-permute-start.6 = (bf16[144,512]{1,0:T(8,128)(2,1)S(1)}, bf16[144,512]{1,0:T(8,128)(2,1)S(1)}, u32[]{:S(2)}, u32[]{:S(2)}) collective-permute-start(bf16[144,512]{1,0:T(8,128)(2,1)S(1)} %constant_dynamic-update-slice_fusion), channel_id=1, source_target_pairs={{0,4},{1,5},{2,6},{3,7},{4,0},{5,1},{6,2},{7,3},{8,12},{9,13},{10,... | collective-permute-start | bytes 442376 | tf_op jit(solution)/shard_map/ppermute | solution.py:619
  30.6 11.6 %collective-permute-start.5 = (bf16[144,512]{1,0:T(8,128)(2,1)S(1)}, bf16[144,512]{1,0:T(8,128)(2,1)S(1)}, u32[]{:S(2)}, u32[]{:S(2)}) collective-permute-start(bf16[144,512]{1,0:T(8,128)(2,1)S(1)} %constant_dynamic-update-slice_fusion), channel_id=1, source_target_pairs={{0,2},{1,3},{2,4},{3,5},{4,6},{5,7},{6,0},{7,1},{8,10},{9,11},{10,... | collective-permute-start | bytes 442376 | tf_op jit(solution)/shard_map/ppermute | solution.py:619
  44.1 36.5 %all-to-all-start = ((bf16[4,4,144,512]{3,2,1,0:T(8,128)(2,1)}), bf16[4,4,144,512]{3,2,1,0:T(8,128)(2,1)S(1)}, u32[]{:S(2)}, u32[]{:S(2)}) async-start(bf16[4,4,144,512]{3,2,1,0:T(8,128)(2,1)} %broadcast_in_dim.15), calls=%async_computation | async-start | bytes 4718592 | tf_op jit(solution)/shard_map/all_to_all | solution.py:640
  47.9 5.5 %collective-permute-start.10 = (bf16[4,144,512]{2,1,0:T(8,128)(2,1)S(1)}, bf16[4,144,512]{2,1,0:T(8,128)(2,1)S(1)}, u32[]{:S(2)}, u32[]{:S(2)}) collective-permute-start(bf16[4,144,512]{2,1,0:T(8,128)(2,1)S(1)} %pad_maximum_fusion.refs_0_), channel_id=1, source_target_pairs={{0,1},{1,0},{2,3},{3,2},{4,5},{5,4},{6,7},{7,6},{8,9},{9,8},{10,11... | collective-permute-start | bytes 1769480 | tf_op jit(solution)/shard_map/ppermute | solution.py:643
  48.5 6.6 %collective-permute-start.12 = (bf16[4,144,512]{2,1,0:T(8,128)(2,1)}, bf16[4,144,512]{2,1,0:T(8,128)(2,1)}, u32[]{:S(2)}, u32[]{:S(2)}) collective-permute-start(bf16[4,144,512]{2,1,0:T(8,128)(2,1)} %copy-done.4), channel_id=1, source_target_pairs={{0,1},{1,0},{2,3},{3,2},{4,5},{5,4},{6,7},{7,6},{8,9},{9,8},{10,11... | collective-permute-start | bytes 1769480 | tf_op jit(solution)/shard_map/ppermute | solution.py:643
  48.6 31.9 %collective-permute-start.8 = (bf16[4,80,512]{2,1,0:T(8,128)(2,1)S(1)}, bf16[4,80,512]{2,1,0:T(8,128)(2,1)}, u32[]{:S(2)}, u32[]{:S(2)}) collective-permute-start(bf16[4,80,512]{2,1,0:T(8,128)(2,1)S(1)} %slice.163), channel_id=1, source_target_pairs={{0,16},{8,24},{16,0},{24,8},{1,17},{9,25},{17,1},{25,9},{2,18},{10... | collective-permute-start | bytes 983048 | tf_op jit(solution)/shard_map/ppermute | solution.py:645
  52.0 27.2 %collective-permute-start.9 = (bf16[4,64,512]{2,1,0:T(8,128)(2,1)}, bf16[4,64,512]{2,1,0:T(8,128)(2,1)}, u32[]{:S(2)}, u32[]{:S(2)}) collective-permute-start(bf16[4,64,512]{2,1,0:T(8,128)(2,1)} %slice.164), channel_id=1, source_target_pairs={{0,8},{8,0},{16,24},{24,16},{1,9},{9,1},{17,25},{25,17},{2,10},{10... | collective-permute-start | bytes 786440 | tf_op jit(solution)/shard_map/ppermute | solution.py:646
  80.6 5.5 %collective-permute-start.15 = (bf16[16,144,512]{2,1,0:T(8,128)(2,1)S(1)}, bf16[16,144,512]{2,1,0:T(8,128)(2,1)}, u32[]{:S(2)}, u32[]{:S(2)}) collective-permute-start(bf16[16,144,512]{2,1,0:T(8,128)(2,1)S(1)} %bitcast.70), channel_id=1, source_target_pairs={{0,1},{1,0},{2,3},{3,2},{4,5},{5,4},{6,7},{7,6},{8,9},{9,8},{10,11... | collective-permute-start | bytes 7077896 | tf_op jit(solution)/shard_map/ppermute | solution.py:669
  137.9 14.1 %collective-permute-start.17 = (bf16[16,144,512]{2,1,0:T(8,128)(2,1)}, bf16[16,144,512]{2,1,0:T(8,128)(2,1)}, u32[]{:S(2)}, u32[]{:S(2)}) collective-permute-start(bf16[16,144,512]{2,1,0:T(8,128)(2,1)} %get-tuple-element.76), channel_id=1, source_target_pairs={{0,1},{1,0},{2,3},{3,2},{4,5},{5,4},{6,7},{7,6},{8,9},{9,8},{10,11... | collective-permute-start | bytes 7077896 | tf_op jit(solution)/shard_map/ppermute | solution.py:689
  151.9 7.6 %collective-permute-start.16 = (bf16[16,144,512]{2,1,0:T(8,128)(2,1)}, bf16[16,144,512]{2,1,0:T(8,128)(2,1)}, u32[]{:S(2)}, u32[]{:S(2)}) collective-permute-start(bf16[16,144,512]{2,1,0:T(8,128)(2,1)} %get-tuple-element.74), channel_id=1, source_target_pairs={{0,1},{1,0},{2,3},{3,2},{4,5},{5,4},{6,7},{7,6},{8,9},{9,8},{10,11... | collective-permute-start | bytes 7077896 | tf_op jit(solution)/shard_map/ppermute | solution.py:692
  155.9 32.2 %all-to-all-start.1 = ((bf16[4,4,144,512]{3,2,1,0:T(8,128)(2,1)}), bf16[4,4,144,512]{3,2,1,0:T(8,128)(2,1)S(1)}, u32[]{:S(2)}, u32[]{:S(2)}) async-start(bf16[4,4,144,512]{3,2,1,0:T(8,128)(2,1)} %bitcast.20), calls=%async_computation.1 | async-start | bytes 4718592 | tf_op jit(solution)/shard_map/all_to_all | solution.py:681
  189.2 31.4 %all-to-all-start.2 = ((bf16[4,4,144,512]{3,2,1,0:T(8,128)(2,1)}), bf16[4,4,144,512]{3,2,1,0:T(8,128)(2,1)S(1)}, u32[]{:S(2)}, u32[]{:S(2)}) async-start(bf16[4,4,144,512]{3,2,1,0:T(8,128)(2,1)} %bitcast.19), calls=%async_computation.2 | async-start | bytes 4718592 | tf_op jit(solution)/shard_map/all_to_all | solution.py:681
  195.3 25.6 %collective-permute-start.20 = (bf16[144,512]{1,0:T(8,128)(2,1)}, bf16[144,512]{1,0:T(8,128)(2,1)S(1)}, u32[]{:S(2)}, u32[]{:S(2)}) collective-permute-start(bf16[144,512]{1,0:T(8,128)(2,1)} %get-tuple-element.101), channel_id=1, source_target_pairs={{0,6},{1,7},{2,0},{3,1},{4,2},{5,3},{6,4},{7,5},{8,14},{9,15},{10,... | collective-permute-start | bytes 442376 | tf_op jit(solution)/shard_map/ppermute | solution.py:686
  196.5 24.4 %collective-permute-start.19 = (bf16[144,512]{1,0:T(8,128)(2,1)}, bf16[144,512]{1,0:T(8,128)(2,1)S(1)}, u32[]{:S(2)}, u32[]{:S(2)}) collective-permute-start(bf16[144,512]{1,0:T(8,128)(2,1)} %get-tuple-element.102), channel_id=1, source_target_pairs={{0,4},{1,5},{2,6},{3,7},{4,0},{5,1},{6,2},{7,3},{8,12},{9,13},{10,... | collective-permute-start | bytes 442376 | tf_op jit(solution)/shard_map/ppermute | solution.py:686
  198.9 22.0 %collective-permute-start.18 = (bf16[144,512]{1,0:T(8,128)(2,1)}, bf16[144,512]{1,0:T(8,128)(2,1)S(1)}, u32[]{:S(2)}, u32[]{:S(2)}) collective-permute-start(bf16[144,512]{1,0:T(8,128)(2,1)} %get-tuple-element.103), channel_id=1, source_target_pairs={{0,2},{1,3},{2,4},{3,5},{4,6},{5,7},{6,0},{7,1},{8,10},{9,11},{10,... | collective-permute-start | bytes 442376 | tf_op jit(solution)/shard_map/ppermute | solution.py:686
  221.3 8.7 %collective-permute-start.21 = (bf16[144,512]{1,0:T(8,128)(2,1)S(1)}, bf16[144,512]{1,0:T(8,128)(2,1)S(1)}, u32[]{:S(2)}, u32[]{:S(2)}) collective-permute-start(bf16[144,512]{1,0:T(8,128)(2,1)S(1)} %get-tuple-element.94), channel_id=1, source_target_pairs={{0,2},{1,3},{2,4},{3,5},{4,6},{5,7},{6,0},{7,1},{8,10},{9,11},{10,... | collective-permute-start | bytes 442376 | tf_op jit(solution)/shard_map/ppermute | solution.py:686
  223.1 8.2 %collective-permute-start.23 = (bf16[144,512]{1,0:T(8,128)(2,1)S(1)}, bf16[144,512]{1,0:T(8,128)(2,1)S(1)}, u32[]{:S(2)}, u32[]{:S(2)}) collective-permute-start(bf16[144,512]{1,0:T(8,128)(2,1)S(1)} %get-tuple-element.95), channel_id=1, source_target_pairs={{0,6},{1,7},{2,0},{3,1},{4,2},{5,3},{6,4},{7,5},{8,14},{9,15},{10,... | collective-permute-start | bytes 442376 | tf_op jit(solution)/shard_map/ppermute | solution.py:686
  225.2 12.2 %collective-permute-start.22 = (bf16[144,512]{1,0:T(8,128)(2,1)S(1)}, bf16[144,512]{1,0:T(8,128)(2,1)S(1)}, u32[]{:S(2)}, u32[]{:S(2)}) collective-permute-start(bf16[144,512]{1,0:T(8,128)(2,1)S(1)} %get-tuple-element.96), channel_id=1, source_target_pairs={{0,4},{1,5},{2,6},{3,7},{4,0},{5,1},{6,2},{7,3},{8,12},{9,13},{10,... | collective-permute-start | bytes 442376 | tf_op jit(solution)/shard_map/ppermute | solution.py:686
  (15 other events, 121.0 us)

commit v3 on v2

--- a/solution.py
+++ b/solution.py
@@ -10,7 +10,6 @@
 STEP = 8
 REACH = (TAPS // 2) * STEP
 EPSILON = 1e-05
-SPLIT = 80
 SLAB = 512
 QUARTERS = 4
 AXES = ("dp", "fsdp")
@@ -140,7 +139,7 @@
             jax.ShapeDtypeStruct((rows, 128), f32),
         ],
         scratch_shapes=[pltpu.VMEM((rows + 2 * REACH, width), bf16), pltpu.VMEM((rows + 2 * REACH, width), bf16)],
-        compiler_params=vmem(60),
+        compiler_params=vmem(63),
         cost_estimate=cost(0, 24 * rows * width),
         name="prep",
     )(lengths, place, tokens, present.reshape(rows // 128, 128))
@@ -156,7 +155,7 @@
         which = core if n < per else 1 - core
         kind = first + n % per
         for hop in range(piece.shape[0]):
-            row = (((z - hop) & 3) * 2 + which) * body + (SPLIT if kind == 4 else 0)
+            row = (((z - hop - (2 if kind == 4 else 0)) & 3) * 2 + which) * body
             sites.append((piece.at[hop], min(kind, 3), row))
     return sites
 
@@ -207,7 +206,7 @@
             pltpu.SemaphoreType.DMA((sum(piece.shape[0] for piece in pieces),)),
             pltpu.SemaphoreType.DMA,
         ],
-        compiler_params=vmem(60),
+        compiler_params=vmem(63),
         cost_estimate=cost(depth * rows * width, 24 * rows * width),
         name="conv_forward",
     )(place, *pieces, stacked)
@@ -216,22 +215,34 @@
 def ff_copies(pieces, place, fast, store, sems):
     if not fast:
         return [pltpu.make_async_copy(pieces[0], store, sems.at[0])]
-    core, z, _ = place
+    core, own_z, dp = place
+    per = len(pieces) // 2
     copies = []
-    for piece, which in zip(pieces, (core, 1 - core)):
-        for seat in range(piece.shape[0]):
-            block = (seat // 4 * 4 + ((z - seat) & 3)) * 2 + which
-            copies.append(pltpu.make_async_copy(piece.at[seat], store.at[block], sems.at[len(copies)]))
+    for n, piece in enumerate(pieces):
+        which = core if n < per else 1 - core
+        kind = n % per
+        for hop in range(piece.shape[0]):
+            z = (own_z - hop - (2 if kind == 4 else 0)) & 3
+            block = ((dp ^ min(kind, 3)) * 4 + z) * 2 + which
+            copies.append(pltpu.make_async_copy(piece.at[hop], store.at[block], sems.at[len(copies)]))
     return copies
 
 
-def feed_kernel(place_ref, *refs, far, count, tiles, chunk, inner_rows, outer_rows, extra, fast, body):
+def relay_seat(r, k):
+    if k < 2:
+        return (1, r // 2 * 2 + k) if r % 2 else (0, r // 2 * 2 + k)
+    return (2, r % 2 * 2 + k - 2) if r // 2 else (0, 4 + r * 2 + k - 2)
+
+
+def feed_kernel(place_ref, *refs, far, count, outs, tiles, chunk, inner_rows, outer_rows, extra, fast, body):
     far_pieces, ff_pieces = refs[:far], refs[far : far + count]
     refs = refs[far + count :]
     stacked_ref, partial_ref, tokens_ref, cot_ref = refs[:4]
-    mixed_ref, d_hidden_ref, d_conv_ref, keep_ref, send_ref, sums_ref, far_ref = refs[4:11]
-    packed, w_in, w_far, small_ref, bend, slope_ref, normed_ref, hiddens, actives, d_outers, d_inners = refs[11:22]
-    tallies, ff_sems, far_sems, grad_sems, last_sems, out_sem = refs[22:]
+    mixed_ref, d_hidden_ref, d_conv_ref, sums_ref, far_ref = refs[4:9]
+    targets = refs[9 : 9 + outs]
+    refs = refs[9 + outs :]
+    packed, w_in, w_far, small_ref, bend, slope_ref, normed_ref, hiddens, actives, d_outers, d_inners = refs[:11]
+    tallies, ff_sems, far_sems, grad_sems, out_sem = refs[11:]
     slab = SLAB
     store = packed
     step = pl.program_id(0)
@@ -345,33 +356,19 @@
             add_tally(1, 0, d_hidden * first)
             add_tally(2, 0, d_hidden)
 
-    def grad_copies(j):
+    def grad_copies():
         copies = []
-        if fast:
-            z = place[1]
-            below = pl.ds(top + extra, outer_rows)
-            for n, (target, which) in enumerate(((keep_ref, core), (send_ref, 1 - core))):
+        if not fast:
+            for n, target in enumerate(targets):
+                copies.append(pltpu.make_async_copy(store.at[pl.ds(n, 1)], target, grad_sems.at[n]))
+            return copies
+        for n, which in enumerate((core, 1 - core)):
+            for r in range(4):
                 for k in range(4):
-                    seat = j * 4 + ((k - z) & 3)
+                    array, seat = relay_seat(r, k)
+                    block = ((place[2] ^ r) * 4 + ((place[1] + k) & 3)) * 2 + which
                     copies.append(
-                        pltpu.make_async_copy(
-                            store.at[2 * (4 * j + k) + which, below], target.at[seat, below], grad_sems.at[j, 4 * n + k]
-                        )
-                    )
-        return copies
-
-    def last_copies():
-        copies = []
-        if fast:
-            z = place[1]
-            above = pl.ds(0, top + extra)
-            for block in range(blocks // 2):
-                seat = block // 4 * 4 + ((block % 4 - z) & 3)
-                for n, (target, which) in enumerate(((keep_ref, core), (send_ref, 1 - core))):
-                    copies.append(
-                        pltpu.make_async_copy(
-                            store.at[2 * block + which, above], target.at[seat, above], last_sems.at[n, block]
-                        )
+                        pltpu.make_async_copy(store.at[block], targets[3 * n + array].at[seat], grad_sems.at[len(copies)])
                     )
         return copies
 
@@ -391,8 +388,6 @@
         d_in = dot_rows(hiddens[...], d_inners[:, part]).astype(bf16)
         above = pl.ds(pl.multiple_of(j * inner_rows, inner_rows), inner_rows)
         store[:, above] = d_in.reshape(blocks, inner_rows, width)
-        for copy in grad_copies(j):
-            copy.start()
 
     @pl.when(step == pl.num_programs(0) - 1)
     def _():
@@ -405,18 +400,11 @@
             for dp in range(blocks // 8):
                 line = jnp.concatenate([head, sums_ref[6 + dp : 7 + dp].astype(bf16), rest])
                 store[8 * dp : 8 * dp + 8, top : top + extra] = jnp.broadcast_to(line, (8, extra, width))
-            copies = last_copies()
-            for copy in copies:
-                copy.start()
-            for j in range(cols):
-                copies += grad_copies(j)
-            for copy in copies:
-                copy.wait()
-        else:
-            for n, target in enumerate((keep_ref, send_ref)):
-                copy = pltpu.make_async_copy(store.at[pl.ds(n, 1)], target, grad_sems.at[0, n])
-                copy.start()
-                copy.wait()
+        copies = grad_copies()
+        for copy in copies:
+            copy.start()
+        for copy in copies:
+            copy.wait()
 
 
 def feed(place, far, pieces, stacked, partial, tokens, cotangent, inner_rows, outer_rows, extra, total, fast, body):
@@ -426,25 +414,24 @@
     tiles, cols = rows // tile, total // width
     share = cols * inner_rows + extra + outer_rows
     depth = stacked.shape[1] // QUARTERS
+    seats = (8, 4, 4) * 2 if fast else (1, 1)
     tall = pl.BlockSpec((tile, width), lambda i: (jnp.minimum(i, tiles - 1), 0))
     last = pl.BlockSpec((tile, depth), lambda i: (jnp.minimum(i, tiles - 1), QUARTERS - 1))
     return pl.pallas_call(
         functools.partial(
-            feed_kernel, far=len(far), count=len(pieces), tiles=tiles, chunk=512, inner_rows=inner_rows,
+            feed_kernel, far=len(far), count=len(pieces), outs=len(seats), tiles=tiles, chunk=512, inner_rows=inner_rows,
             outer_rows=outer_rows, extra=extra, fast=fast, body=body,
         ),
         grid=(tiles + cols,),
         in_specs=[SMEM] + [ANY] * (len(far) + len(pieces)) + [last, tall, tall, tall],
-        out_specs=[tall, tall, tall, ANY, ANY, pl.BlockSpec((16, width), lambda i: (0, 0)), ANY],
+        out_specs=[tall, tall, tall, pl.BlockSpec((16, width), lambda i: (0, 0)), ANY] + [ANY] * len(seats),
         out_shape=[
             jax.ShapeDtypeStruct((rows, width), bf16),
             jax.ShapeDtypeStruct((rows, width), f32),
             jax.ShapeDtypeStruct((rows, width), bf16),
-            jax.ShapeDtypeStruct((blocks // 2, share, width), bf16),
-            jax.ShapeDtypeStruct((blocks // 2, share, width), bf16),
             jax.ShapeDtypeStruct((16, width), f32),
             jax.ShapeDtypeStruct((depth, width), bf16),
-        ],
+        ] + [jax.ShapeDtypeStruct((count, share, width), bf16) for count in seats],
         scratch_shapes=[
             pltpu.VMEM((blocks, share, width), bf16),
             pltpu.VMEM((width, total), bf16),
@@ -458,13 +445,12 @@
             pltpu.VMEM((rows, width), bf16),
             pltpu.VMEM((rows, total), bf16),
             pltpu.VMEM((8 * extra, width), f32),
+            pltpu.SemaphoreType.DMA((sum(piece.shape[0] for piece in pieces),)),
+            pltpu.SemaphoreType.DMA((sum(piece.shape[0] for piece in far),)),
             pltpu.SemaphoreType.DMA((blocks,)),
-            pltpu.SemaphoreType.DMA((sum(piece.shape[0] for piece in far),)),
-            pltpu.SemaphoreType.DMA((cols, 8)),
-            pltpu.SemaphoreType.DMA((2, max(blocks // 2, 1))),
             pltpu.SemaphoreType.DMA,
         ],
-        compiler_params=vmem(60),
+        compiler_params=vmem(63),
         cost_estimate=cost(6 * rows * width * total, 40 * rows * width),
         name="feed",
     )(place, *far, *pieces, stacked, partial, tokens, cotangent)
@@ -530,7 +516,7 @@
             pltpu.VMEM((TAPS * channels, width), bf16),
             pltpu.SemaphoreType.DMA((2, blocks)),
         ],
-        compiler_params=vmem(60),
+        compiler_params=vmem(63),
         cost_estimate=cost(TAPS * rows * width * channels, 12 * rows * width),
         name="conv_grad",
     )(lengths, place, masked, d_conv)
@@ -586,7 +572,7 @@
             pltpu.VMEM((TAPS * width, width), bf16),
             pltpu.SemaphoreType.DMA((QUARTERS,)),
         ],
-        compiler_params=vmem(60),
+        compiler_params=vmem(63),
         cost_estimate=cost(TAPS * rows * width * width, 12 * rows * width),
         name="token_grad",
     )(lengths, place, near, far, d_conv, d_hidden, keep)
@@ -631,20 +617,22 @@
         own_line = ((line < 6) & (lane // n == seat)) | ((line == 6 + dp) & (lane // few == fsdp))
         lines = jnp.where(own_line, lines, 0)
         ff_own = jnp.concatenate([w_in[:, j * width : (j + 1) * width] for j in range(cols)] + [lines, w_out], axis=0)
-        stacked, masked, keep = prep(lengths, place, tokens, present)
-        column, ff_own, stacked, masked, keep = bar((column, ff_own, stacked, masked, keep))
+        column, ff_own, late_tokens = bar((column, ff_own, tokens))
         beside_x = lax.ppermute(column, "dp", across[1])
         beside_y = lax.ppermute(column, "dp", across[2])
-        ff_column = jnp.stack(from_column(ff_own))
-        column, beside_x, beside_y, ff_column = bar((column, beside_x, beside_y, ff_column))
-        ff = lax.all_to_all(jnp.broadcast_to(ff_column, (n_dp,) + ff_column.shape), "dp", 0, 0, tiled=True)
-        ff = (ff.reshape((blocks,) + ff_own.shape),)
+        ff_rest = from_column(ff_own)
+        stacked, masked, keep = prep(lengths, place, late_tokens, present)
+        column, beside_x, beside_y, ff_rest, stacked, masked, keep = bar(
+            (column, beside_x, beside_y, ff_rest, stacked, masked, keep)
+        )
+        ff_column = jnp.stack(ff_rest)
         near = (column, beside_x, beside_y)
         near = near + tuple(lax.ppermute(piece, "fsdp", swap) for piece in near)
         far = (
-            lax.ppermute(beside_x[:, :SPLIT], "dp", across[2]),
-            lax.ppermute(beside_y[:, SPLIT:], "dp", across[1]),
+            lax.ppermute(beside_x[:2], "dp", across[2]),
+            lax.ppermute(beside_y[2:], "dp", across[1]),
         )
+        ff = (ff_column, lax.ppermute(ff_column, "dp", across[1]), lax.ppermute(ff_column, "dp", across[2]))
     else:
         place = jnp.zeros((3,), jnp.int32)
         gather = functools.partial(lax.all_gather, axis_name=AXES, axis=0, tiled=True)
@@ -664,38 +652,45 @@
 
     partial, w_near = conv_forward(place, near, stacked, fast, body)
     if fast:
-        far, ff, partial = lax.optimization_barrier((far, ff, partial))
+        far, ff, partial = bar((far, ff, partial))
+        ff = ff + (
+            lax.ppermute(ff[1][:2], "dp", across[2]),
+            lax.ppermute(ff[2][2:], "dp", across[1]),
+        )
         far = far + tuple(lax.ppermute(piece, "fsdp", swap) for piece in far)
         ff = ff + tuple(lax.ppermute(piece, "fsdp", swap) for piece in ff)
-    mixed, d_hidden, d_conv, ff_keep, ff_send, sums, w_far = feed(
+    mixed, d_hidden, d_conv, sums, w_far, *ff_grads = feed(
         place, far, ff, stacked, partial, tokens, cotangent, inner_rows, outer_rows, extra, total, fast, body
     )
     def added(terms):
         return sum(term.astype(f32) for term in terms)
 
-    def chip_sum(kept, came):
-        chip = added((kept, came)).astype(bf16)
-        return chip.reshape((n_dp, blocks // n_dp) + chip.shape[1:])
-
-    def plane_swap(chip):
-        plane = lax.all_to_all(chip, "dp", 0, 0, tiled=True)
-        return [plane[r] for r in range(n_dp)]
-
-    def line_swap(plane):
-        line = [added(part[k] for part in plane).astype(bf16) for k in range(4)]
+    def line_swap(line):
         return [line[0]] + [lax.ppermute(line[k], "fsdp", along[k]) for k in (1, 2, 3)]
 
+    def rounded(*terms):
+        return added(terms).astype(bf16)
+
     if fast:
-        ff_came = lax.ppermute(ff_send, "fsdp", swap)
-        ff_plane = plane_swap(chip_sum(ff_keep, ff_came))
+        ff_near, ff_far_a, ff_far_b = ff_grads[:3]
+        came_a, came_b, came = (lax.ppermute(ff_grads[3 + n], "fsdp", swap) for n in (1, 2, 0))
+        a_far, b_far, d_conv = bar((ff_far_a + came_a, ff_far_b + came_b, d_conv))
+        a_came = lax.ppermute(a_far, "dp", across[1])
+        b_came = lax.ppermute(b_far, "dp", across[2])
         conv_keep, conv_send = conv_grad(lengths, place, masked, d_conv, blocks, body)
+        a_came, b_came, came, conv_keep, conv_send, d_conv = bar((a_came, b_came, came, conv_keep, conv_send, d_conv))
         conv_came = lax.ppermute(conv_send, "fsdp", swap)
-        conv_chip, ff_plane, d_conv = bar((chip_sum(conv_keep, conv_came), ff_plane, d_conv))
-        conv_plane = plane_swap(conv_chip)
-        ff_line = line_swap(ff_plane)
+        a_last = lax.ppermute(rounded(ff_near[2:4], came[2:4], a_came[2:]), "dp", across[2])
+        b_last = lax.ppermute(rounded(ff_near[6:], came[6:], b_came[2:]), "dp", across[1])
+        conv_chip = conv_keep + conv_came
+        conv_chip, a_last, b_last, d_conv = bar((conv_chip, a_last, b_last, d_conv))
+        conv_plane = lax.all_to_all(conv_chip.reshape(4, 4, body, width), "dp", 0, 0, tiled=True)
+        line = [rounded(ff_near[k], came[k], a_came[k], a_last[k]) for k in (0, 1)]
+        line += [rounded(ff_near[4 + k], came[4 + k], b_came[k], b_last[k]) for k in (0, 1)]
+        ff_line = line_swap(line)
         d_tokens = token_grad(lengths, place, w_near, w_far, d_conv, d_hidden, keep)
         d_tokens, ff_line, conv_plane = bar((d_tokens, ff_line, conv_plane))
-        conv_line = line_swap(conv_plane)
+        conv_line = line_swap([added(conv_plane[r, k] for r in range(4)).astype(bf16) for k in range(4)])
         ff_share = added(ff_line)
         d_conv_w = added(conv_line)
         top = cols * inner_rows
@@ -708,7 +703,7 @@
     else:
         conv_pair = conv_grad(lengths, place, masked, d_conv, blocks, body)
         d_tokens = token_grad(lengths, place, w_near, w_far, d_conv, d_hidden, keep)
-        ff_share = jnp.concatenate((ff_keep, ff_send), axis=0)
+        ff_share = jnp.concatenate(ff_grads, axis=0)
         scatter = functools.partial(lax.psum_scatter, axis_name=AXES, scatter_dimension=0, tiled=True)
         d_in_full = jnp.concatenate(
             [ff_share[:, j * inner_rows : (j + 1) * inner_rows].reshape(-1, width) for j in range(cols)], axis=1

time: 239 us -> 214 us (0.90)
  waiting for transfers between devices: 62.3 us -> 32.4 us
  other arithmetic: 13.4 us -> 17.1 us
    all_to_all x3 -> x1, waiting for transfers between devices: 27.6 us -> 4.21 us  [on_device(): lax.all_to_all(conv_chip.reshape(4, 4, body, width), 'dp', 0, 0, tiled=True)]
    ppermute x3 -> x13, starting transfers between devices: 3.62 us -> 12.1 us  [the longest x1 1.59 us: on_device(): lax.ppermute(ff[1][:2], 'dp', across[2])]
    convert_element_type x2 -> x1, other arithmetic: 8.41 us -> 1.66 us  [rounded(): return added(terms).astype(bf16)]
    all_to_all x3 -> x1, starting transfers between devices: 11.1 us -> 4.64 us  [on_device(): lax.all_to_all(conv_chip.reshape(4, 4, body, width), 'dp', 0, 0, tiled=True)]
    add x0 -> x3, other arithmetic: none -> 5.22 us  [the longest x2 3 us: on_device(): a_far, b_far, d_conv = bar((ff_far_a + came_a, ff_far_b + came_b, d_conv))]
    ppermute x2, waiting for transfers between devices: 4.64 us -> 0.01 us  [on_device(): far = far + tuple((lax.ppermute(piece, 'fsdp', swap) for piece in far))]
    ppermute x6, waiting for transfers between devices: 10.5 us -> 7.02 us  [from_column(): return [shard] + [lax.ppermute(shard, 'fsdp', along[k]) for k in (1, 2, 3)]]
    slice x2 -> x4, local copies, waits for them, and re-layouts: 1.69 us -> 4.85 us  [the longest x1 1.7 us: on_device(): beside_y[2:]]
  transfers between devices with their start and end apart: 27 -> 39, of which waited for: 11 -> 15; matrix products, arithmetic and copies ran while one was open for 9% -> 11% of each run, Pallas kernels for 24% -> 26%
where the time goes in v3:
time: 214 us; the launch traced here: 213 us
  Pallas kernels  107 us (50%)
  starting transfers between devices  40.3 us (19%)
  waiting for transfers between devices  32.4 us (15%)
  other arithmetic  17.1 us (8%)
  local copies, waits for them, and re-layouts  14.7 us (7%)
    pallas_call x1, Pallas kernels, feed(): pl.pallas_call(functools.partial(feed_kernel, far=len(far), count=len(pie...  51.3 us
    pallas_call x1, Pallas kernels, token_grad(): pl.pallas_call(functools.partial(token_grad_kernel, wins=lengths.shape[1]...  16.2 us
    pallas_call x1, Pallas kernels, conv_forward(): pl.pallas_call(functools.partial(conv_kernel, fast=fast, body=body), grid...  14.1 us
    pallas_call x1, Pallas kernels, conv_grad(): pl.pallas_call(functools.partial(conv_grad_kernel, wins=lengths.shape[1],...  13.3 us
    pallas_call x1, Pallas kernels, prep(): pl.pallas_call(functools.partial(prep_kernel, tile=tile, wins=lengths.sha...  12.3 us
    ppermute x6, starting transfers between devices, line_swap(): lax.ppermute(line[k], 'fsdp', along[k])  10.5 us
    ppermute x6, starting transfers between devices, from_column(): return [shard] + [lax.ppermute(shard, 'fsdp', along[k]) for k in (1, 2, 3)]  8.31 us
    ppermute x6, waiting for transfers between devices, from_column(): return [shard] + [lax.ppermute(shard, 'fsdp', along[k]) for k in (1, 2, 3)]  7.02 us
  transfers between devices with their start and end apart: 39, of which 15 were waited for; matrix products, arithmetic and copies ran while one was open for 11% of the time, Pallas kernels for 26%

profile of v3, /device:TPU:0, one launch (start us, length us, event | category | flops | bytes accessed | tf_op | source)
XLA Modules:
  0.0 212.7 jit_solution(11367023306773586618)
XLA Ops:
  0.6 3.1 %collective-permute-start = (bf16[144,512]{1,0:T(8,128)(2,1)}, bf16[144,512]{1,0:T(8,128)(2,1)S(1)}, u32[]{:S(2)}, u32[]{:S(2)}) collective-permute-start(bf16[144,512]{1,0:T(8,128)(2,1)} %param.17), channel_id=1, source_target_pairs={{0,2},{1,3},{2,4},{3,5},{4,6},{5,7},{6,0},{7,1},{8,10},{9,11},{10,... | collective-permute-start | bytes 442376 | tf_op jit(solution)/shard_map/ppermute | solution.py:605
  3.7 2.1 collective-permute-start.2
  12.4 6.9 %collective-permute-done.1 = bf16[144,512]{1,0:T(8,128)(2,1)S(1)} collective-permute-done((bf16[144,512]{1,0:T(8,128)(2,1)}, bf16[144,512]{1,0:T(8,128)(2,1)S(1)}, u32[]{:S(2)}, u32[]{:S(2)}) %collective-permute-start.1) | collective-permute-done | bytes 147488 | tf_op jit(solution)/shard_map/ppermute | solution.py:605
  26.1 12.3 %prep.1 = (bf16[2048,4608]{1,0:T(8,128)(2,1)}, bf16[512,2048]{1,0:T(8,128)(2,1)}, f32[2048,128]{1,0:T(8,128)}) custom-call(s32[1,4]{1,0:T(1,128)} %len_ref.5, s32[3]{0:T(128)} %pad_add_fusion.place_ref, bf16[2048,512]{1,0:T(8,128)(2,1)} %refs_16_.1, s32[16,128]{1,0:T(8,128)} %bitcast.58), custom_call_target="tpu_custom_call" | custom-call | bytes 786432 | tf_op jit(solution)/shard_map/prep/pallas_call | solution.py:129
  39.1 1.9 pad_maximum_fusion.1.refs_4_
  43.0 1.7 slice.164
  48.6 14.1 %conv_forward.1 = (f32[2048,512]{1,0:T(8,128)}, bf16[3456,512]{1,0:T(8,128)(2,1)}) custom-call(s32[3]{0:T(128)} %pad_add_fusion.place_ref, bf16[4,144,512]{2,1,0:T(8,128)(2,1)} %copy-done, bf16[4,144,512]{2,1,0:T(8,128)(2,1)} %collective-permute-done.3.refs_1_, bf16[4,144,512]{2,1,0:T(8,128)(2,1)} %collective-permute-done.4.refs_2_, ...), custom_call_target="tpu_custom_call" | custom-call | flops 113246208 | bytes 786432 | tf_op jit(solution)/shard_map/conv_forward/pallas_call | solution.py:198
  68.3 4.6 %collective-permute-done.18.refs_8_ = bf16[2,144,512]{2,1,0:T(8,128)(2,1)S(1)} collective-permute-done((bf16[2,144,512]{2,1,0:T(8,128)(2,1)S(1)}, bf16[2,144,512]{2,1,0:T(8,128)(2,1)S(1)}, u32[]{:S(2)}, u32[]{:S(2)}) %collective-permute-start.18) | collective-permute-done | bytes 294944 | tf_op jit(solution)/shard_map/ppermute | solution.py:658
  74.9 1.8 collective-permute-done.23.refs_13_
  78.9 51.3 %feed.1 = (bf16[2048,512]{1,0:T(8,128)(2,1)}, f32[2048,512]{1,0:T(8,128)}, bf16[2048,512]{1,0:T(8,128)(2,1)}, f32[16,512]{1,0:T(8,128)}, bf16[1152,512]{1,0:T(8,...) custom-call(s32[3]{0:T(128)} %pad_add_fusion.place_ref, ...), custom_call_target="tpu_custom_call" | custom-call | flops 402653184 | bytes 1310720 | tf_op jit(solution)/shard_map/feed/pallas_call | solution.py:420
  132.5 2.0 add.176
  138.5 13.3 %conv_grad.1 = (bf16[16,144,512]{2,1,0:T(8,128)(2,1)}, bf16[16,144,512]{2,1,0:T(8,128)(2,1)}) custom-call(s32[1,4]{1,0:T(1,128)} %len_ref.5, s32[3]{0:T(128)} %pad_add_fusion.place_ref, bf16[512,2048]{1,0:T(8,128)(2,1)} %get-tuple-element.99.masked_ref, bf16[2048,512]{1,0:T(8,128)(2,1)} %get-tuple-element.110.d_conv_ref), custom_call_target="tpu_custom_call" | custom-call | flops 150994944 | bytes 393216 | tf_op jit(solution)/shard_map/conv_grad/pallas_call | solution.py:507
  157.2 2.2 %add.178 = bf16[16,144,512]{2,1,0:T(8,128)(2,1)} add(bf16[16,144,512]{2,1,0:T(8,128)(2,1)S(1)} %copy-done.1, bf16[16,144,512]{2,1,0:T(8,128)(2,1)S(1)} %collective-permute-done.29) | non-fusion elementwise | flops 1179648 | bytes 7077888 | tf_op jit(solution)/shard_map/add | solution.py:685
  159.4 4.1 %collective-permute-done.31 = bf16[2,144,512]{2,1,0:T(8,128)(2,1)S(1)} collective-permute-done((bf16[2,144,512]{2,1,0:T(8,128)(2,1)S(1)}, bf16[2,144,512]{2,1,0:T(8,128)(2,1)S(1)}, u32[]{:S(2)}, u32[]{:S(2)}) %collective-permute-start.31) | collective-permute-done | bytes 294944 | tf_op jit(solution)/shard_map/ppermute | solution.py:684
  163.7 4.6 %all-to-all-start = ((bf16[4,4,144,512]{3,2,1,0:T(8,128)(2,1)}), bf16[4,4,144,512]{3,2,1,0:T(8,128)(2,1)}, u32[]{:S(2)}, u32[]{:S(2)}) async-start(bf16[4,4,144,512]{3,2,1,0:T(8,128)(2,1)} %bitcast.22), calls=%async_computation | async-start | bytes 4718592 | tf_op jit(solution)/shard_map/all_to_all | solution.py:687
  168.4 2.3 %fusion.5 = (bf16[144,512]{1,0:T(8,128)(2,1)}, bf16[144,512]{1,0:T(8,128)(2,1)}, bf16[144,512]{1,0:T(8,128)(2,1)S(1)}, bf16[144,512]{1,0:T(8,128)(2,1)S(1)}) fusion(bf16[2,144,512]{2,1,0:T(8,128)(2,1)S(1)} %collective-permute-done.31, bf16[4,144,512]{2,1,0:T(8,128)(2,1)} %collective-permute-done.27, bf16[8,144,512]{2,1,0:T(8,128)(2,1)} %collective-permute-done.28, ...), kind=kLoop, calls=%fused_computation.19 | loop fusion | flops 2359296 | bytes 2949120 | tf_op jit(solution)/shard_map/add | solution.py:666
  170.7 3.3 %collective-permute-start.34 = (bf16[144,512]{1,0:T(8,128)(2,1)}, bf16[144,512]{1,0:T(8,128)(2,1)S(1)}, u32[]{:S(2)}, u32[]{:S(2)}) collective-permute-start(bf16[144,512]{1,0:T(8,128)(2,1)} %get-tuple-element.122), channel_id=1, source_target_pairs={{0,6},{1,7},{2,0},{3,1},{4,2},{5,3},{6,4},{7,5},{8,14},{9,15},{10,... | collective-permute-start | bytes 442376 | tf_op jit(solution)/shard_map/ppermute | solution.py:669
  175.4 16.2 %token_grad.1 = f32[2048,512]{1,0:T(8,128)} custom-call(s32[1,4]{1,0:T(1,128)} %len_ref.5, s32[3]{0:T(128)} %pad_add_fusion.place_ref, bf16[3456,512]{1,0:T(8,128)(2,1)} %get-tuple-element.89.near_ref, bf16[1152,512]{1,0:T(8,128)(2,1)} %get-tuple-element.90.far_ref, bf16[2048,512]{1,0:T(8,128)(2,1)} %get-tuple-element.110.d_conv_ref, ...), custom_call_target="tpu_custom_call" | custom-call | flops 150994944 | bytes 393216 | tf_op jit(solution)/shard_map/token_grad/pallas_call | solution.py:563
  191.6 4.2 %all-to-all-done = bf16[4,4,144,512]{3,2,1,0:T(8,128)(2,1)} async-done(((bf16[4,4,144,512]{3,2,1,0:T(8,128)(2,1)}), bf16[4,4,144,512]{3,2,1,0:T(8,128)(2,1)}, u32[]{:S(2)}, u32[]{:S(2)}) %all-to-all-start) | async-done | bytes 2359328 | tf_op jit(solution)/shard_map/all_to_all | solution.py:687
  196.0 1.7 fusion.7
  197.7 3.0 %collective-permute-start.35 = (bf16[144,512]{1,0:T(8,128)(2,1)S(1)}, bf16[144,512]{1,0:T(8,128)(2,1)S(1)}, u32[]{:S(2)}, u32[]{:S(2)}) collective-permute-start(bf16[144,512]{1,0:T(8,128)(2,1)S(1)} %get-tuple-element.126), channel_id=1, source_target_pairs={{0,2},{1,3},{2,4},{3,5},{4,6},{5,7},{6,0},{7,1},{8,10},{9,11},{10,... | collective-permute-start | bytes 442376 | tf_op jit(solution)/shard_map/ppermute | solution.py:669
  201.6 1.8 collective-permute-start.37
  206.3 4.5 %collective-permute-done.36 = bf16[144,512]{1,0:T(8,128)(2,1)S(1)} collective-permute-done((bf16[144,512]{1,0:T(8,128)(2,1)S(1)}, bf16[144,512]{1,0:T(8,128)(2,1)S(1)}, u32[]{:S(2)}, u32[]{:S(2)}) %collective-permute-start.36) | collective-permute-done | bytes 147488 | tf_op jit(solution)/shard_map/ppermute | solution.py:669
  210.7 2.0 fusion.1
  (127 shorter events, 46.9 us)
Async XLA Ops:
  0.6 11.6 %collective-permute-start = (bf16[144,512]{1,0:T(8,128)(2,1)}, bf16[144,512]{1,0:T(8,128)(2,1)S(1)}, u32[]{:S(2)}, u32[]{:S(2)}) collective-permute-start(bf16[144,512]{1,0:T(8,128)(2,1)} %param.17), channel_id=1, source_target_pairs={{0,2},{1,3},{2,4},{3,5},{4,6},{5,7},{6,0},{7,1},{8,10},{9,11},{10,... | collective-permute-start | bytes 442376 | tf_op jit(solution)/shard_map/ppermute | solution.py:605
  5.8 13.5 %collective-permute-start.1 = (bf16[144,512]{1,0:T(8,128)(2,1)}, bf16[144,512]{1,0:T(8,128)(2,1)S(1)}, u32[]{:S(2)}, u32[]{:S(2)}) collective-permute-start(bf16[144,512]{1,0:T(8,128)(2,1)} %param.17), channel_id=1, source_target_pairs={{0,4},{1,5},{2,6},{3,7},{4,0},{5,1},{6,2},{7,3},{8,12},{9,13},{10,... | collective-permute-start | bytes 442376 | tf_op jit(solution)/shard_map/ppermute | solution.py:605
  20.3 18.2 %collective-permute-start.4 = (bf16[4,144,512]{2,1,0:T(8,128)(2,1)S(1)}, bf16[4,144,512]{2,1,0:T(8,128)(2,1)}, u32[]{:S(2)}, u32[]{:S(2)}) collective-permute-start(bf16[4,144,512]{2,1,0:T(8,128)(2,1)S(1)} %pad_maximum_fusion.refs_0_), channel_id=1, source_target_pairs={{0,16},{8,24},{16,0},{24,8},{1,17},{9,25},{17,1},{25,9},{2,18},{10... | collective-permute-start | bytes 1769480 | tf_op jit(solution)/shard_map/ppermute | solution.py:622
  21.9 16.6 %collective-permute-start.3 = (bf16[4,144,512]{2,1,0:T(8,128)(2,1)S(1)}, bf16[4,144,512]{2,1,0:T(8,128)(2,1)}, u32[]{:S(2)}, u32[]{:S(2)}) collective-permute-start(bf16[4,144,512]{2,1,0:T(8,128)(2,1)S(1)} %pad_maximum_fusion.refs_0_), channel_id=1, source_target_pairs={{0,8},{8,0},{16,24},{24,16},{1,9},{9,1},{17,25},{25,17},{2,10},{10... | collective-permute-start | bytes 1769480 | tf_op jit(solution)/shard_map/ppermute | solution.py:621
  23.4 15.0 %collective-permute-start.7 = (bf16[144,512]{1,0:T(8,128)(2,1)S(1)}, bf16[144,512]{1,0:T(8,128)(2,1)S(1)}, u32[]{:S(2)}, u32[]{:S(2)}) collective-permute-start(bf16[144,512]{1,0:T(8,128)(2,1)S(1)} %constant_dynamic-update-slice_fusion), channel_id=1, source_target_pairs={{0,6},{1,7},{2,0},{3,1},{4,2},{5,3},{6,4},{7,5},{8,14},{9,15},{10,... | collective-permute-start | bytes 442376 | tf_op jit(solution)/shard_map/ppermute | solution.py:605
  25.0 13.4 %collective-permute-start.6 = (bf16[144,512]{1,0:T(8,128)(2,1)S(1)}, bf16[144,512]{1,0:T(8,128)(2,1)}, u32[]{:S(2)}, u32[]{:S(2)}) collective-permute-start(bf16[144,512]{1,0:T(8,128)(2,1)S(1)} %constant_dynamic-update-slice_fusion), channel_id=1, source_target_pairs={{0,4},{1,5},{2,6},{3,7},{4,0},{5,1},{6,2},{7,3},{8,12},{9,13},{10,... | collective-permute-start | bytes 442376 | tf_op jit(solution)/shard_map/ppermute | solution.py:605
  25.0 13.4 %collective-permute-start.5 = (bf16[144,512]{1,0:T(8,128)(2,1)S(1)}, bf16[144,512]{1,0:T(8,128)(2,1)}, u32[]{:S(2)}, u32[]{:S(2)}) collective-permute-start(bf16[144,512]{1,0:T(8,128)(2,1)S(1)} %constant_dynamic-update-slice_fusion), channel_id=1, source_target_pairs={{0,2},{1,3},{2,4},{3,5},{4,6},{5,7},{6,0},{7,1},{8,10},{9,11},{10,... | collective-permute-start | bytes 442376 | tf_op jit(solution)/shard_map/ppermute | solution.py:605
  39.0 9.6 %collective-permute-start.14 = (bf16[4,144,512]{2,1,0:T(8,128)(2,1)}, bf16[4,144,512]{2,1,0:T(8,128)(2,1)}, u32[]{:S(2)}, u32[]{:S(2)}) collective-permute-start(bf16[4,144,512]{2,1,0:T(8,128)(2,1)} %collective-permute-done.4.refs_2_), channel_id=1, source_target_pairs={{0,1},{1,0},{2,3},{3,2},{4,5},{5,4},{6,7},{7,6},{8,9},{9,8},{10,11... | collective-permute-start | bytes 1769480 | tf_op jit(solution)/shard_map/ppermute | solution.py:630
  41.0 22.4 %collective-permute-start.11 = (bf16[4,144,512]{2,1,0:T(8,128)(2,1)}, bf16[4,144,512]{2,1,0:T(8,128)(2,1)}, u32[]{:S(2)}, u32[]{:S(2)}) collective-permute-start(bf16[4,144,512]{2,1,0:T(8,128)(2,1)} %pad_maximum_fusion.1.refs_4_), channel_id=1, source_target_pairs={{0,16},{8,24},{16,0},{24,8},{1,17},{9,25},{17,1},{25,9},{2,18},{10... | collective-permute-start | bytes 1769480 | tf_op jit(solution)/shard_map/ppermute | solution.py:635
  41.5 21.9 %collective-permute-start.10 = (bf16[4,144,512]{2,1,0:T(8,128)(2,1)}, bf16[4,144,512]{2,1,0:T(8,128)(2,1)}, u32[]{:S(2)}, u32[]{:S(2)}) collective-permute-start(bf16[4,144,512]{2,1,0:T(8,128)(2,1)} %pad_maximum_fusion.1.refs_4_), channel_id=1, source_target_pairs={{0,8},{8,0},{16,24},{24,16},{1,9},{9,1},{17,25},{25,17},{2,10},{10... | collective-permute-start | bytes 1769480 | tf_op jit(solution)/shard_map/ppermute | solution.py:635
  45.6 17.9 %collective-permute-start.9 = (bf16[2,144,512]{2,1,0:T(8,128)(2,1)}, bf16[2,144,512]{2,1,0:T(8,128)(2,1)S(1)}, u32[]{:S(2)}, u32[]{:S(2)}) collective-permute-start(bf16[2,144,512]{2,1,0:T(8,128)(2,1)} %slice.164), channel_id=1, source_target_pairs={{0,8},{8,0},{16,24},{24,16},{1,9},{9,1},{17,25},{25,17},{2,10},{10... | collective-permute-start | bytes 884744 | tf_op jit(solution)/shard_map/ppermute | solution.py:633
  47.1 16.4 %collective-permute-start.8 = (bf16[2,144,512]{2,1,0:T(8,128)(2,1)S(1)}, bf16[2,144,512]{2,1,0:T(8,128)(2,1)S(1)}, u32[]{:S(2)}, u32[]{:S(2)}) collective-permute-start(bf16[2,144,512]{2,1,0:T(8,128)(2,1)S(1)} %slice.163), channel_id=1, source_target_pairs={{0,16},{8,24},{16,0},{24,8},{1,17},{9,25},{17,1},{25,9},{2,18},{10... | collective-permute-start | bytes 884744 | tf_op jit(solution)/shard_map/ppermute | solution.py:632
  67.8 9.3 %collective-permute-start.20 = (bf16[4,144,512]{2,1,0:T(8,128)(2,1)}, bf16[4,144,512]{2,1,0:T(8,128)(2,1)S(1)}, u32[]{:S(2)}, u32[]{:S(2)}) collective-permute-start(bf16[4,144,512]{2,1,0:T(8,128)(2,1)} %collective-permute-done.10.refs_5_), channel_id=1, source_target_pairs={{0,1},{1,0},{2,3},{3,2},{4,5},{5,4},{6,7},{7,6},{8,9},{9,8},{10,11... | collective-permute-start | bytes 1769480 | tf_op jit(solution)/shard_map/ppermute | solution.py:661
  130.8 21.1 %collective-permute-start.28 = (bf16[8,144,512]{2,1,0:T(8,128)(2,1)}, bf16[8,144,512]{2,1,0:T(8,128)(2,1)}, u32[]{:S(2)}, u32[]{:S(2)}) collective-permute-start(bf16[8,144,512]{2,1,0:T(8,128)(2,1)} %get-tuple-element.98), channel_id=1, source_target_pairs={{0,1},{1,0},{2,3},{3,2},{4,5},{5,4},{6,7},{7,6},{8,9},{9,8},{10,11... | collective-permute-start | bytes 3538952 | tf_op jit(solution)/shard_map/ppermute | solution.py:676
  135.5 16.4 %collective-permute-start.26 = (bf16[4,144,512]{2,1,0:T(8,128)(2,1)}, bf16[4,144,512]{2,1,0:T(8,128)(2,1)S(1)}, u32[]{:S(2)}, u32[]{:S(2)}) collective-permute-start(bf16[4,144,512]{2,1,0:T(8,128)(2,1)} %add.176), channel_id=1, source_target_pairs={{0,8},{8,0},{16,24},{24,16},{1,9},{9,1},{17,25},{25,17},{2,10},{10... | collective-permute-start | bytes 1769480 | tf_op jit(solution)/shard_map/ppermute | solution.py:678
  137.0 15.5 %collective-permute-start.27 = (bf16[4,144,512]{2,1,0:T(8,128)(2,1)}, bf16[4,144,512]{2,1,0:T(8,128)(2,1)}, u32[]{:S(2)}, u32[]{:S(2)}) collective-permute-start(bf16[4,144,512]{2,1,0:T(8,128)(2,1)} %add.177), channel_id=1, source_target_pairs={{0,16},{8,24},{16,0},{24,8},{1,17},{9,25},{17,1},{25,9},{2,18},{10... | collective-permute-start | bytes 1769480 | tf_op jit(solution)/shard_map/ppermute | solution.py:679
  154.1 9.4 %collective-permute-start.31 = (bf16[2,144,512]{2,1,0:T(8,128)(2,1)S(1)}, bf16[2,144,512]{2,1,0:T(8,128)(2,1)S(1)}, u32[]{:S(2)}, u32[]{:S(2)}) collective-permute-start(bf16[2,144,512]{2,1,0:T(8,128)(2,1)S(1)} %get-tuple-element.131), channel_id=1, source_target_pairs={{0,8},{8,0},{16,24},{24,16},{1,9},{9,1},{17,25},{25,17},{2,10},{10... | collective-permute-start | bytes 884744 | tf_op jit(solution)/shard_map/ppermute | solution.py:684
  154.8 9.0 %collective-permute-start.30 = (bf16[2,144,512]{2,1,0:T(8,128)(2,1)S(1)}, bf16[2,144,512]{2,1,0:T(8,128)(2,1)S(1)}, u32[]{:S(2)}, u32[]{:S(2)}) collective-permute-start(bf16[2,144,512]{2,1,0:T(8,128)(2,1)S(1)} %get-tuple-element.132), channel_id=1, source_target_pairs={{0,16},{8,24},{16,0},{24,8},{1,17},{9,25},{17,1},{25,9},{2,18},{10... | collective-permute-start | bytes 884744 | tf_op jit(solution)/shard_map/ppermute | solution.py:683
  163.7 32.1 %all-to-all-start = ((bf16[4,4,144,512]{3,2,1,0:T(8,128)(2,1)}), bf16[4,4,144,512]{3,2,1,0:T(8,128)(2,1)}, u32[]{:S(2)}, u32[]{:S(2)}) async-start(bf16[4,4,144,512]{3,2,1,0:T(8,128)(2,1)} %bitcast.22), calls=%async_computation | async-start | bytes 4718592 | tf_op jit(solution)/shard_map/all_to_all | solution.py:687
  170.7 21.0 %collective-permute-start.34 = (bf16[144,512]{1,0:T(8,128)(2,1)}, bf16[144,512]{1,0:T(8,128)(2,1)S(1)}, u32[]{:S(2)}, u32[]{:S(2)}) collective-permute-start(bf16[144,512]{1,0:T(8,128)(2,1)} %get-tuple-element.122), channel_id=1, source_target_pairs={{0,6},{1,7},{2,0},{3,1},{4,2},{5,3},{6,4},{7,5},{8,14},{9,15},{10,... | collective-permute-start | bytes 442376 | tf_op jit(solution)/shard_map/ppermute | solution.py:669
  173.9 17.7 %collective-permute-start.33 = (bf16[144,512]{1,0:T(8,128)(2,1)}, bf16[144,512]{1,0:T(8,128)(2,1)S(1)}, u32[]{:S(2)}, u32[]{:S(2)}) collective-permute-start(bf16[144,512]{1,0:T(8,128)(2,1)} %get-tuple-element.123), channel_id=1, source_target_pairs={{0,4},{1,5},{2,6},{3,7},{4,0},{5,1},{6,2},{7,3},{8,12},{9,13},{10,... | collective-permute-start | bytes 442376 | tf_op jit(solution)/shard_map/ppermute | solution.py:669
  175.0 16.6 %collective-permute-start.32 = (bf16[144,512]{1,0:T(8,128)(2,1)S(1)}, bf16[144,512]{1,0:T(8,128)(2,1)S(1)}, u32[]{:S(2)}, u32[]{:S(2)}) collective-permute-start(bf16[144,512]{1,0:T(8,128)(2,1)S(1)} %get-tuple-element.130), channel_id=1, source_target_pairs={{0,2},{1,3},{2,4},{3,5},{4,6},{5,7},{6,0},{7,1},{8,10},{9,11},{10,... | collective-permute-start | bytes 442376 | tf_op jit(solution)/shard_map/ppermute | solution.py:669
  200.7 10.1 %collective-permute-start.36 = (bf16[144,512]{1,0:T(8,128)(2,1)S(1)}, bf16[144,512]{1,0:T(8,128)(2,1)S(1)}, u32[]{:S(2)}, u32[]{:S(2)}) collective-permute-start(bf16[144,512]{1,0:T(8,128)(2,1)S(1)} %get-tuple-element.127), channel_id=1, source_target_pairs={{0,4},{1,5},{2,6},{3,7},{4,0},{5,1},{6,2},{7,3},{8,12},{9,13},{10,... | collective-permute-start | bytes 442376 | tf_op jit(solution)/shard_map/ppermute | solution.py:669
  201.6 9.2 %collective-permute-start.37 = (bf16[144,512]{1,0:T(8,128)(2,1)S(1)}, bf16[144,512]{1,0:T(8,128)(2,1)S(1)}, u32[]{:S(2)}, u32[]{:S(2)}) collective-permute-start(bf16[144,512]{1,0:T(8,128)(2,1)S(1)} %get-tuple-element.128), channel_id=1, source_target_pairs={{0,6},{1,7},{2,0},{3,1},{4,2},{5,3},{6,4},{7,5},{8,14},{9,15},{10,... | collective-permute-start | bytes 442376 | tf_op jit(solution)/shard_map/ppermute | solution.py:669
  (30 other events, 146.6 us)

commit v4 on v3

--- a/solution.py
+++ b/solution.py
@@ -87,62 +87,33 @@
     return jnp.concatenate([mask] * (width // 128), axis=1)
 
 
-def prep_kernel(len_ref, place_ref, tokens_ref, present_ref, stacked_ref, masked_ref, keep_ref, even, odd, *, tile, wins):
-    step = pl.program_id(0)
-    rows, width = tokens_ref.shape
-    start = pl.multiple_of(step * tile, tile)
-
-    @pl.when(step == 0)
-    def _():
-        edge = jnp.zeros((REACH, width), bf16)
-        even[:REACH] = edge
-        even[rows + REACH :] = edge
-        odd[:REACH] = edge
-        odd[rows : rows + REACH] = edge
-        odd[rows + REACH :] = edge
-        for r in range(0, rows, 128):
-            line = jnp.broadcast_to((present_ref[r // 128 : r // 128 + 1] > 0).astype(f32), (128, 128))
-            kept = line.T
-            keep_ref[r : r + 128] = kept
-            block = tokens_ref[r : r + 128] * wide(kept.astype(bf16), width)
-            even[REACH + r : REACH + r + 128] = block
-            odd[REACH - STEP + r : REACH - STEP + r + 128] = block
-
-    masked_ref[...] = even[pl.ds(start + REACH, tile)].T
-    position = lax.broadcasted_iota(jnp.int32, (tile, 128), 0) + start
-    first, last = window_bounds(len_ref, position, wins, rows)
-    per = TAPS * width // 128 // QUARTERS
-    for tap in range(TAPS):
-        other = position + (tap - TAPS // 2) * STEP
-        valid = ((other >= first) & (other < last)).astype(bf16)
-        offset = pl.multiple_of(start + tap // 2 * 2 * STEP, 2 * STEP)
-        block = (odd if tap % 2 else even)[pl.ds(offset, tile)] * wide(valid, width)
-        for lane in range(0, width, 128):
-            chunk = (tap * width + lane) // 128
-            seat = ((chunk // per) ^ place_ref[2]) * per + chunk % per
-            stacked_ref[:, pl.ds(pl.multiple_of(seat * 128, 128), 128)] = block[:, lane : lane + 128]
-
-
-def prep(lengths, place, tokens, present):
+def prep_kernel(tokens_ref, present_ref, masked_ref, across_ref, keep_ref):
+    tile, width = tokens_ref.shape
+    for r in range(0, tile, 128):
+        line = jnp.broadcast_to((present_ref[0, r // 128 : r // 128 + 1] > 0).astype(f32), (128, 128))
+        kept = line.T
+        keep_ref[r : r + 128] = kept
+        masked_ref[r : r + 128] = tokens_ref[r : r + 128] * wide(kept.astype(bf16), width)
+    across_ref[...] = masked_ref[...].T
+
+
+def prep(tokens, present):
     rows, width = tokens.shape
-    tile = 256
+    tile = 512
     return pl.pallas_call(
-        functools.partial(prep_kernel, tile=tile, wins=lengths.shape[1]),
+        prep_kernel,
         grid=(rows // tile,),
-        in_specs=[SMEM, SMEM, whole((rows, width)), whole((rows // 128, 128))],
-        out_specs=[
-            rows_of(tile, TAPS * width), pl.BlockSpec((width, tile), lambda i: (0, i)), pl.BlockSpec((rows, 128), lambda i: (0, 0))
-        ],
+        in_specs=[rows_of(tile, width), pl.BlockSpec((1, tile // 128, 128), lambda i: (i, 0, 0))],
+        out_specs=[rows_of(tile, width), pl.BlockSpec((width, tile), lambda i: (0, i)), rows_of(tile, 128)],
         out_shape=[
-            jax.ShapeDtypeStruct((rows, TAPS * width), bf16),
+            jax.ShapeDtypeStruct((rows, width), bf16),
             jax.ShapeDtypeStruct((width, rows), bf16),
             jax.ShapeDtypeStruct((rows, 128), f32),
         ],
-        scratch_shapes=[pltpu.VMEM((rows + 2 * REACH, width), bf16), pltpu.VMEM((rows + 2 * REACH, width), bf16)],
         compiler_params=vmem(63),
         cost_estimate=cost(0, 24 * rows * width),
         name="prep",
-    )(lengths, place, tokens, present.reshape(rows // 128, 128))
+    )(tokens, present.reshape(rows // tile, tile // 128, 128))
 
 
 def conv_sites(pieces, first, place, fast, body):
@@ -168,48 +139,77 @@
     return copies
 
 
-def conv_kernel(place_ref, *refs, fast, body):
-    *pieces, stacked_ref, conv_ref, near_ref, store, sems, out_sem = refs
+def conv_kernel(len_ref, place_ref, *refs, count, fast, body, wins):
+    pieces = refs[:count]
+    masked_ref, conv_ref, far_ref, near_ref, store, stack, even, odd, sems, out_sem = refs[count:]
+    step = pl.program_id(0)
+    rows, width = masked_ref.shape
+    tile = conv_ref.shape[0]
     depth = store.shape[0] // (QUARTERS - 1)
     back = pltpu.make_async_copy(store, near_ref, out_sem)
-
-    @pl.when(pl.program_id(0) == 0)
-    def _():
-        sites = conv_sites(pieces, 0, tuple(place_ref[i] for i in range(3)), fast, body)
-        copies = conv_copies(sites, lambda kind: kind * depth, store, sems)
+    sites = conv_sites(pieces, 0, tuple(place_ref[i] for i in range(3)), fast, body)
+    copies = conv_copies(sites, lambda kind: kind * depth, store, sems)
+
+    @pl.when(step == 0)
+    def _():
         for copy in copies:
             copy.start()
+        lay_shifted(masked_ref, even, odd, 256)
+
+    start = pl.multiple_of(step * tile, tile)
+    position = lax.broadcasted_iota(jnp.int32, (tile, 128), 0) + start
+    first, last = window_bounds(len_ref, position, wins, rows)
+    per = depth // 128
+    for tap in range(TAPS):
+        other = position + (tap - TAPS // 2) * STEP
+        valid = ((other >= first) & (other < last)).astype(bf16)
+        offset = pl.multiple_of(start + tap // 2 * 2 * STEP, 2 * STEP)
+        block = (odd if tap % 2 else even)[pl.ds(offset, tile)] * wide(valid, width)
+        for lane in range(0, width, 128):
+            chunk = (tap * width + lane) // 128
+            seat = ((chunk // per) ^ place_ref[2]) * per + chunk % per
+            stack[:, pl.ds(pl.multiple_of(seat * 128, 128), 128)] = block[:, lane : lane + 128]
+
+    @pl.when(step == 0)
+    def _():
         for copy in copies:
             copy.wait()
         back.start()
 
-    conv_ref[...] = dot(stacked_ref[...], store[...])
-
-    @pl.when(pl.program_id(0) == pl.num_programs(0) - 1)
+    far_ref[...] = stack[:, store.shape[0] :]
+    conv_ref[...] = dot(stack[:, : store.shape[0]], store[...])
+
+    @pl.when(step == pl.num_programs(0) - 1)
     def _():
         back.wait()
 
 
-def conv_forward(place, pieces, stacked, fast, body):
-    rows, depth = stacked.shape
-    width = pieces[0].shape[2]
-    depth = depth // QUARTERS * (QUARTERS - 1)
+def conv_forward(lengths, place, pieces, masked, fast, body):
+    rows, width = masked.shape
+    depth = TAPS * width // QUARTERS
     tile = 512
     return pl.pallas_call(
-        functools.partial(conv_kernel, fast=fast, body=body),
+        functools.partial(conv_kernel, count=len(pieces), fast=fast, body=body, wins=lengths.shape[1]),
         grid=(rows // tile,),
-        in_specs=[SMEM] + [ANY] * len(pieces) + [rows_of(tile, depth)],
-        out_specs=[rows_of(tile, width), ANY],
-        out_shape=[jax.ShapeDtypeStruct((rows, width), f32), jax.ShapeDtypeStruct((depth, width), bf16)],
+        in_specs=[SMEM, SMEM] + [ANY] * len(pieces) + [whole((rows, width))],
+        out_specs=[rows_of(tile, width), rows_of(tile, depth), ANY],
+        out_shape=[
+            jax.ShapeDtypeStruct((rows, width), f32),
+            jax.ShapeDtypeStruct((rows, depth), bf16),
+            jax.ShapeDtypeStruct(((QUARTERS - 1) * depth, width), bf16),
+        ],
         scratch_shapes=[
-            pltpu.VMEM((depth, width), bf16),
+            pltpu.VMEM(((QUARTERS - 1) * depth, width), bf16),
+            pltpu.VMEM((tile, QUARTERS * depth), bf16),
+            pltpu.VMEM((rows + 2 * REACH, width), bf16),
+            pltpu.VMEM((rows + 2 * REACH, width), bf16),
             pltpu.SemaphoreType.DMA((sum(piece.shape[0] for piece in pieces),)),
             pltpu.SemaphoreType.DMA,
         ],
         compiler_params=vmem(63),
-        cost_estimate=cost(depth * rows * width, 24 * rows * width),
+        cost_estimate=cost(3 * depth * rows * width, 24 * rows * width),
         name="conv_forward",
-    )(place, *pieces, stacked)
+    )(lengths, place, *pieces, masked)
 
 
 def ff_copies(pieces, place, fast, store, sems):
@@ -413,10 +413,10 @@
     tile = 512
     tiles, cols = rows // tile, total // width
     share = cols * inner_rows + extra + outer_rows
-    depth = stacked.shape[1] // QUARTERS
+    depth = stacked.shape[1]
     seats = (8, 4, 4) * 2 if fast else (1, 1)
     tall = pl.BlockSpec((tile, width), lambda i: (jnp.minimum(i, tiles - 1), 0))
-    last = pl.BlockSpec((tile, depth), lambda i: (jnp.minimum(i, tiles - 1), QUARTERS - 1))
+    last = pl.BlockSpec((tile, depth), lambda i: (jnp.minimum(i, tiles - 1), 0))
     return pl.pallas_call(
         functools.partial(
             feed_kernel, far=len(far), count=len(pieces), outs=len(seats), tiles=tiles, chunk=512, inner_rows=inner_rows,
@@ -617,14 +617,12 @@
         own_line = ((line < 6) & (lane // n == seat)) | ((line == 6 + dp) & (lane // few == fsdp))
         lines = jnp.where(own_line, lines, 0)
         ff_own = jnp.concatenate([w_in[:, j * width : (j + 1) * width] for j in range(cols)] + [lines, w_out], axis=0)
-        column, ff_own, late_tokens = bar((column, ff_own, tokens))
+        masked, masked_across, keep = prep(tokens, present)
+        column, ff_own, masked, masked_across, keep = bar((column, ff_own, masked, masked_across, keep))
         beside_x = lax.ppermute(column, "dp", across[1])
         beside_y = lax.ppermute(column, "dp", across[2])
         ff_rest = from_column(ff_own)
-        stacked, masked, keep = prep(lengths, place, late_tokens, present)
-        column, beside_x, beside_y, ff_rest, stacked, masked, keep = bar(
-            (column, beside_x, beside_y, ff_rest, stacked, masked, keep)
-        )
+        column, beside_x, beside_y, ff_rest = bar((column, beside_x, beside_y, ff_rest))
         ff_column = jnp.stack(ff_rest)
         near = (column, beside_x, beside_y)
         near = near + tuple(lax.ppermute(piece, "fsdp", swap) for piece in near)
@@ -648,9 +646,9 @@
         ff = [full_in[:, j * width : (j + 1) * width].reshape(2, inner_rows, width) for j in range(cols)]
         ff.append(jnp.stack([lines, jnp.zeros_like(lines)]))
         ff = (jnp.concatenate(ff + [full_out.reshape(2, outer_rows, width)], axis=1),)
-        stacked, masked, keep = prep(lengths, place, tokens, present)
-
-    partial, w_near = conv_forward(place, near, stacked, fast, body)
+        masked, masked_across, keep = prep(tokens, present)
+
+    partial, stacked, w_near = conv_forward(lengths, place, near, masked, fast, body)
     if fast:
         far, ff, partial = bar((far, ff, partial))
         ff = ff + (
@@ -677,7 +675,7 @@
         a_far, b_far, d_conv = bar((ff_far_a + came_a, ff_far_b + came_b, d_conv))
         a_came = lax.ppermute(a_far, "dp", across[1])
         b_came = lax.ppermute(b_far, "dp", across[2])
-        conv_keep, conv_send = conv_grad(lengths, place, masked, d_conv, blocks, body)
+        conv_keep, conv_send = conv_grad(lengths, place, masked_across, d_conv, blocks, body)
         a_came, b_came, came, conv_keep, conv_send, d_conv = bar((a_came, b_came, came, conv_keep, conv_send, d_conv))
         conv_came = lax.ppermute(conv_send, "fsdp", swap)
         a_last = lax.ppermute(rounded(ff_near[2:4], came[2:4], a_came[2:]), "dp", across[2])
@@ -701,7 +699,7 @@
         vector_grads = list(own)
         vector_grads.append(lax.dynamic_slice(ff_share[top + 6], (fsdp * few,), (few,)))
     else:
-        conv_pair = conv_grad(lengths, place, masked, d_conv, blocks, body)
+        conv_pair = conv_grad(lengths, place, masked_across, d_conv, blocks, body)
         d_tokens = token_grad(lengths, place, w_near, w_far, d_conv, d_hidden, keep)
         ff_share = jnp.concatenate(ff_grads, axis=0)
         scatter = functools.partial(lax.psum_scatter, axis_name=AXES, scatter_dimension=0, tiled=True)

time: 214 us -> 212 us (level)
  waiting for transfers between devices: 32.4 us -> 43.2 us
  local copies, waits for them, and re-layouts: 14.7 us -> 11.3 us
  Pallas kernels: 107 us -> 104 us
  starting transfers between devices: 40.3 us -> 37.3 us
  other arithmetic: 17.1 us -> 14.3 us
    ppermute x6, waiting for transfers between devices: 7.02 us -> 14.1 us  [from_column(): return [shard] + [lax.ppermute(shard, 'fsdp', along[k]) for k in (1, 2, 3)]]
    pallas_call x2, Pallas kernels: 26.3 us -> 22.8 us  [the longest x1 18.2 us: conv_forward(): pl.pallas_call(functools.partial(conv_kernel, count=len(pieces), fast=fas...]
    unnamed x34 -> x40, local copies, waits for them, and re-layouts: 5.45 us -> 4.98 us
  transfers between devices with their start and end apart: 39 -> 39, of which waited for: 15 -> 17; matrix products, arithmetic and copies ran while one was open for 11% -> 9% of each run, Pallas kernels for 26% -> 25%
where the time goes in v4:
time: 212 us; the launch traced here: 211 us
  Pallas kernels  104 us (49%)
  waiting for transfers between devices  43.2 us (20%)
  starting transfers between devices  37.3 us (18%)
  other arithmetic  14.3 us (7%)
  local copies, waits for them, and re-layouts  11.3 us (5%)
    pallas_call x1, Pallas kernels, feed(): pl.pallas_call(functools.partial(feed_kernel, far=len(far), count=len(pie...  51.7 us
    pallas_call x1, Pallas kernels, conv_forward(): pl.pallas_call(functools.partial(conv_kernel, count=len(pieces), fast=fas...  18.2 us
    pallas_call x1, Pallas kernels, token_grad(): pl.pallas_call(functools.partial(token_grad_kernel, wins=lengths.shape[1]...  16.2 us
    ppermute x6, waiting for transfers between devices, from_column(): return [shard] + [lax.ppermute(shard, 'fsdp', along[k]) for k in (1, 2, 3)]  14.1 us
    pallas_call x1, Pallas kernels, conv_grad(): pl.pallas_call(functools.partial(conv_grad_kernel, wins=lengths.shape[1],...  13.3 us
    ppermute x6, starting transfers between devices, line_swap(): lax.ppermute(line[k], 'fsdp', along[k])  9.76 us
    ppermute x6, starting transfers between devices, from_column(): return [shard] + [lax.ppermute(shard, 'fsdp', along[k]) for k in (1, 2, 3)]  8.31 us
    add x4, other arithmetic, added(): return sum((term.astype(f32) for term in terms))  6.05 us
  transfers between devices with their start and end apart: 39, of which 17 were waited for; matrix products, arithmetic and copies ran while one was open for 9% of the time, Pallas kernels for 25%

profile of v4, /device:TPU:0, one launch (start us, length us, event | category | flops | bytes accessed | tf_op | source)
XLA Modules:
  0.0 211.0 jit_solution(9800094900144008202)
XLA Ops:
  0.7 3.1 %collective-permute-start = (bf16[144,512]{1,0:T(8,128)(2,1)}, bf16[144,512]{1,0:T(8,128)(2,1)S(1)}, u32[]{:S(2)}, u32[]{:S(2)}) collective-permute-start(bf16[144,512]{1,0:T(8,128)(2,1)} %param.17), channel_id=1, source_target_pairs={{0,2},{1,3},{2,4},{3,5},{4,6},{5,7},{6,0},{7,1},{8,10},{9,11},{10,... | collective-permute-start | bytes 442376 | tf_op jit(solution)/shard_map/ppermute | solution.py:605
  3.7 2.1 collective-permute-start.2
  11.4 4.6 %prep.1 = (bf16[2048,512]{1,0:T(8,128)(2,1)}, bf16[512,2048]{1,0:T(8,128)(2,1)}, f32[2048,128]{1,0:T(8,128)}) custom-call(bf16[2048,512]{1,0:T(8,128)(2,1)} %refs_16_.1, s32[4,4,128]{2,1,0:T(4,128)} %bitcast.60), custom_call_target="tpu_custom_call" | custom-call | bytes 786432 | tf_op jit(solution)/shard_map/prep/pallas_call | solution.py:103
  16.0 3.3 %collective-permute-done.1 = bf16[144,512]{1,0:T(8,128)(2,1)S(1)} collective-permute-done((bf16[144,512]{1,0:T(8,128)(2,1)}, bf16[144,512]{1,0:T(8,128)(2,1)S(1)}, u32[]{:S(2)}, u32[]{:S(2)}) %collective-permute-start.1) | collective-permute-done | bytes 147488 | tf_op jit(solution)/shard_map/ppermute | solution.py:605
  24.7 4.3 %collective-permute-done.7 = bf16[144,512]{1,0:T(8,128)(2,1)S(1)} collective-permute-done((bf16[144,512]{1,0:T(8,128)(2,1)S(1)}, bf16[144,512]{1,0:T(8,128)(2,1)S(1)}, u32[]{:S(2)}, u32[]{:S(2)}) %collective-permute-start.7) | collective-permute-done | bytes 147488 | tf_op jit(solution)/shard_map/ppermute | solution.py:605
  28.9 6.5 %collective-permute-done.6 = bf16[144,512]{1,0:T(8,128)(2,1)S(1)} collective-permute-done((bf16[144,512]{1,0:T(8,128)(2,1)S(1)}, bf16[144,512]{1,0:T(8,128)(2,1)S(1)}, u32[]{:S(2)}, u32[]{:S(2)}) %collective-permute-start.6) | collective-permute-done | bytes 147488 | tf_op jit(solution)/shard_map/ppermute | solution.py:605
  43.3 18.2 %conv_forward.1 = (f32[2048,512]{1,0:T(8,128)}, bf16[2048,1152]{1,0:T(8,128)(2,1)}, bf16[3456,512]{1,0:T(8,128)(2,1)}) custom-call(s32[1,4]{1,0:T(1,128)} %len_ref.5, s32[3]{0:T(128)} %pad_add_fusion.place_ref, bf16[4,144,512]{2,1,0:T(8,128)(2,1)} %copy-done.1, bf16[4,144,512]{2,1,0:T(8,128)(2,1)} %copy-done.4, bf16[4,144,512]{2,1,0:T(8,128)(2,1)} %copy-done.3, ...), custom_call_target="tpu_custom_call" | custom-call | flops 113246208 | bytes 786432 | tf_op jit(solution)/shard_map/conv_forward/pallas_call | solution.py:191
  65.9 5.3 %collective-permute-done.18.refs_8_ = bf16[2,144,512]{2,1,0:T(8,128)(2,1)S(1)} collective-permute-done((bf16[2,144,512]{2,1,0:T(8,128)(2,1)S(1)}, bf16[2,144,512]{2,1,0:T(8,128)(2,1)S(1)}, u32[]{:S(2)}, u32[]{:S(2)}) %collective-permute-start.18) | collective-permute-done | bytes 294944 | tf_op jit(solution)/shard_map/ppermute | solution.py:656
  73.5 1.8 collective-permute-done.23.refs_13_
  76.7 51.7 %feed.1 = (bf16[2048,512]{1,0:T(8,128)(2,1)}, f32[2048,512]{1,0:T(8,128)}, bf16[2048,512]{1,0:T(8,128)(2,1)}, f32[16,512]{1,0:T(8,128)}, bf16[1152,512]{1,0:T(8,...) custom-call(s32[3]{0:T(128)} %pad_add_fusion.place_ref, ...), custom_call_target="tpu_custom_call" | custom-call | flops 402653184 | bytes 1310720 | tf_op jit(solution)/shard_map/feed/pallas_call | solution.py:420
  130.6 2.0 add.176
  135.1 13.3 %conv_grad.1 = (bf16[16,144,512]{2,1,0:T(8,128)(2,1)}, bf16[16,144,512]{2,1,0:T(8,128)(2,1)}) custom-call(s32[1,4]{1,0:T(1,128)} %len_ref.5, s32[3]{0:T(128)} %pad_add_fusion.place_ref, bf16[512,2048]{1,0:T(8,128)(2,1)} %get-tuple-element.99.masked_ref, bf16[2048,512]{1,0:T(8,128)(2,1)} %get-tuple-element.110.d_conv_ref), custom_call_target="tpu_custom_call" | custom-call | flops 150994944 | bytes 393216 | tf_op jit(solution)/shard_map/conv_grad/pallas_call | solution.py:507
  154.9 2.2 %add.178 = bf16[16,144,512]{2,1,0:T(8,128)(2,1)} add(bf16[16,144,512]{2,1,0:T(8,128)(2,1)S(1)} %copy-done.2, bf16[16,144,512]{2,1,0:T(8,128)(2,1)S(1)} %collective-permute-done.29) | non-fusion elementwise | flops 1179648 | bytes 7077888 | tf_op jit(solution)/shard_map/add | solution.py:683
  157.1 4.1 %collective-permute-done.31 = bf16[2,144,512]{2,1,0:T(8,128)(2,1)S(1)} collective-permute-done((bf16[2,144,512]{2,1,0:T(8,128)(2,1)S(1)}, bf16[2,144,512]{2,1,0:T(8,128)(2,1)S(1)}, u32[]{:S(2)}, u32[]{:S(2)}) %collective-permute-start.31) | collective-permute-done | bytes 294944 | tf_op jit(solution)/shard_map/ppermute | solution.py:682
  161.8 4.6 %all-to-all-start = ((bf16[4,4,144,512]{3,2,1,0:T(8,128)(2,1)}), bf16[4,4,144,512]{3,2,1,0:T(8,128)(2,1)}, u32[]{:S(2)}, u32[]{:S(2)}) async-start(bf16[4,4,144,512]{3,2,1,0:T(8,128)(2,1)} %bitcast.22), calls=%async_computation | async-start | bytes 4718592 | tf_op jit(solution)/shard_map/all_to_all | solution.py:685
  166.5 2.3 %fusion.5 = (bf16[144,512]{1,0:T(8,128)(2,1)}, bf16[144,512]{1,0:T(8,128)(2,1)}, bf16[144,512]{1,0:T(8,128)(2,1)S(1)}, bf16[144,512]{1,0:T(8,128)(2,1)S(1)}) fusion(bf16[2,144,512]{2,1,0:T(8,128)(2,1)S(1)} %collective-permute-done.31, bf16[4,144,512]{2,1,0:T(8,128)(2,1)} %collective-permute-done.27, bf16[8,144,512]{2,1,0:T(8,128)(2,1)} %collective-permute-done.28, ...), kind=kLoop, calls=%fused_computation.19 | loop fusion | flops 2359296 | bytes 2949120 | tf_op jit(solution)/shard_map/add | solution.py:664
  171.1 2.0 collective-permute-start.32
  173.2 16.2 %token_grad.1 = f32[2048,512]{1,0:T(8,128)} custom-call(s32[1,4]{1,0:T(1,128)} %len_ref.5, s32[3]{0:T(128)} %pad_add_fusion.place_ref, bf16[3456,512]{1,0:T(8,128)(2,1)} %get-tuple-element.89.near_ref, bf16[1152,512]{1,0:T(8,128)(2,1)} %get-tuple-element.90.far_ref, bf16[2048,512]{1,0:T(8,128)(2,1)} %get-tuple-element.110.d_conv_ref, ...), custom_call_target="tpu_custom_call" | custom-call | flops 150994944 | bytes 393216 | tf_op jit(solution)/shard_map/token_grad/pallas_call | solution.py:563
  189.4 4.7 %all-to-all-done = bf16[4,4,144,512]{3,2,1,0:T(8,128)(2,1)} async-done(((bf16[4,4,144,512]{3,2,1,0:T(8,128)(2,1)}), bf16[4,4,144,512]{3,2,1,0:T(8,128)(2,1)}, u32[]{:S(2)}, u32[]{:S(2)}) %all-to-all-start) | async-done | bytes 2359328 | tf_op jit(solution)/shard_map/all_to_all | solution.py:685
  194.2 1.7 fusion.7
  196.4 2.0 collective-permute-start.36
  198.4 2.8 %collective-permute-start.37 = (bf16[144,512]{1,0:T(8,128)(2,1)S(1)}, bf16[144,512]{1,0:T(8,128)(2,1)S(1)}, u32[]{:S(2)}, u32[]{:S(2)}) collective-permute-start(bf16[144,512]{1,0:T(8,128)(2,1)S(1)} %get-tuple-element.128), channel_id=1, source_target_pairs={{0,6},{1,7},{2,0},{3,1},{4,2},{5,3},{6,4},{7,5},{8,14},{9,15},{10,... | collective-permute-start | bytes 442376 | tf_op jit(solution)/shard_map/ppermute | solution.py:667
  204.6 4.4 %collective-permute-done.36 = bf16[144,512]{1,0:T(8,128)(2,1)S(1)} collective-permute-done((bf16[144,512]{1,0:T(8,128)(2,1)S(1)}, bf16[144,512]{1,0:T(8,128)(2,1)S(1)}, u32[]{:S(2)}, u32[]{:S(2)}) %collective-permute-start.36) | collective-permute-done | bytes 147488 | tf_op jit(solution)/shard_map/ppermute | solution.py:667
  209.0 2.0 fusion.1
  (133 shorter events, 44.8 us)
Async XLA Ops:
  0.7 15.4 %collective-permute-start = (bf16[144,512]{1,0:T(8,128)(2,1)}, bf16[144,512]{1,0:T(8,128)(2,1)S(1)}, u32[]{:S(2)}, u32[]{:S(2)}) collective-permute-start(bf16[144,512]{1,0:T(8,128)(2,1)} %param.17), channel_id=1, source_target_pairs={{0,2},{1,3},{2,4},{3,5},{4,6},{5,7},{6,0},{7,1},{8,10},{9,11},{10,... | collective-permute-start | bytes 442376 | tf_op jit(solution)/shard_map/ppermute | solution.py:605
  3.7 12.3 %collective-permute-start.2 = (bf16[144,512]{1,0:T(8,128)(2,1)}, bf16[144,512]{1,0:T(8,128)(2,1)S(1)}, u32[]{:S(2)}, u32[]{:S(2)}) collective-permute-start(bf16[144,512]{1,0:T(8,128)(2,1)} %param.17), channel_id=1, source_target_pairs={{0,6},{1,7},{2,0},{3,1},{4,2},{5,3},{6,4},{7,5},{8,14},{9,15},{10,... | collective-permute-start | bytes 442376 | tf_op jit(solution)/shard_map/ppermute | solution.py:605
  5.8 13.5 %collective-permute-start.1 = (bf16[144,512]{1,0:T(8,128)(2,1)}, bf16[144,512]{1,0:T(8,128)(2,1)S(1)}, u32[]{:S(2)}, u32[]{:S(2)}) collective-permute-start(bf16[144,512]{1,0:T(8,128)(2,1)} %param.17), channel_id=1, source_target_pairs={{0,4},{1,5},{2,6},{3,7},{4,0},{5,1},{6,2},{7,3},{8,12},{9,13},{10,... | collective-permute-start | bytes 442376 | tf_op jit(solution)/shard_map/ppermute | solution.py:605
  19.4 16.1 %collective-permute-start.4 = (bf16[4,144,512]{2,1,0:T(8,128)(2,1)S(1)}, bf16[4,144,512]{2,1,0:T(8,128)(2,1)S(1)}, u32[]{:S(2)}, u32[]{:S(2)}) collective-permute-start(bf16[4,144,512]{2,1,0:T(8,128)(2,1)S(1)} %pad_maximum_fusion.refs_0_), channel_id=1, source_target_pairs={{0,16},{8,24},{16,0},{24,8},{1,17},{9,25},{17,1},{25,9},{2,18},{10... | collective-permute-start | bytes 1769480 | tf_op jit(solution)/shard_map/ppermute | solution.py:623
  21.0 15.0 %collective-permute-start.3 = (bf16[4,144,512]{2,1,0:T(8,128)(2,1)S(1)}, bf16[4,144,512]{2,1,0:T(8,128)(2,1)S(1)}, u32[]{:S(2)}, u32[]{:S(2)}) collective-permute-start(bf16[4,144,512]{2,1,0:T(8,128)(2,1)S(1)} %pad_maximum_fusion.refs_0_), channel_id=1, source_target_pairs={{0,8},{8,0},{16,24},{24,16},{1,9},{9,1},{17,25},{25,17},{2,10},{10... | collective-permute-start | bytes 1769480 | tf_op jit(solution)/shard_map/ppermute | solution.py:622
  24.1 11.4 %collective-permute-start.6 = (bf16[144,512]{1,0:T(8,128)(2,1)S(1)}, bf16[144,512]{1,0:T(8,128)(2,1)S(1)}, u32[]{:S(2)}, u32[]{:S(2)}) collective-permute-start(bf16[144,512]{1,0:T(8,128)(2,1)S(1)} %constant_dynamic-update-slice_fusion), channel_id=1, source_target_pairs={{0,4},{1,5},{2,6},{3,7},{4,0},{5,1},{6,2},{7,3},{8,12},{9,13},{10,... | collective-permute-start | bytes 442376 | tf_op jit(solution)/shard_map/ppermute | solution.py:605
  24.1 11.4 %collective-permute-start.5 = (bf16[144,512]{1,0:T(8,128)(2,1)S(1)}, bf16[144,512]{1,0:T(8,128)(2,1)S(1)}, u32[]{:S(2)}, u32[]{:S(2)}) collective-permute-start(bf16[144,512]{1,0:T(8,128)(2,1)S(1)} %constant_dynamic-update-slice_fusion), channel_id=1, source_target_pairs={{0,2},{1,3},{2,4},{3,5},{4,6},{5,7},{6,0},{7,1},{8,10},{9,11},{10,... | collective-permute-start | bytes 442376 | tf_op jit(solution)/shard_map/ppermute | solution.py:605
  36.6 25.0 %collective-permute-start.11 = (bf16[4,144,512]{2,1,0:T(8,128)(2,1)S(1)}, bf16[4,144,512]{2,1,0:T(8,128)(2,1)}, u32[]{:S(2)}, u32[]{:S(2)}) collective-permute-start(bf16[4,144,512]{2,1,0:T(8,128)(2,1)S(1)} %pad_maximum_fusion.1.refs_4_), channel_id=1, source_target_pairs={{0,16},{8,24},{16,0},{24,8},{1,17},{9,25},{17,1},{25,9},{2,18},{10... | collective-permute-start | bytes 1769480 | tf_op jit(solution)/shard_map/ppermute | solution.py:633
  37.1 24.4 %collective-permute-start.10 = (bf16[4,144,512]{2,1,0:T(8,128)(2,1)S(1)}, bf16[4,144,512]{2,1,0:T(8,128)(2,1)}, u32[]{:S(2)}, u32[]{:S(2)}) collective-permute-start(bf16[4,144,512]{2,1,0:T(8,128)(2,1)S(1)} %pad_maximum_fusion.1.refs_4_), channel_id=1, source_target_pairs={{0,8},{8,0},{16,24},{24,16},{1,9},{9,1},{17,25},{25,17},{2,10},{10... | collective-permute-start | bytes 1769480 | tf_op jit(solution)/shard_map/ppermute | solution.py:633
  39.4 22.1 %collective-permute-start.9 = (bf16[2,144,512]{2,1,0:T(8,128)(2,1)}, bf16[2,144,512]{2,1,0:T(8,128)(2,1)}, u32[]{:S(2)}, u32[]{:S(2)}) collective-permute-start(bf16[2,144,512]{2,1,0:T(8,128)(2,1)} %slice.164), channel_id=1, source_target_pairs={{0,8},{8,0},{16,24},{24,16},{1,9},{9,1},{17,25},{25,17},{2,10},{10... | collective-permute-start | bytes 884744 | tf_op jit(solution)/shard_map/ppermute | solution.py:631
  41.1 20.4 %collective-permute-start.8 = (bf16[2,144,512]{2,1,0:T(8,128)(2,1)S(1)}, bf16[2,144,512]{2,1,0:T(8,128)(2,1)}, u32[]{:S(2)}, u32[]{:S(2)}) collective-permute-start(bf16[2,144,512]{2,1,0:T(8,128)(2,1)S(1)} %slice.163), channel_id=1, source_target_pairs={{0,16},{8,24},{16,0},{24,8},{1,17},{9,25},{17,1},{25,9},{2,18},{10... | collective-permute-start | bytes 884744 | tf_op jit(solution)/shard_map/ppermute | solution.py:630
  65.3 11.2 %collective-permute-start.20 = (bf16[4,144,512]{2,1,0:T(8,128)(2,1)}, bf16[4,144,512]{2,1,0:T(8,128)(2,1)}, u32[]{:S(2)}, u32[]{:S(2)}) collective-permute-start(bf16[4,144,512]{2,1,0:T(8,128)(2,1)} %collective-permute-done.10.refs_5_), channel_id=1, source_target_pairs={{0,1},{1,0},{2,3},{3,2},{4,5},{5,4},{6,7},{7,6},{8,9},{9,8},{10,11... | collective-permute-start | bytes 1769480 | tf_op jit(solution)/shard_map/ppermute | solution.py:659
  128.9 19.6 %collective-permute-start.28 = (bf16[8,144,512]{2,1,0:T(8,128)(2,1)}, bf16[8,144,512]{2,1,0:T(8,128)(2,1)}, u32[]{:S(2)}, u32[]{:S(2)}) collective-permute-start(bf16[8,144,512]{2,1,0:T(8,128)(2,1)} %get-tuple-element.98), channel_id=1, source_target_pairs={{0,1},{1,0},{2,3},{3,2},{4,5},{5,4},{6,7},{7,6},{8,9},{9,8},{10,11... | collective-permute-start | bytes 3538952 | tf_op jit(solution)/shard_map/ppermute | solution.py:674
  133.6 15.6 %collective-permute-start.26 = (bf16[4,144,512]{2,1,0:T(8,128)(2,1)}, bf16[4,144,512]{2,1,0:T(8,128)(2,1)S(1)}, u32[]{:S(2)}, u32[]{:S(2)}) collective-permute-start(bf16[4,144,512]{2,1,0:T(8,128)(2,1)} %add.176), channel_id=1, source_target_pairs={{0,8},{8,0},{16,24},{24,16},{1,9},{9,1},{17,25},{25,17},{2,10},{10... | collective-permute-start | bytes 1769480 | tf_op jit(solution)/shard_map/ppermute | solution.py:676
  134.7 15.4 %collective-permute-start.27 = (bf16[4,144,512]{2,1,0:T(8,128)(2,1)}, bf16[4,144,512]{2,1,0:T(8,128)(2,1)}, u32[]{:S(2)}, u32[]{:S(2)}) collective-permute-start(bf16[4,144,512]{2,1,0:T(8,128)(2,1)} %add.177), channel_id=1, source_target_pairs={{0,16},{8,24},{16,0},{24,8},{1,17},{9,25},{17,1},{25,9},{2,18},{10... | collective-permute-start | bytes 1769480 | tf_op jit(solution)/shard_map/ppermute | solution.py:677
  151.7 9.5 %collective-permute-start.31 = (bf16[2,144,512]{2,1,0:T(8,128)(2,1)S(1)}, bf16[2,144,512]{2,1,0:T(8,128)(2,1)S(1)}, u32[]{:S(2)}, u32[]{:S(2)}) collective-permute-start(bf16[2,144,512]{2,1,0:T(8,128)(2,1)S(1)} %get-tuple-element.131), channel_id=1, source_target_pairs={{0,8},{8,0},{16,24},{24,16},{1,9},{9,1},{17,25},{25,17},{2,10},{10... | collective-permute-start | bytes 884744 | tf_op jit(solution)/shard_map/ppermute | solution.py:682
  152.7 9.1 %collective-permute-start.30 = (bf16[2,144,512]{2,1,0:T(8,128)(2,1)S(1)}, bf16[2,144,512]{2,1,0:T(8,128)(2,1)S(1)}, u32[]{:S(2)}, u32[]{:S(2)}) collective-permute-start(bf16[2,144,512]{2,1,0:T(8,128)(2,1)S(1)} %get-tuple-element.132), channel_id=1, source_target_pairs={{0,16},{8,24},{16,0},{24,8},{1,17},{9,25},{17,1},{25,9},{2,18},{10... | collective-permute-start | bytes 884744 | tf_op jit(solution)/shard_map/ppermute | solution.py:681
  161.8 32.2 %all-to-all-start = ((bf16[4,4,144,512]{3,2,1,0:T(8,128)(2,1)}), bf16[4,4,144,512]{3,2,1,0:T(8,128)(2,1)}, u32[]{:S(2)}, u32[]{:S(2)}) async-start(bf16[4,4,144,512]{3,2,1,0:T(8,128)(2,1)} %bitcast.22), calls=%async_computation | async-start | bytes 4718592 | tf_op jit(solution)/shard_map/all_to_all | solution.py:685
  168.8 20.6 %collective-permute-start.34 = (bf16[144,512]{1,0:T(8,128)(2,1)}, bf16[144,512]{1,0:T(8,128)(2,1)S(1)}, u32[]{:S(2)}, u32[]{:S(2)}) collective-permute-start(bf16[144,512]{1,0:T(8,128)(2,1)} %get-tuple-element.122), channel_id=1, source_target_pairs={{0,6},{1,7},{2,0},{3,1},{4,2},{5,3},{6,4},{7,5},{8,14},{9,15},{10,... | collective-permute-start | bytes 442376 | tf_op jit(solution)/shard_map/ppermute | solution.py:667
  169.6 19.8 %collective-permute-start.33 = (bf16[144,512]{1,0:T(8,128)(2,1)}, bf16[144,512]{1,0:T(8,128)(2,1)S(1)}, u32[]{:S(2)}, u32[]{:S(2)}) collective-permute-start(bf16[144,512]{1,0:T(8,128)(2,1)} %get-tuple-element.123), channel_id=1, source_target_pairs={{0,4},{1,5},{2,6},{3,7},{4,0},{5,1},{6,2},{7,3},{8,12},{9,13},{10,... | collective-permute-start | bytes 442376 | tf_op jit(solution)/shard_map/ppermute | solution.py:667
  171.1 18.2 %collective-permute-start.32 = (bf16[144,512]{1,0:T(8,128)(2,1)S(1)}, bf16[144,512]{1,0:T(8,128)(2,1)S(1)}, u32[]{:S(2)}, u32[]{:S(2)}) collective-permute-start(bf16[144,512]{1,0:T(8,128)(2,1)S(1)} %get-tuple-element.130), channel_id=1, source_target_pairs={{0,2},{1,3},{2,4},{3,5},{4,6},{5,7},{6,0},{7,1},{8,10},{9,11},{10,... | collective-permute-start | bytes 442376 | tf_op jit(solution)/shard_map/ppermute | solution.py:667
  195.9 8.7 %collective-permute-start.35 = (bf16[144,512]{1,0:T(8,128)(2,1)S(1)}, bf16[144,512]{1,0:T(8,128)(2,1)S(1)}, u32[]{:S(2)}, u32[]{:S(2)}) collective-permute-start(bf16[144,512]{1,0:T(8,128)(2,1)S(1)} %get-tuple-element.126), channel_id=1, source_target_pairs={{0,2},{1,3},{2,4},{3,5},{4,6},{5,7},{6,0},{7,1},{8,10},{9,11},{10,... | collective-permute-start | bytes 442376 | tf_op jit(solution)/shard_map/ppermute | solution.py:667
  196.4 12.6 %collective-permute-start.36 = (bf16[144,512]{1,0:T(8,128)(2,1)S(1)}, bf16[144,512]{1,0:T(8,128)(2,1)S(1)}, u32[]{:S(2)}, u32[]{:S(2)}) collective-permute-start(bf16[144,512]{1,0:T(8,128)(2,1)S(1)} %get-tuple-element.127), channel_id=1, source_target_pairs={{0,4},{1,5},{2,6},{3,7},{4,0},{5,1},{6,2},{7,3},{8,12},{9,13},{10,... | collective-permute-start | bytes 442376 | tf_op jit(solution)/shard_map/ppermute | solution.py:667
  198.4 10.6 %collective-permute-start.37 = (bf16[144,512]{1,0:T(8,128)(2,1)S(1)}, bf16[144,512]{1,0:T(8,128)(2,1)S(1)}, u32[]{:S(2)}, u32[]{:S(2)}) collective-permute-start(bf16[144,512]{1,0:T(8,128)(2,1)S(1)} %get-tuple-element.128), channel_id=1, source_target_pairs={{0,6},{1,7},{2,0},{3,1},{4,2},{5,3},{6,4},{7,5},{8,14},{9,15},{10,... | collective-permute-start | bytes 442376 | tf_op jit(solution)/shard_map/ppermute | solution.py:667
  (33 other events, 206.7 us)

commit v5 on v4

--- a/solution.py
+++ b/solution.py
@@ -68,9 +68,9 @@
     return pl.BlockSpec((tile, width), lambda i: (i, 0))
 
 
-def window_bounds(len_ref, position, wins, total):
+def window_reach(len_ref, position, wins, total):
     first = jnp.zeros_like(position)
-    last = jnp.full_like(position, total)
+    last = jnp.full_like(position, total - 1)
     edge = jnp.int32(0)
     edges = []
     for w in range(wins - 1):
@@ -79,8 +79,17 @@
     for edge in edges:
         first = jnp.where(position >= edge, edge, first)
     for edge in reversed(edges):
-        last = jnp.where(position < edge, edge, last)
-    return first, last
+        last = jnp.where(position < edge, edge - 1, last)
+    return position - first, last - position
+
+
+def within(block, reach, tap):
+    shift = (tap - TAPS // 2) * STEP
+    if shift == 0:
+        return block
+    before, after = reach
+    valid = (before >= -shift) if shift < 0 else (after >= shift)
+    return block * wide(jnp.where(valid, 1.0, 0.0).astype(bf16), block.shape[1])
 
 
 def wide(mask, width):
@@ -158,13 +167,11 @@
 
     start = pl.multiple_of(step * tile, tile)
     position = lax.broadcasted_iota(jnp.int32, (tile, 128), 0) + start
-    first, last = window_bounds(len_ref, position, wins, rows)
+    reach = window_reach(len_ref, position, wins, rows)
     per = depth // 128
     for tap in range(TAPS):
-        other = position + (tap - TAPS // 2) * STEP
-        valid = ((other >= first) & (other < last)).astype(bf16)
         offset = pl.multiple_of(start + tap // 2 * 2 * STEP, 2 * STEP)
-        block = (odd if tap % 2 else even)[pl.ds(offset, tile)] * wide(valid, width)
+        block = within((odd if tap % 2 else even)[pl.ds(offset, tile)], reach, tap)
         for lane in range(0, width, 128):
             chunk = (tap * width + lane) // 128
             seat = ((chunk // per) ^ place_ref[2]) * per + chunk % per
@@ -327,9 +334,9 @@
             mixed_ref[part] = (hiddens[at(part)].astype(f32) + normal * gain_two + small_ref[5:6]).astype(bf16)
             cot = cot_ref[part].astype(f32)
             q = cot * gain_two
-            d_outer = (root * (q - mean(q) - normal * mean(q * normal))).astype(bf16)
-            d_outers[at(part)] = d_outer
-            add_tally(3, 0, d_outer.astype(f32))
+            d_outer_full = root * (q - mean(q) - normal * mean(q * normal))
+            d_outers[at(part)] = d_outer_full.astype(bf16)
+            add_tally(3, 0, d_outer_full)
             add_tally(4, 0, cot * normal)
             add_tally(5, 0, cot)
 
@@ -339,9 +346,9 @@
         @pl.when(in_rows)
         def _(j=j, cut=cut):
             for part in slabs(tile, slab):
-                d_inner = (dot_t(d_outers[at(part)], out_rows(j)) * bend[part, cut]).astype(bf16)
-                d_inners[at(part), cut] = d_inner
-                add_tally(6 + j, 0, d_inner.astype(f32))
+                d_inner = dot_t(d_outers[at(part)], out_rows(j)) * bend[part, cut]
+                d_inners[at(part), cut] = d_inner.astype(bf16)
+                add_tally(6 + j, 0, d_inner)
 
     @pl.when(in_rows)
     def _():
@@ -350,48 +357,26 @@
             d_hidden_ref[part] = d_hidden
             first = normed_ref[part]
             p = d_hidden * small_ref[1:2]
-            d_conv = (slope_ref[part] * (p - mean(p) - first * mean(p * first))).astype(bf16)
-            d_conv_ref[part] = d_conv
-            add_tally(0, 0, d_conv.astype(f32))
+            d_conv = slope_ref[part] * (p - mean(p) - first * mean(p * first))
+            d_conv_ref[part] = d_conv.astype(bf16)
+            add_tally(0, 0, d_conv)
             add_tally(1, 0, d_hidden * first)
             add_tally(2, 0, d_hidden)
 
-    def grad_copies():
-        copies = []
-        if not fast:
-            for n, target in enumerate(targets):
-                copies.append(pltpu.make_async_copy(store.at[pl.ds(n, 1)], target, grad_sems.at[n]))
-            return copies
-        for n, which in enumerate((core, 1 - core)):
-            for r in range(4):
-                for k in range(4):
-                    array, seat = relay_seat(r, k)
-                    block = ((place[2] ^ r) * 4 + ((place[1] + k) & 3)) * 2 + which
-                    copies.append(
-                        pltpu.make_async_copy(store.at[block], targets[3 * n + array].at[seat], grad_sems.at[len(copies)])
-                    )
-        return copies
-
-    @pl.when(step >= tiles)
-    def _():
-        j = step - tiles
-        part = pl.ds(pl.multiple_of(j * width, width), width)
-        d_out = dot_rows(actives[:, part], d_outers[...]).astype(bf16)
-        first = top + extra
-        if fast:
-            many = width // outer_rows
-            store[pl.ds(j * many, many), first : first + outer_rows] = d_out.reshape(many, outer_rows, width)
-        else:
-            per = outer_rows // width
-            start = pl.multiple_of(first + (j % per) * width, 16)
-            store[pl.ds(j // per, 1), pl.ds(start, width)] = d_out.reshape(1, width, width)
-        d_in = dot_rows(hiddens[...], d_inners[:, part]).astype(bf16)
-        above = pl.ds(pl.multiple_of(j * inner_rows, inner_rows), inner_rows)
-        store[:, above] = d_in.reshape(blocks, inner_rows, width)
-
-    @pl.when(step == pl.num_programs(0) - 1)
-    def _():
-        back.wait()
+    def put_blocks(dp):
+        for r in range(4):
+
+            @pl.when((dp ^ place[2]) == r)
+            def _(r=r):
+                for n, which in enumerate((core, 1 - core)):
+                    for k in range(4):
+                        array, seat = relay_seat(r, k)
+                        target = targets[3 * n + array].at[seat]
+                        block = (dp * 4 + ((place[1] + k) & 3)) * 2 + which
+                        pltpu.make_async_copy(store.at[block], target, grad_sems.at[dp * 8 + 4 * n + k]).start()
+
+    @pl.when(step == tiles)
+    def _():
         for row in range(sums_ref.shape[0]):
             sums_ref[row : row + 1] = colsum(tallies[8 * row : 8 * row + 8])
         if fast:
@@ -400,11 +385,45 @@
             for dp in range(blocks // 8):
                 line = jnp.concatenate([head, sums_ref[6 + dp : 7 + dp].astype(bf16), rest])
                 store[8 * dp : 8 * dp + 8, top : top + extra] = jnp.broadcast_to(line, (8, extra, width))
-        copies = grad_copies()
-        for copy in copies:
-            copy.start()
-        for copy in copies:
-            copy.wait()
+
+    for j in range(cols):
+        part = slice(j * width, (j + 1) * width)
+
+        @pl.when(step == tiles)
+        def _(j=j, part=part):
+            d_in = dot_rows(hiddens[...], d_inners[:, part]).astype(bf16)
+            store[:, j * inner_rows : (j + 1) * inner_rows] = d_in.reshape(blocks, inner_rows, width)
+
+    for j in range(cols):
+        part = slice(j * width, (j + 1) * width)
+
+        @pl.when(step == tiles)
+        def _(j=j, part=part):
+            d_out = dot_rows(actives[:, part], d_outers[...]).astype(bf16)
+            first = top + extra
+            if fast:
+                many = width // outer_rows
+                store[j * many : (j + 1) * many, first : first + outer_rows] = d_out.reshape(many, outer_rows, width)
+                put_blocks(j)
+            else:
+                per = outer_rows // width
+                start = first + j % per * width
+                store[j // per, start : start + width] = d_out
+
+    @pl.when(step == pl.num_programs(0) - 1)
+    def _():
+        back.wait()
+        if fast:
+            for n in range(blocks):
+                pltpu.make_async_copy(store.at[n], targets[0].at[0], grad_sems.at[n]).wait()
+        else:
+            copies = [
+                pltpu.make_async_copy(store.at[pl.ds(n, 1)], target, grad_sems.at[n]) for n, target in enumerate(targets)
+            ]
+            for copy in copies:
+                copy.start()
+            for copy in copies:
+                copy.wait()
 
 
 def feed(place, far, pieces, stacked, partial, tokens, cotangent, inner_rows, outer_rows, extra, total, fast, body):
@@ -422,7 +441,7 @@
             feed_kernel, far=len(far), count=len(pieces), outs=len(seats), tiles=tiles, chunk=512, inner_rows=inner_rows,
             outer_rows=outer_rows, extra=extra, fast=fast, body=body,
         ),
-        grid=(tiles + cols,),
+        grid=(tiles + 1,),
         in_specs=[SMEM] + [ANY] * (len(far) + len(pieces)) + [last, tall, tall, tall],
         out_specs=[tall, tall, tall, pl.BlockSpec((16, width), lambda i: (0, 0)), ANY] + [ANY] * len(seats),
         out_shape=[
@@ -474,14 +493,12 @@
     width = part.stop - part.start
     core = place[0]
     position = lax.broadcasted_iota(jnp.int32, (rows, 128), 0)
-    first, last = window_bounds(len_ref, position, wins, rows)
+    reach = window_reach(len_ref, position, wins, rows)
     copies = []
     for tap in range(TAPS):
         mirror = TAPS - 1 - tap
-        other = position + (mirror - TAPS // 2) * STEP
-        valid = ((other >= first) & (other < last)).astype(bf16)
         source = (odd if mirror % 2 else even)[mirror // 2 * 2 * STEP : mirror // 2 * 2 * STEP + rows, part]
-        store[tap * channels : (tap + 1) * channels] = dot(masked_ref[...], source * wide(valid, width)).astype(bf16)
+        store[tap * channels : (tap + 1) * channels] = dot(masked_ref[...], within(source, reach, mirror)).astype(bf16)
         while len(copies) // 2 < blocks and (len(copies) // 2 + 1) * 2 * body <= (tap + 1) * channels:
             block = len(copies) // 2
             seat = ((block // 4) ^ turn) * 4 + ((block % 4 - place[1]) & 3) if blocks == 16 else block
@@ -544,14 +561,12 @@
 
     start = pl.multiple_of(step * tile, tile)
     position = lax.broadcasted_iota(jnp.int32, (tile, 128), 0) + start
-    first, last = window_bounds(len_ref, position, wins, rows)
+    reach = window_reach(len_ref, position, wins, rows)
     total = None
     for tap in range(TAPS):
         mirror = TAPS - 1 - tap
-        other_row = position + (mirror - TAPS // 2) * STEP
-        valid = ((other_row >= first) & (other_row < last)).astype(bf16)
         offset = pl.multiple_of(start + mirror // 2 * 2 * STEP, 2 * STEP)
-        block = (odd if mirror % 2 else even)[pl.ds(offset, tile)] * wide(valid, width)
+        block = within((odd if mirror % 2 else even)[pl.ds(offset, tile)], reach, mirror)
         term = dot_t(block, store[tap * width : (tap + 1) * width])
         total = term if total is None else total + term
     d_tokens_ref[...] = d_hidden_ref[...] + total * wide(keep_ref[...], width)

time: 212 us -> 209 us (0.986)
  Pallas kernels: 104 us -> 101 us
    pallas_call x1, Pallas kernels: 51.7 us -> 48.8 us  [feed(): pl.pallas_call(functools.partial(feed_kernel, far=len(far), count=len(pie...]
where the time goes in v5:
time: 209 us; the launch traced here: 208 us
  Pallas kernels  101 us (48%)
  waiting for transfers between devices  43.5 us (21%)
  starting transfers between devices  37.1 us (18%)
  other arithmetic  14.3 us (7%)
  local copies, waits for them, and re-layouts  11.3 us (5%)
    pallas_call x1, Pallas kernels, feed(): pl.pallas_call(functools.partial(feed_kernel, far=len(far), count=len(pie...  48.8 us
    pallas_call x1, Pallas kernels, conv_forward(): pl.pallas_call(functools.partial(conv_kernel, count=len(pieces), fast=fas...  17.9 us
    pallas_call x1, Pallas kernels, token_grad(): pl.pallas_call(functools.partial(token_grad_kernel, wins=lengths.shape[1]...  16.1 us
    ppermute x6, waiting for transfers between devices, from_column(): return [shard] + [lax.ppermute(shard, 'fsdp', along[k]) for k in (1, 2, 3)]  14.1 us
    pallas_call x1, Pallas kernels, conv_grad(): pl.pallas_call(functools.partial(conv_grad_kernel, wins=lengths.shape[1],...  13.3 us
    ppermute x6, starting transfers between devices, line_swap(): lax.ppermute(line[k], 'fsdp', along[k])  9.81 us
    ppermute x6, starting transfers between devices, from_column(): return [shard] + [lax.ppermute(shard, 'fsdp', along[k]) for k in (1, 2, 3)]  8.31 us
    add x4, other arithmetic, added(): return sum((term.astype(f32) for term in terms))  6.05 us
  transfers between devices with their start and end apart: 39, of which 17 were waited for; matrix products, arithmetic and copies ran while one was open for 9% of the time, Pallas kernels for 25%

profile of v5, /device:TPU:0, one launch (start us, length us, event | category | flops | bytes accessed | tf_op | source)
XLA Modules:
  0.0 207.8 jit_solution(8127695172077412733)
XLA Ops:
  0.7 3.1 %collective-permute-start = (bf16[144,512]{1,0:T(8,128)(2,1)}, bf16[144,512]{1,0:T(8,128)(2,1)S(1)}, u32[]{:S(2)}, u32[]{:S(2)}) collective-permute-start(bf16[144,512]{1,0:T(8,128)(2,1)} %param.17), channel_id=1, source_target_pairs={{0,2},{1,3},{2,4},{3,5},{4,6},{5,7},{6,0},{7,1},{8,10},{9,11},{10,... | collective-permute-start | bytes 442376 | tf_op jit(solution)/shard_map/ppermute | solution.py:620
  3.7 2.1 %collective-permute-start.2 = (bf16[144,512]{1,0:T(8,128)(2,1)}, bf16[144,512]{1,0:T(8,128)(2,1)S(1)}, u32[]{:S(2)}, u32[]{:S(2)}) collective-permute-start(bf16[144,512]{1,0:T(8,128)(2,1)} %param.17), channel_id=1, source_target_pairs={{0,6},{1,7},{2,0},{3,1},{4,2},{5,3},{6,4},{7,5},{8,14},{9,15},{10,... | collective-permute-start | bytes 442376 | tf_op jit(solution)/shard_map/ppermute | solution.py:620
  11.4 4.6 %prep.1 = (bf16[2048,512]{1,0:T(8,128)(2,1)}, bf16[512,2048]{1,0:T(8,128)(2,1)}, f32[2048,128]{1,0:T(8,128)}) custom-call(bf16[2048,512]{1,0:T(8,128)(2,1)} %refs_16_.1, s32[4,4,128]{2,1,0:T(4,128)} %bitcast.60), custom_call_target="tpu_custom_call" | custom-call | bytes 786432 | tf_op jit(solution)/shard_map/prep/pallas_call | solution.py:112
  16.0 3.3 %collective-permute-done.1 = bf16[144,512]{1,0:T(8,128)(2,1)S(1)} collective-permute-done((bf16[144,512]{1,0:T(8,128)(2,1)}, bf16[144,512]{1,0:T(8,128)(2,1)S(1)}, u32[]{:S(2)}, u32[]{:S(2)}) %collective-permute-start.1) | collective-permute-done | bytes 147488 | tf_op jit(solution)/shard_map/ppermute | solution.py:620
  24.7 4.3 %collective-permute-done.7 = bf16[144,512]{1,0:T(8,128)(2,1)S(1)} collective-permute-done((bf16[144,512]{1,0:T(8,128)(2,1)S(1)}, bf16[144,512]{1,0:T(8,128)(2,1)S(1)}, u32[]{:S(2)}, u32[]{:S(2)}) %collective-permute-start.7) | collective-permute-done | bytes 147488 | tf_op jit(solution)/shard_map/ppermute | solution.py:620
  28.9 6.5 %collective-permute-done.6 = bf16[144,512]{1,0:T(8,128)(2,1)S(1)} collective-permute-done((bf16[144,512]{1,0:T(8,128)(2,1)S(1)}, bf16[144,512]{1,0:T(8,128)(2,1)S(1)}, u32[]{:S(2)}, u32[]{:S(2)}) %collective-permute-start.6) | collective-permute-done | bytes 147488 | tf_op jit(solution)/shard_map/ppermute | solution.py:620
  43.3 17.9 %conv_forward.1 = (f32[2048,512]{1,0:T(8,128)}, bf16[2048,1152]{1,0:T(8,128)(2,1)}, bf16[3456,512]{1,0:T(8,128)(2,1)}) custom-call(s32[1,4]{1,0:T(1,128)} %len_ref.5, s32[3]{0:T(128)} %pad_add_fusion.place_ref, bf16[4,144,512]{2,1,0:T(8,128)(2,1)} %copy-done.1, bf16[4,144,512]{2,1,0:T(8,128)(2,1)} %copy-done.4, bf16[4,144,512]{2,1,0:T(8,128)(2,1)} %copy-done.3, ...), custom_call_target="tpu_custom_call" | custom-call | flops 113246208 | bytes 786432 | tf_op jit(solution)/shard_map/conv_forward/pallas_call | solution.py:198
  65.5 5.4 %collective-permute-done.18.refs_8_ = bf16[2,144,512]{2,1,0:T(8,128)(2,1)S(1)} collective-permute-done((bf16[2,144,512]{2,1,0:T(8,128)(2,1)S(1)}, bf16[2,144,512]{2,1,0:T(8,128)(2,1)S(1)}, u32[]{:S(2)}, u32[]{:S(2)}) %collective-permute-start.18) | collective-permute-done | bytes 294944 | tf_op jit(solution)/shard_map/ppermute | solution.py:671
  73.1 1.8 collective-permute-done.23.refs_13_
  76.3 48.8 %feed.1 = (bf16[2048,512]{1,0:T(8,128)(2,1)}, f32[2048,512]{1,0:T(8,128)}, bf16[2048,512]{1,0:T(8,128)(2,1)}, f32[16,512]{1,0:T(8,128)}, bf16[1152,512]{1,0:T(8,...) custom-call(s32[3]{0:T(128)} %pad_add_fusion.place_ref, ...), custom_call_target="tpu_custom_call" | custom-call | flops 402653184 | bytes 1310720 | tf_op jit(solution)/shard_map/feed/pallas_call | solution.py:439
  127.4 2.0 add.176
  131.8 13.3 %conv_grad.1 = (bf16[16,144,512]{2,1,0:T(8,128)(2,1)}, bf16[16,144,512]{2,1,0:T(8,128)(2,1)}) custom-call(s32[1,4]{1,0:T(1,128)} %len_ref.5, s32[3]{0:T(128)} %pad_add_fusion.place_ref, bf16[512,2048]{1,0:T(8,128)(2,1)} %get-tuple-element.99.masked_ref, bf16[2048,512]{1,0:T(8,128)(2,1)} %get-tuple-element.110.d_conv_ref), custom_call_target="tpu_custom_call" | custom-call | flops 150994944 | bytes 393216 | tf_op jit(solution)/shard_map/conv_grad/pallas_call | solution.py:524
  151.7 2.2 %add.178 = bf16[16,144,512]{2,1,0:T(8,128)(2,1)} add(bf16[16,144,512]{2,1,0:T(8,128)(2,1)S(1)} %copy-done.2, bf16[16,144,512]{2,1,0:T(8,128)(2,1)S(1)} %collective-permute-done.29) | non-fusion elementwise | flops 1179648 | bytes 7077888 | tf_op jit(solution)/shard_map/add | solution.py:698
  153.9 4.1 %collective-permute-done.31 = bf16[2,144,512]{2,1,0:T(8,128)(2,1)S(1)} collective-permute-done((bf16[2,144,512]{2,1,0:T(8,128)(2,1)S(1)}, bf16[2,144,512]{2,1,0:T(8,128)(2,1)S(1)}, u32[]{:S(2)}, u32[]{:S(2)}) %collective-permute-start.31) | collective-permute-done | bytes 294944 | tf_op jit(solution)/shard_map/ppermute | solution.py:697
  158.6 4.6 %all-to-all-start = ((bf16[4,4,144,512]{3,2,1,0:T(8,128)(2,1)}), bf16[4,4,144,512]{3,2,1,0:T(8,128)(2,1)}, u32[]{:S(2)}, u32[]{:S(2)}) async-start(bf16[4,4,144,512]{3,2,1,0:T(8,128)(2,1)} %bitcast.22), calls=%async_computation | async-start | bytes 4718592 | tf_op jit(solution)/shard_map/all_to_all | solution.py:700
  163.3 2.3 %fusion.5 = (bf16[144,512]{1,0:T(8,128)(2,1)}, bf16[144,512]{1,0:T(8,128)(2,1)}, bf16[144,512]{1,0:T(8,128)(2,1)S(1)}, bf16[144,512]{1,0:T(8,128)(2,1)S(1)}) fusion(bf16[2,144,512]{2,1,0:T(8,128)(2,1)S(1)} %collective-permute-done.31, bf16[4,144,512]{2,1,0:T(8,128)(2,1)} %collective-permute-done.27, bf16[8,144,512]{2,1,0:T(8,128)(2,1)} %collective-permute-done.28, ...), kind=kLoop, calls=%fused_computation.19 | loop fusion | flops 2359296 | bytes 2949120 | tf_op jit(solution)/shard_map/add | solution.py:679
  168.0 2.0 collective-permute-start.32
  170.0 16.1 %token_grad.1 = f32[2048,512]{1,0:T(8,128)} custom-call(s32[1,4]{1,0:T(1,128)} %len_ref.5, s32[3]{0:T(128)} %pad_add_fusion.place_ref, bf16[3456,512]{1,0:T(8,128)(2,1)} %get-tuple-element.89.near_ref, bf16[1152,512]{1,0:T(8,128)(2,1)} %get-tuple-element.90.far_ref, bf16[2048,512]{1,0:T(8,128)(2,1)} %get-tuple-element.110.d_conv_ref, ...), custom_call_target="tpu_custom_call" | custom-call | flops 150994944 | bytes 393216 | tf_op jit(solution)/shard_map/token_grad/pallas_call | solution.py:578
  186.2 4.7 %all-to-all-done = bf16[4,4,144,512]{3,2,1,0:T(8,128)(2,1)} async-done(((bf16[4,4,144,512]{3,2,1,0:T(8,128)(2,1)}), bf16[4,4,144,512]{3,2,1,0:T(8,128)(2,1)}, u32[]{:S(2)}, u32[]{:S(2)}) %all-to-all-start) | async-done | bytes 2359328 | tf_op jit(solution)/shard_map/all_to_all | solution.py:700
  191.0 1.7 fusion.7
  193.2 2.0 collective-permute-start.36
  195.3 2.8 %collective-permute-start.37 = (bf16[144,512]{1,0:T(8,128)(2,1)S(1)}, bf16[144,512]{1,0:T(8,128)(2,1)S(1)}, u32[]{:S(2)}, u32[]{:S(2)}) collective-permute-start(bf16[144,512]{1,0:T(8,128)(2,1)S(1)} %get-tuple-element.128), channel_id=1, source_target_pairs={{0,6},{1,7},{2,0},{3,1},{4,2},{5,3},{6,4},{7,5},{8,14},{9,15},{10,... | collective-permute-start | bytes 442376 | tf_op jit(solution)/shard_map/ppermute | solution.py:682
  201.4 4.4 %collective-permute-done.36 = bf16[144,512]{1,0:T(8,128)(2,1)S(1)} collective-permute-done((bf16[144,512]{1,0:T(8,128)(2,1)S(1)}, bf16[144,512]{1,0:T(8,128)(2,1)S(1)}, u32[]{:S(2)}, u32[]{:S(2)}) %collective-permute-start.36) | collective-permute-done | bytes 147488 | tf_op jit(solution)/shard_map/ppermute | solution.py:682
  205.8 2.0 fusion.1
  (133 shorter events, 44.8 us)
Async XLA Ops:
  0.7 15.4 %collective-permute-start = (bf16[144,512]{1,0:T(8,128)(2,1)}, bf16[144,512]{1,0:T(8,128)(2,1)S(1)}, u32[]{:S(2)}, u32[]{:S(2)}) collective-permute-start(bf16[144,512]{1,0:T(8,128)(2,1)} %param.17), channel_id=1, source_target_pairs={{0,2},{1,3},{2,4},{3,5},{4,6},{5,7},{6,0},{7,1},{8,10},{9,11},{10,... | collective-permute-start | bytes 442376 | tf_op jit(solution)/shard_map/ppermute | solution.py:620
  3.7 12.3 %collective-permute-start.2 = (bf16[144,512]{1,0:T(8,128)(2,1)}, bf16[144,512]{1,0:T(8,128)(2,1)S(1)}, u32[]{:S(2)}, u32[]{:S(2)}) collective-permute-start(bf16[144,512]{1,0:T(8,128)(2,1)} %param.17), channel_id=1, source_target_pairs={{0,6},{1,7},{2,0},{3,1},{4,2},{5,3},{6,4},{7,5},{8,14},{9,15},{10,... | collective-permute-start | bytes 442376 | tf_op jit(solution)/shard_map/ppermute | solution.py:620
  5.8 13.5 %collective-permute-start.1 = (bf16[144,512]{1,0:T(8,128)(2,1)}, bf16[144,512]{1,0:T(8,128)(2,1)S(1)}, u32[]{:S(2)}, u32[]{:S(2)}) collective-permute-start(bf16[144,512]{1,0:T(8,128)(2,1)} %param.17), channel_id=1, source_target_pairs={{0,4},{1,5},{2,6},{3,7},{4,0},{5,1},{6,2},{7,3},{8,12},{9,13},{10,... | collective-permute-start | bytes 442376 | tf_op jit(solution)/shard_map/ppermute | solution.py:620
  19.4 16.1 %collective-permute-start.4 = (bf16[4,144,512]{2,1,0:T(8,128)(2,1)S(1)}, bf16[4,144,512]{2,1,0:T(8,128)(2,1)S(1)}, u32[]{:S(2)}, u32[]{:S(2)}) collective-permute-start(bf16[4,144,512]{2,1,0:T(8,128)(2,1)S(1)} %pad_maximum_fusion.refs_0_), channel_id=1, source_target_pairs={{0,16},{8,24},{16,0},{24,8},{1,17},{9,25},{17,1},{25,9},{2,18},{10... | collective-permute-start | bytes 1769480 | tf_op jit(solution)/shard_map/ppermute | solution.py:638
  21.0 15.0 %collective-permute-start.3 = (bf16[4,144,512]{2,1,0:T(8,128)(2,1)S(1)}, bf16[4,144,512]{2,1,0:T(8,128)(2,1)S(1)}, u32[]{:S(2)}, u32[]{:S(2)}) collective-permute-start(bf16[4,144,512]{2,1,0:T(8,128)(2,1)S(1)} %pad_maximum_fusion.refs_0_), channel_id=1, source_target_pairs={{0,8},{8,0},{16,24},{24,16},{1,9},{9,1},{17,25},{25,17},{2,10},{10... | collective-permute-start | bytes 1769480 | tf_op jit(solution)/shard_map/ppermute | solution.py:637
  24.1 11.4 %collective-permute-start.6 = (bf16[144,512]{1,0:T(8,128)(2,1)S(1)}, bf16[144,512]{1,0:T(8,128)(2,1)S(1)}, u32[]{:S(2)}, u32[]{:S(2)}) collective-permute-start(bf16[144,512]{1,0:T(8,128)(2,1)S(1)} %constant_dynamic-update-slice_fusion), channel_id=1, source_target_pairs={{0,4},{1,5},{2,6},{3,7},{4,0},{5,1},{6,2},{7,3},{8,12},{9,13},{10,... | collective-permute-start | bytes 442376 | tf_op jit(solution)/shard_map/ppermute | solution.py:620
  24.1 11.4 %collective-permute-start.5 = (bf16[144,512]{1,0:T(8,128)(2,1)S(1)}, bf16[144,512]{1,0:T(8,128)(2,1)S(1)}, u32[]{:S(2)}, u32[]{:S(2)}) collective-permute-start(bf16[144,512]{1,0:T(8,128)(2,1)S(1)} %constant_dynamic-update-slice_fusion), channel_id=1, source_target_pairs={{0,2},{1,3},{2,4},{3,5},{4,6},{5,7},{6,0},{7,1},{8,10},{9,11},{10,... | collective-permute-start | bytes 442376 | tf_op jit(solution)/shard_map/ppermute | solution.py:620
  36.6 24.7 %collective-permute-start.11 = (bf16[4,144,512]{2,1,0:T(8,128)(2,1)S(1)}, bf16[4,144,512]{2,1,0:T(8,128)(2,1)}, u32[]{:S(2)}, u32[]{:S(2)}) collective-permute-start(bf16[4,144,512]{2,1,0:T(8,128)(2,1)S(1)} %pad_maximum_fusion.1.refs_4_), channel_id=1, source_target_pairs={{0,16},{8,24},{16,0},{24,8},{1,17},{9,25},{17,1},{25,9},{2,18},{10... | collective-permute-start | bytes 1769480 | tf_op jit(solution)/shard_map/ppermute | solution.py:648
  37.1 24.1 %collective-permute-start.10 = (bf16[4,144,512]{2,1,0:T(8,128)(2,1)S(1)}, bf16[4,144,512]{2,1,0:T(8,128)(2,1)}, u32[]{:S(2)}, u32[]{:S(2)}) collective-permute-start(bf16[4,144,512]{2,1,0:T(8,128)(2,1)S(1)} %pad_maximum_fusion.1.refs_4_), channel_id=1, source_target_pairs={{0,8},{8,0},{16,24},{24,16},{1,9},{9,1},{17,25},{25,17},{2,10},{10... | collective-permute-start | bytes 1769480 | tf_op jit(solution)/shard_map/ppermute | solution.py:648
  39.4 21.8 %collective-permute-start.9 = (bf16[2,144,512]{2,1,0:T(8,128)(2,1)}, bf16[2,144,512]{2,1,0:T(8,128)(2,1)}, u32[]{:S(2)}, u32[]{:S(2)}) collective-permute-start(bf16[2,144,512]{2,1,0:T(8,128)(2,1)} %slice.164), channel_id=1, source_target_pairs={{0,8},{8,0},{16,24},{24,16},{1,9},{9,1},{17,25},{25,17},{2,10},{10... | collective-permute-start | bytes 884744 | tf_op jit(solution)/shard_map/ppermute | solution.py:646
  41.1 20.1 %collective-permute-start.8 = (bf16[2,144,512]{2,1,0:T(8,128)(2,1)S(1)}, bf16[2,144,512]{2,1,0:T(8,128)(2,1)}, u32[]{:S(2)}, u32[]{:S(2)}) collective-permute-start(bf16[2,144,512]{2,1,0:T(8,128)(2,1)S(1)} %slice.163), channel_id=1, source_target_pairs={{0,16},{8,24},{16,0},{24,8},{1,17},{9,25},{17,1},{25,9},{2,18},{10... | collective-permute-start | bytes 884744 | tf_op jit(solution)/shard_map/ppermute | solution.py:645
  65.0 11.2 %collective-permute-start.20 = (bf16[4,144,512]{2,1,0:T(8,128)(2,1)}, bf16[4,144,512]{2,1,0:T(8,128)(2,1)}, u32[]{:S(2)}, u32[]{:S(2)}) collective-permute-start(bf16[4,144,512]{2,1,0:T(8,128)(2,1)} %collective-permute-done.10.refs_5_), channel_id=1, source_target_pairs={{0,1},{1,0},{2,3},{3,2},{4,5},{5,4},{6,7},{7,6},{8,9},{9,8},{10,11... | collective-permute-start | bytes 1769480 | tf_op jit(solution)/shard_map/ppermute | solution.py:674
  125.7 19.4 %collective-permute-start.28 = (bf16[8,144,512]{2,1,0:T(8,128)(2,1)}, bf16[8,144,512]{2,1,0:T(8,128)(2,1)}, u32[]{:S(2)}, u32[]{:S(2)}) collective-permute-start(bf16[8,144,512]{2,1,0:T(8,128)(2,1)} %get-tuple-element.98), channel_id=1, source_target_pairs={{0,1},{1,0},{2,3},{3,2},{4,5},{5,4},{6,7},{7,6},{8,9},{9,8},{10,11... | collective-permute-start | bytes 3538952 | tf_op jit(solution)/shard_map/ppermute | solution.py:689
  130.4 15.6 %collective-permute-start.26 = (bf16[4,144,512]{2,1,0:T(8,128)(2,1)}, bf16[4,144,512]{2,1,0:T(8,128)(2,1)S(1)}, u32[]{:S(2)}, u32[]{:S(2)}) collective-permute-start(bf16[4,144,512]{2,1,0:T(8,128)(2,1)} %add.176), channel_id=1, source_target_pairs={{0,8},{8,0},{16,24},{24,16},{1,9},{9,1},{17,25},{25,17},{2,10},{10... | collective-permute-start | bytes 1769480 | tf_op jit(solution)/shard_map/ppermute | solution.py:691
  131.5 15.4 %collective-permute-start.27 = (bf16[4,144,512]{2,1,0:T(8,128)(2,1)}, bf16[4,144,512]{2,1,0:T(8,128)(2,1)}, u32[]{:S(2)}, u32[]{:S(2)}) collective-permute-start(bf16[4,144,512]{2,1,0:T(8,128)(2,1)} %add.177), channel_id=1, source_target_pairs={{0,16},{8,24},{16,0},{24,8},{1,17},{9,25},{17,1},{25,9},{2,18},{10... | collective-permute-start | bytes 1769480 | tf_op jit(solution)/shard_map/ppermute | solution.py:692
  148.5 9.5 %collective-permute-start.31 = (bf16[2,144,512]{2,1,0:T(8,128)(2,1)S(1)}, bf16[2,144,512]{2,1,0:T(8,128)(2,1)S(1)}, u32[]{:S(2)}, u32[]{:S(2)}) collective-permute-start(bf16[2,144,512]{2,1,0:T(8,128)(2,1)S(1)} %get-tuple-element.131), channel_id=1, source_target_pairs={{0,8},{8,0},{16,24},{24,16},{1,9},{9,1},{17,25},{25,17},{2,10},{10... | collective-permute-start | bytes 884744 | tf_op jit(solution)/shard_map/ppermute | solution.py:697
  149.5 9.1 %collective-permute-start.30 = (bf16[2,144,512]{2,1,0:T(8,128)(2,1)S(1)}, bf16[2,144,512]{2,1,0:T(8,128)(2,1)S(1)}, u32[]{:S(2)}, u32[]{:S(2)}) collective-permute-start(bf16[2,144,512]{2,1,0:T(8,128)(2,1)S(1)} %get-tuple-element.132), channel_id=1, source_target_pairs={{0,16},{8,24},{16,0},{24,8},{1,17},{9,25},{17,1},{25,9},{2,18},{10... | collective-permute-start | bytes 884744 | tf_op jit(solution)/shard_map/ppermute | solution.py:696
  158.6 32.2 %all-to-all-start = ((bf16[4,4,144,512]{3,2,1,0:T(8,128)(2,1)}), bf16[4,4,144,512]{3,2,1,0:T(8,128)(2,1)}, u32[]{:S(2)}, u32[]{:S(2)}) async-start(bf16[4,4,144,512]{3,2,1,0:T(8,128)(2,1)} %bitcast.22), calls=%async_computation | async-start | bytes 4718592 | tf_op jit(solution)/shard_map/all_to_all | solution.py:700
  165.6 20.6 %collective-permute-start.34 = (bf16[144,512]{1,0:T(8,128)(2,1)}, bf16[144,512]{1,0:T(8,128)(2,1)S(1)}, u32[]{:S(2)}, u32[]{:S(2)}) collective-permute-start(bf16[144,512]{1,0:T(8,128)(2,1)} %get-tuple-element.122), channel_id=1, source_target_pairs={{0,6},{1,7},{2,0},{3,1},{4,2},{5,3},{6,4},{7,5},{8,14},{9,15},{10,... | collective-permute-start | bytes 442376 | tf_op jit(solution)/shard_map/ppermute | solution.py:682
  166.4 19.7 %collective-permute-start.33 = (bf16[144,512]{1,0:T(8,128)(2,1)}, bf16[144,512]{1,0:T(8,128)(2,1)S(1)}, u32[]{:S(2)}, u32[]{:S(2)}) collective-permute-start(bf16[144,512]{1,0:T(8,128)(2,1)} %get-tuple-element.123), channel_id=1, source_target_pairs={{0,4},{1,5},{2,6},{3,7},{4,0},{5,1},{6,2},{7,3},{8,12},{9,13},{10,... | collective-permute-start | bytes 442376 | tf_op jit(solution)/shard_map/ppermute | solution.py:682
  168.0 18.2 %collective-permute-start.32 = (bf16[144,512]{1,0:T(8,128)(2,1)S(1)}, bf16[144,512]{1,0:T(8,128)(2,1)S(1)}, u32[]{:S(2)}, u32[]{:S(2)}) collective-permute-start(bf16[144,512]{1,0:T(8,128)(2,1)S(1)} %get-tuple-element.130), channel_id=1, source_target_pairs={{0,2},{1,3},{2,4},{3,5},{4,6},{5,7},{6,0},{7,1},{8,10},{9,11},{10,... | collective-permute-start | bytes 442376 | tf_op jit(solution)/shard_map/ppermute | solution.py:682
  192.7 8.7 %collective-permute-start.35 = (bf16[144,512]{1,0:T(8,128)(2,1)S(1)}, bf16[144,512]{1,0:T(8,128)(2,1)S(1)}, u32[]{:S(2)}, u32[]{:S(2)}) collective-permute-start(bf16[144,512]{1,0:T(8,128)(2,1)S(1)} %get-tuple-element.126), channel_id=1, source_target_pairs={{0,2},{1,3},{2,4},{3,5},{4,6},{5,7},{6,0},{7,1},{8,10},{9,11},{10,... | collective-permute-start | bytes 442376 | tf_op jit(solution)/shard_map/ppermute | solution.py:682
  193.2 12.6 %collective-permute-start.36 = (bf16[144,512]{1,0:T(8,128)(2,1)S(1)}, bf16[144,512]{1,0:T(8,128)(2,1)S(1)}, u32[]{:S(2)}, u32[]{:S(2)}) collective-permute-start(bf16[144,512]{1,0:T(8,128)(2,1)S(1)} %get-tuple-element.127), channel_id=1, source_target_pairs={{0,4},{1,5},{2,6},{3,7},{4,0},{5,1},{6,2},{7,3},{8,12},{9,13},{10,... | collective-permute-start | bytes 442376 | tf_op jit(solution)/shard_map/ppermute | solution.py:682
  195.3 10.6 %collective-permute-start.37 = (bf16[144,512]{1,0:T(8,128)(2,1)S(1)}, bf16[144,512]{1,0:T(8,128)(2,1)S(1)}, u32[]{:S(2)}, u32[]{:S(2)}) collective-permute-start(bf16[144,512]{1,0:T(8,128)(2,1)S(1)} %get-tuple-element.128), channel_id=1, source_target_pairs={{0,6},{1,7},{2,0},{3,1},{4,2},{5,3},{6,4},{7,5},{8,14},{9,15},{10,... | collective-permute-start | bytes 442376 | tf_op jit(solution)/shard_map/ppermute | solution.py:682
  (33 other events, 206.6 us)

commit v6 on v5

--- a/solution.py
+++ b/solution.py
@@ -633,12 +633,12 @@
         lines = jnp.where(own_line, lines, 0)
         ff_own = jnp.concatenate([w_in[:, j * width : (j + 1) * width] for j in range(cols)] + [lines, w_out], axis=0)
         masked, masked_across, keep = prep(tokens, present)
-        column, ff_own, masked, masked_across, keep = bar((column, ff_own, masked, masked_across, keep))
+        column, ff_own, masked, masked_across, keep, place = bar((column, ff_own, masked, masked_across, keep, place))
         beside_x = lax.ppermute(column, "dp", across[1])
         beside_y = lax.ppermute(column, "dp", across[2])
         ff_rest = from_column(ff_own)
-        column, beside_x, beside_y, ff_rest = bar((column, beside_x, beside_y, ff_rest))
         ff_column = jnp.stack(ff_rest)
+        column, beside_x, beside_y, ff_column = bar((column, beside_x, beside_y, ff_column))
         near = (column, beside_x, beside_y)
         near = near + tuple(lax.ppermute(piece, "fsdp", swap) for piece in near)
         far = (

time: 209 us -> 207 us (level)
  waiting for transfers between devices: 43.5 us -> 41.3 us
where the time goes in v6:
time: 207 us; the launch traced here: 206 us
  Pallas kernels  101 us (49%)
  waiting for transfers between devices  41.3 us (20%)
  starting transfers between devices  38.5 us (19%)
  other arithmetic  14.3 us (7%)
  local copies, waits for them, and re-layouts  10.4 us (5%)
    pallas_call x1, Pallas kernels, feed(): pl.pallas_call(functools.partial(feed_kernel, far=len(far), count=len(pie...  48.8 us
    pallas_call x1, Pallas kernels, conv_forward(): pl.pallas_call(functools.partial(conv_kernel, count=len(pieces), fast=fas...  18 us
    pallas_call x1, Pallas kernels, token_grad(): pl.pallas_call(functools.partial(token_grad_kernel, wins=lengths.shape[1]...  16.1 us
    ppermute x6, waiting for transfers between devices, from_column(): return [shard] + [lax.ppermute(shard, 'fsdp', along[k]) for k in (1, 2, 3)]  13.5 us
    pallas_call x1, Pallas kernels, conv_grad(): pl.pallas_call(functools.partial(conv_grad_kernel, wins=lengths.shape[1],...  13.3 us
    ppermute x6, starting transfers between devices, line_swap(): lax.ppermute(line[k], 'fsdp', along[k])  9.84 us
    ppermute x6, starting transfers between devices, from_column(): return [shard] + [lax.ppermute(shard, 'fsdp', along[k]) for k in (1, 2, 3)]  8.31 us
    add x4, other arithmetic, added(): return sum((term.astype(f32) for term in terms))  6.05 us
  transfers between devices with their start and end apart: 39, of which 17 were waited for; matrix products, arithmetic and copies ran while one was open for 9% of the time, Pallas kernels for 25%

profile of v6, /device:TPU:0, one launch (start us, length us, event | category | flops | bytes accessed | tf_op | source)
XLA Modules:
  0.0 206.3 jit_solution(13886395883866403772)
XLA Ops:
  0.7 3.1 %collective-permute-start = (bf16[144,512]{1,0:T(8,128)(2,1)}, bf16[144,512]{1,0:T(8,128)(2,1)S(1)}, u32[]{:S(2)}, u32[]{:S(2)}) collective-permute-start(bf16[144,512]{1,0:T(8,128)(2,1)} %param.17), channel_id=1, source_target_pairs={{0,2},{1,3},{2,4},{3,5},{4,6},{5,7},{6,0},{7,1},{8,10},{9,11},{10,... | collective-permute-start | bytes 442376 | tf_op jit(solution)/shard_map/ppermute | solution.py:620
  3.7 2.1 %collective-permute-start.2 = (bf16[144,512]{1,0:T(8,128)(2,1)}, bf16[144,512]{1,0:T(8,128)(2,1)S(1)}, u32[]{:S(2)}, u32[]{:S(2)}) collective-permute-start(bf16[144,512]{1,0:T(8,128)(2,1)} %param.17), channel_id=1, source_target_pairs={{0,6},{1,7},{2,0},{3,1},{4,2},{5,3},{6,4},{7,5},{8,14},{9,15},{10,... | collective-permute-start | bytes 442376 | tf_op jit(solution)/shard_map/ppermute | solution.py:620
  12.0 4.6 %prep.1 = (bf16[2048,512]{1,0:T(8,128)(2,1)}, bf16[512,2048]{1,0:T(8,128)(2,1)}, f32[2048,128]{1,0:T(8,128)}) custom-call(bf16[2048,512]{1,0:T(8,128)(2,1)} %refs_16_.1, s32[4,4,128]{2,1,0:T(4,128)} %bitcast.60), custom_call_target="tpu_custom_call" | custom-call | bytes 786432 | tf_op jit(solution)/shard_map/prep/pallas_call | solution.py:112
  16.6 2.7 %collective-permute-done.1 = bf16[144,512]{1,0:T(8,128)(2,1)S(1)} collective-permute-done((bf16[144,512]{1,0:T(8,128)(2,1)}, bf16[144,512]{1,0:T(8,128)(2,1)S(1)}, u32[]{:S(2)}, u32[]{:S(2)}) %collective-permute-start.1) | collective-permute-done | bytes 147488 | tf_op jit(solution)/shard_map/ppermute | solution.py:620
  24.7 4.3 %collective-permute-done.7 = bf16[144,512]{1,0:T(8,128)(2,1)S(1)} collective-permute-done((bf16[144,512]{1,0:T(8,128)(2,1)S(1)}, bf16[144,512]{1,0:T(8,128)(2,1)S(1)}, u32[]{:S(2)}, u32[]{:S(2)}) %collective-permute-start.7) | collective-permute-done | bytes 147488 | tf_op jit(solution)/shard_map/ppermute | solution.py:620
  28.9 6.5 %collective-permute-done.6 = bf16[144,512]{1,0:T(8,128)(2,1)S(1)} collective-permute-done((bf16[144,512]{1,0:T(8,128)(2,1)S(1)}, bf16[144,512]{1,0:T(8,128)(2,1)S(1)}, u32[]{:S(2)}, u32[]{:S(2)}) %collective-permute-start.6) | collective-permute-done | bytes 147488 | tf_op jit(solution)/shard_map/ppermute | solution.py:620
  41.6 18.0 %conv_forward.1 = (f32[2048,512]{1,0:T(8,128)}, bf16[2048,1152]{1,0:T(8,128)(2,1)}, bf16[3456,512]{1,0:T(8,128)(2,1)}) custom-call(s32[1,4]{1,0:T(1,128)} %len_ref.5, s32[3]{0:T(128)} %pad_add_fusion.place_ref, bf16[4,144,512]{2,1,0:T(8,128)(2,1)} %copy-done.1, bf16[4,144,512]{2,1,0:T(8,128)(2,1)} %copy-done.4, bf16[4,144,512]{2,1,0:T(8,128)(2,1)} %copy-done.3, ...), custom_call_target="tpu_custom_call" | custom-call | flops 113246208 | bytes 786432 | tf_op jit(solution)/shard_map/conv_forward/pallas_call | solution.py:198
  64.5 4.8 %collective-permute-done.18.refs_8_ = bf16[2,144,512]{2,1,0:T(8,128)(2,1)S(1)} collective-permute-done((bf16[2,144,512]{2,1,0:T(8,128)(2,1)S(1)}, bf16[2,144,512]{2,1,0:T(8,128)(2,1)S(1)}, u32[]{:S(2)}, u32[]{:S(2)}) %collective-permute-start.18) | collective-permute-done | bytes 294944 | tf_op jit(solution)/shard_map/ppermute | solution.py:671
  71.6 1.8 collective-permute-done.23.refs_13_
  74.8 48.8 %feed.1 = (bf16[2048,512]{1,0:T(8,128)(2,1)}, f32[2048,512]{1,0:T(8,128)}, bf16[2048,512]{1,0:T(8,128)(2,1)}, f32[16,512]{1,0:T(8,128)}, bf16[1152,512]{1,0:T(8,...) custom-call(s32[3]{0:T(128)} %pad_add_fusion.place_ref, ...), custom_call_target="tpu_custom_call" | custom-call | flops 402653184 | bytes 1310720 | tf_op jit(solution)/shard_map/feed/pallas_call | solution.py:439
  125.9 2.0 add.176
  130.8 13.3 %conv_grad.1 = (bf16[16,144,512]{2,1,0:T(8,128)(2,1)}, bf16[16,144,512]{2,1,0:T(8,128)(2,1)}) custom-call(s32[1,4]{1,0:T(1,128)} %len_ref.5, s32[3]{0:T(128)} %pad_add_fusion.place_ref, bf16[512,2048]{1,0:T(8,128)(2,1)} %get-tuple-element.95.masked_ref, bf16[2048,512]{1,0:T(8,128)(2,1)} %get-tuple-element.106.d_conv_ref), custom_call_target="tpu_custom_call" | custom-call | flops 150994944 | bytes 393216 | tf_op jit(solution)/shard_map/conv_grad/pallas_call | solution.py:524
  150.1 2.2 %add.178 = bf16[16,144,512]{2,1,0:T(8,128)(2,1)} add(bf16[16,144,512]{2,1,0:T(8,128)(2,1)S(1)} %copy-done.2, bf16[16,144,512]{2,1,0:T(8,128)(2,1)S(1)} %collective-permute-done.29) | non-fusion elementwise | flops 1179648 | bytes 7077888 | tf_op jit(solution)/shard_map/add | solution.py:698
  152.3 4.1 %collective-permute-done.31 = bf16[2,144,512]{2,1,0:T(8,128)(2,1)S(1)} collective-permute-done((bf16[2,144,512]{2,1,0:T(8,128)(2,1)S(1)}, bf16[2,144,512]{2,1,0:T(8,128)(2,1)S(1)}, u32[]{:S(2)}, u32[]{:S(2)}) %collective-permute-start.31) | collective-permute-done | bytes 294944 | tf_op jit(solution)/shard_map/ppermute | solution.py:697
  157.1 4.6 %all-to-all-start = ((bf16[4,4,144,512]{3,2,1,0:T(8,128)(2,1)}), bf16[4,4,144,512]{3,2,1,0:T(8,128)(2,1)}, u32[]{:S(2)}, u32[]{:S(2)}) async-start(bf16[4,4,144,512]{3,2,1,0:T(8,128)(2,1)} %bitcast.22), calls=%async_computation | async-start | bytes 4718592 | tf_op jit(solution)/shard_map/all_to_all | solution.py:700
  161.8 2.3 %fusion.5 = (bf16[144,512]{1,0:T(8,128)(2,1)}, bf16[144,512]{1,0:T(8,128)(2,1)}, bf16[144,512]{1,0:T(8,128)(2,1)S(1)}, bf16[144,512]{1,0:T(8,128)(2,1)S(1)}) fusion(bf16[2,144,512]{2,1,0:T(8,128)(2,1)S(1)} %collective-permute-done.31, bf16[4,144,512]{2,1,0:T(8,128)(2,1)} %collective-permute-done.27, bf16[8,144,512]{2,1,0:T(8,128)(2,1)} %collective-permute-done.28, ...), kind=kLoop, calls=%fused_computation.19 | loop fusion | flops 2359296 | bytes 2949120 | tf_op jit(solution)/shard_map/add | solution.py:679
  166.5 2.0 collective-permute-start.32
  168.5 16.1 %token_grad.1 = f32[2048,512]{1,0:T(8,128)} custom-call(s32[1,4]{1,0:T(1,128)} %len_ref.5, s32[3]{0:T(128)} %pad_add_fusion.place_ref, bf16[3456,512]{1,0:T(8,128)(2,1)} %get-tuple-element.85.near_ref, bf16[1152,512]{1,0:T(8,128)(2,1)} %get-tuple-element.86.far_ref, bf16[2048,512]{1,0:T(8,128)(2,1)} %get-tuple-element.106.d_conv_ref, ...), custom_call_target="tpu_custom_call" | custom-call | flops 150994944 | bytes 393216 | tf_op jit(solution)/shard_map/token_grad/pallas_call | solution.py:578
  184.7 4.7 %all-to-all-done = bf16[4,4,144,512]{3,2,1,0:T(8,128)(2,1)} async-done(((bf16[4,4,144,512]{3,2,1,0:T(8,128)(2,1)}), bf16[4,4,144,512]{3,2,1,0:T(8,128)(2,1)}, u32[]{:S(2)}, u32[]{:S(2)}) %all-to-all-start) | async-done | bytes 2359328 | tf_op jit(solution)/shard_map/all_to_all | solution.py:700
  189.5 1.7 fusion.7
  191.8 2.0 collective-permute-start.36
  193.8 2.8 %collective-permute-start.37 = (bf16[144,512]{1,0:T(8,128)(2,1)S(1)}, bf16[144,512]{1,0:T(8,128)(2,1)S(1)}, u32[]{:S(2)}, u32[]{:S(2)}) collective-permute-start(bf16[144,512]{1,0:T(8,128)(2,1)S(1)} %get-tuple-element.124), channel_id=1, source_target_pairs={{0,6},{1,7},{2,0},{3,1},{4,2},{5,3},{6,4},{7,5},{8,14},{9,15},{10,... | collective-permute-start | bytes 442376 | tf_op jit(solution)/shard_map/ppermute | solution.py:682
  199.9 4.4 %collective-permute-done.36 = bf16[144,512]{1,0:T(8,128)(2,1)S(1)} collective-permute-done((bf16[144,512]{1,0:T(8,128)(2,1)S(1)}, bf16[144,512]{1,0:T(8,128)(2,1)S(1)}, u32[]{:S(2)}, u32[]{:S(2)}) %collective-permute-start.36) | collective-permute-done | bytes 147488 | tf_op jit(solution)/shard_map/ppermute | solution.py:682
  204.3 2.0 fusion.1
  (133 shorter events, 44.4 us)
Async XLA Ops:
  0.7 15.9 %collective-permute-start = (bf16[144,512]{1,0:T(8,128)(2,1)}, bf16[144,512]{1,0:T(8,128)(2,1)S(1)}, u32[]{:S(2)}, u32[]{:S(2)}) collective-permute-start(bf16[144,512]{1,0:T(8,128)(2,1)} %param.17), channel_id=1, source_target_pairs={{0,2},{1,3},{2,4},{3,5},{4,6},{5,7},{6,0},{7,1},{8,10},{9,11},{10,... | collective-permute-start | bytes 442376 | tf_op jit(solution)/shard_map/ppermute | solution.py:620
  3.7 12.9 %collective-permute-start.2 = (bf16[144,512]{1,0:T(8,128)(2,1)}, bf16[144,512]{1,0:T(8,128)(2,1)S(1)}, u32[]{:S(2)}, u32[]{:S(2)}) collective-permute-start(bf16[144,512]{1,0:T(8,128)(2,1)} %param.17), channel_id=1, source_target_pairs={{0,6},{1,7},{2,0},{3,1},{4,2},{5,3},{6,4},{7,5},{8,14},{9,15},{10,... | collective-permute-start | bytes 442376 | tf_op jit(solution)/shard_map/ppermute | solution.py:620
  5.8 13.5 %collective-permute-start.1 = (bf16[144,512]{1,0:T(8,128)(2,1)}, bf16[144,512]{1,0:T(8,128)(2,1)S(1)}, u32[]{:S(2)}, u32[]{:S(2)}) collective-permute-start(bf16[144,512]{1,0:T(8,128)(2,1)} %param.17), channel_id=1, source_target_pairs={{0,4},{1,5},{2,6},{3,7},{4,0},{5,1},{6,2},{7,3},{8,12},{9,13},{10,... | collective-permute-start | bytes 442376 | tf_op jit(solution)/shard_map/ppermute | solution.py:620
  19.4 16.2 %collective-permute-start.4 = (bf16[4,144,512]{2,1,0:T(8,128)(2,1)S(1)}, bf16[4,144,512]{2,1,0:T(8,128)(2,1)S(1)}, u32[]{:S(2)}, u32[]{:S(2)}) collective-permute-start(bf16[4,144,512]{2,1,0:T(8,128)(2,1)S(1)} %pad_maximum_fusion.refs_0_), channel_id=1, source_target_pairs={{0,16},{8,24},{16,0},{24,8},{1,17},{9,25},{17,1},{25,9},{2,18},{10... | collective-permute-start | bytes 1769480 | tf_op jit(solution)/shard_map/ppermute | solution.py:638
  21.0 15.0 %collective-permute-start.3 = (bf16[4,144,512]{2,1,0:T(8,128)(2,1)S(1)}, bf16[4,144,512]{2,1,0:T(8,128)(2,1)S(1)}, u32[]{:S(2)}, u32[]{:S(2)}) collective-permute-start(bf16[4,144,512]{2,1,0:T(8,128)(2,1)S(1)} %pad_maximum_fusion.refs_0_), channel_id=1, source_target_pairs={{0,8},{8,0},{16,24},{24,16},{1,9},{9,1},{17,25},{25,17},{2,10},{10... | collective-permute-start | bytes 1769480 | tf_op jit(solution)/shard_map/ppermute | solution.py:637
  24.1 11.4 %collective-permute-start.6 = (bf16[144,512]{1,0:T(8,128)(2,1)S(1)}, bf16[144,512]{1,0:T(8,128)(2,1)S(1)}, u32[]{:S(2)}, u32[]{:S(2)}) collective-permute-start(bf16[144,512]{1,0:T(8,128)(2,1)S(1)} %constant_dynamic-update-slice_fusion), channel_id=1, source_target_pairs={{0,4},{1,5},{2,6},{3,7},{4,0},{5,1},{6,2},{7,3},{8,12},{9,13},{10,... | collective-permute-start | bytes 442376 | tf_op jit(solution)/shard_map/ppermute | solution.py:620
  24.1 11.4 %collective-permute-start.5 = (bf16[144,512]{1,0:T(8,128)(2,1)S(1)}, bf16[144,512]{1,0:T(8,128)(2,1)S(1)}, u32[]{:S(2)}, u32[]{:S(2)}) collective-permute-start(bf16[144,512]{1,0:T(8,128)(2,1)S(1)} %constant_dynamic-update-slice_fusion), channel_id=1, source_target_pairs={{0,2},{1,3},{2,4},{3,5},{4,6},{5,7},{6,0},{7,1},{8,10},{9,11},{10,... | collective-permute-start | bytes 442376 | tf_op jit(solution)/shard_map/ppermute | solution.py:620
  36.5 23.2 %collective-permute-start.11 = (bf16[4,144,512]{2,1,0:T(8,128)(2,1)S(1)}, bf16[4,144,512]{2,1,0:T(8,128)(2,1)}, u32[]{:S(2)}, u32[]{:S(2)}) collective-permute-start(bf16[4,144,512]{2,1,0:T(8,128)(2,1)S(1)} %pad_maximum_fusion.1.refs_4_), channel_id=1, source_target_pairs={{0,16},{8,24},{16,0},{24,8},{1,17},{9,25},{17,1},{25,9},{2,18},{10... | collective-permute-start | bytes 1769480 | tf_op jit(solution)/shard_map/ppermute | solution.py:648
  37.0 22.7 %collective-permute-start.10 = (bf16[4,144,512]{2,1,0:T(8,128)(2,1)S(1)}, bf16[4,144,512]{2,1,0:T(8,128)(2,1)}, u32[]{:S(2)}, u32[]{:S(2)}) collective-permute-start(bf16[4,144,512]{2,1,0:T(8,128)(2,1)S(1)} %pad_maximum_fusion.1.refs_4_), channel_id=1, source_target_pairs={{0,8},{8,0},{16,24},{24,16},{1,9},{9,1},{17,25},{25,17},{2,10},{10... | collective-permute-start | bytes 1769480 | tf_op jit(solution)/shard_map/ppermute | solution.py:648
  39.2 20.4 %collective-permute-start.9 = (bf16[2,144,512]{2,1,0:T(8,128)(2,1)}, bf16[2,144,512]{2,1,0:T(8,128)(2,1)}, u32[]{:S(2)}, u32[]{:S(2)}) collective-permute-start(bf16[2,144,512]{2,1,0:T(8,128)(2,1)} %slice.164), channel_id=1, source_target_pairs={{0,8},{8,0},{16,24},{24,16},{1,9},{9,1},{17,25},{25,17},{2,10},{10... | collective-permute-start | bytes 884744 | tf_op jit(solution)/shard_map/ppermute | solution.py:646
  40.1 19.5 %collective-permute-start.8 = (bf16[2,144,512]{2,1,0:T(8,128)(2,1)S(1)}, bf16[2,144,512]{2,1,0:T(8,128)(2,1)}, u32[]{:S(2)}, u32[]{:S(2)}) collective-permute-start(bf16[2,144,512]{2,1,0:T(8,128)(2,1)S(1)} %slice.163), channel_id=1, source_target_pairs={{0,16},{8,24},{16,0},{24,8},{1,17},{9,25},{17,1},{25,9},{2,18},{10... | collective-permute-start | bytes 884744 | tf_op jit(solution)/shard_map/ppermute | solution.py:645
  64.0 10.7 %collective-permute-start.20 = (bf16[4,144,512]{2,1,0:T(8,128)(2,1)}, bf16[4,144,512]{2,1,0:T(8,128)(2,1)}, u32[]{:S(2)}, u32[]{:S(2)}) collective-permute-start(bf16[4,144,512]{2,1,0:T(8,128)(2,1)} %collective-permute-done.10.refs_5_), channel_id=1, source_target_pairs={{0,1},{1,0},{2,3},{3,2},{4,5},{5,4},{6,7},{7,6},{8,9},{9,8},{10,11... | collective-permute-start | bytes 1769480 | tf_op jit(solution)/shard_map/ppermute | solution.py:674
  124.2 19.9 %collective-permute-start.28 = (bf16[8,144,512]{2,1,0:T(8,128)(2,1)}, bf16[8,144,512]{2,1,0:T(8,128)(2,1)}, u32[]{:S(2)}, u32[]{:S(2)}) collective-permute-start(bf16[8,144,512]{2,1,0:T(8,128)(2,1)} %get-tuple-element.94), channel_id=1, source_target_pairs={{0,1},{1,0},{2,3},{3,2},{4,5},{5,4},{6,7},{7,6},{8,9},{9,8},{10,11... | collective-permute-start | bytes 3538952 | tf_op jit(solution)/shard_map/ppermute | solution.py:689
  128.9 15.6 %collective-permute-start.26 = (bf16[4,144,512]{2,1,0:T(8,128)(2,1)}, bf16[4,144,512]{2,1,0:T(8,128)(2,1)S(1)}, u32[]{:S(2)}, u32[]{:S(2)}) collective-permute-start(bf16[4,144,512]{2,1,0:T(8,128)(2,1)} %add.176), channel_id=1, source_target_pairs={{0,8},{8,0},{16,24},{24,16},{1,9},{9,1},{17,25},{25,17},{2,10},{10... | collective-permute-start | bytes 1769480 | tf_op jit(solution)/shard_map/ppermute | solution.py:691
  129.9 15.4 %collective-permute-start.27 = (bf16[4,144,512]{2,1,0:T(8,128)(2,1)}, bf16[4,144,512]{2,1,0:T(8,128)(2,1)}, u32[]{:S(2)}, u32[]{:S(2)}) collective-permute-start(bf16[4,144,512]{2,1,0:T(8,128)(2,1)} %add.177), channel_id=1, source_target_pairs={{0,16},{8,24},{16,0},{24,8},{1,17},{9,25},{17,1},{25,9},{2,18},{10... | collective-permute-start | bytes 1769480 | tf_op jit(solution)/shard_map/ppermute | solution.py:692
  146.9 9.5 %collective-permute-start.31 = (bf16[2,144,512]{2,1,0:T(8,128)(2,1)S(1)}, bf16[2,144,512]{2,1,0:T(8,128)(2,1)S(1)}, u32[]{:S(2)}, u32[]{:S(2)}) collective-permute-start(bf16[2,144,512]{2,1,0:T(8,128)(2,1)S(1)} %get-tuple-element.127), channel_id=1, source_target_pairs={{0,8},{8,0},{16,24},{24,16},{1,9},{9,1},{17,25},{25,17},{2,10},{10... | collective-permute-start | bytes 884744 | tf_op jit(solution)/shard_map/ppermute | solution.py:697
  148.0 9.1 %collective-permute-start.30 = (bf16[2,144,512]{2,1,0:T(8,128)(2,1)S(1)}, bf16[2,144,512]{2,1,0:T(8,128)(2,1)S(1)}, u32[]{:S(2)}, u32[]{:S(2)}) collective-permute-start(bf16[2,144,512]{2,1,0:T(8,128)(2,1)S(1)} %get-tuple-element.128), channel_id=1, source_target_pairs={{0,16},{8,24},{16,0},{24,8},{1,17},{9,25},{17,1},{25,9},{2,18},{10... | collective-permute-start | bytes 884744 | tf_op jit(solution)/shard_map/ppermute | solution.py:696
  157.1 32.2 %all-to-all-start = ((bf16[4,4,144,512]{3,2,1,0:T(8,128)(2,1)}), bf16[4,4,144,512]{3,2,1,0:T(8,128)(2,1)}, u32[]{:S(2)}, u32[]{:S(2)}) async-start(bf16[4,4,144,512]{3,2,1,0:T(8,128)(2,1)} %bitcast.22), calls=%async_computation | async-start | bytes 4718592 | tf_op jit(solution)/shard_map/all_to_all | solution.py:700
  164.0 20.6 %collective-permute-start.34 = (bf16[144,512]{1,0:T(8,128)(2,1)}, bf16[144,512]{1,0:T(8,128)(2,1)S(1)}, u32[]{:S(2)}, u32[]{:S(2)}) collective-permute-start(bf16[144,512]{1,0:T(8,128)(2,1)} %get-tuple-element.118), channel_id=1, source_target_pairs={{0,6},{1,7},{2,0},{3,1},{4,2},{5,3},{6,4},{7,5},{8,14},{9,15},{10,... | collective-permute-start | bytes 442376 | tf_op jit(solution)/shard_map/ppermute | solution.py:682
  164.9 19.8 %collective-permute-start.33 = (bf16[144,512]{1,0:T(8,128)(2,1)}, bf16[144,512]{1,0:T(8,128)(2,1)S(1)}, u32[]{:S(2)}, u32[]{:S(2)}) collective-permute-start(bf16[144,512]{1,0:T(8,128)(2,1)} %get-tuple-element.119), channel_id=1, source_target_pairs={{0,4},{1,5},{2,6},{3,7},{4,0},{5,1},{6,2},{7,3},{8,12},{9,13},{10,... | collective-permute-start | bytes 442376 | tf_op jit(solution)/shard_map/ppermute | solution.py:682
  166.5 18.2 %collective-permute-start.32 = (bf16[144,512]{1,0:T(8,128)(2,1)S(1)}, bf16[144,512]{1,0:T(8,128)(2,1)S(1)}, u32[]{:S(2)}, u32[]{:S(2)}) collective-permute-start(bf16[144,512]{1,0:T(8,128)(2,1)S(1)} %get-tuple-element.126), channel_id=1, source_target_pairs={{0,2},{1,3},{2,4},{3,5},{4,6},{5,7},{6,0},{7,1},{8,10},{9,11},{10,... | collective-permute-start | bytes 442376 | tf_op jit(solution)/shard_map/ppermute | solution.py:682
  191.2 8.7 %collective-permute-start.35 = (bf16[144,512]{1,0:T(8,128)(2,1)S(1)}, bf16[144,512]{1,0:T(8,128)(2,1)S(1)}, u32[]{:S(2)}, u32[]{:S(2)}) collective-permute-start(bf16[144,512]{1,0:T(8,128)(2,1)S(1)} %get-tuple-element.122), channel_id=1, source_target_pairs={{0,2},{1,3},{2,4},{3,5},{4,6},{5,7},{6,0},{7,1},{8,10},{9,11},{10,... | collective-permute-start | bytes 442376 | tf_op jit(solution)/shard_map/ppermute | solution.py:682
  191.8 12.5 %collective-permute-start.36 = (bf16[144,512]{1,0:T(8,128)(2,1)S(1)}, bf16[144,512]{1,0:T(8,128)(2,1)S(1)}, u32[]{:S(2)}, u32[]{:S(2)}) collective-permute-start(bf16[144,512]{1,0:T(8,128)(2,1)S(1)} %get-tuple-element.123), channel_id=1, source_target_pairs={{0,4},{1,5},{2,6},{3,7},{4,0},{5,1},{6,2},{7,3},{8,12},{9,13},{10,... | collective-permute-start | bytes 442376 | tf_op jit(solution)/shard_map/ppermute | solution.py:682
  193.8 10.5 %collective-permute-start.37 = (bf16[144,512]{1,0:T(8,128)(2,1)S(1)}, bf16[144,512]{1,0:T(8,128)(2,1)S(1)}, u32[]{:S(2)}, u32[]{:S(2)}) collective-permute-start(bf16[144,512]{1,0:T(8,128)(2,1)S(1)} %get-tuple-element.124), channel_id=1, source_target_pairs={{0,6},{1,7},{2,0},{3,1},{4,2},{5,3},{6,4},{7,5},{8,14},{9,15},{10,... | collective-permute-start | bytes 442376 | tf_op jit(solution)/shard_map/ppermute | solution.py:682
  (33 other events, 203.4 us)

commit v7 on v6

--- a/solution.py
+++ b/solution.py
@@ -325,7 +325,7 @@
     @pl.when(in_rows)
     def _():
         gain_two = small_ref[4:5]
-        for part in slabs(tile, slab):
+        for part in slabs(tile, slab // 2):
             full = packed[:, top + extra :].reshape(blocks * outer_rows, width)
             outer = dot(actives[at(part)], full) + small_ref[3:4]
             shifted = outer - mean(outer)

time: 207 us -> 207 us (level)
  no operation moved by 1% of the time
where the time goes in v7:
time: 207 us; the launch traced here: 206 us
  Pallas kernels  100 us (48%)
  waiting for transfers between devices  41.2 us (20%)
  starting transfers between devices  38.6 us (19%)
  other arithmetic  14.3 us (7%)
  local copies, waits for them, and re-layouts  10.4 us (5%)
    pallas_call x1, Pallas kernels, feed(): pl.pallas_call(functools.partial(feed_kernel, far=len(far), count=len(pie...  48.4 us
    pallas_call x1, Pallas kernels, conv_forward(): pl.pallas_call(functools.partial(conv_kernel, count=len(pieces), fast=fas...  18 us
    pallas_call x1, Pallas kernels, token_grad(): pl.pallas_call(functools.partial(token_grad_kernel, wins=lengths.shape[1]...  16.1 us
    ppermute x6, waiting for transfers between devices, from_column(): return [shard] + [lax.ppermute(shard, 'fsdp', along[k]) for k in (1, 2, 3)]  13.5 us
    pallas_call x1, Pallas kernels, conv_grad(): pl.pallas_call(functools.partial(conv_grad_kernel, wins=lengths.shape[1],...  13.3 us
    ppermute x6, starting transfers between devices, line_swap(): lax.ppermute(line[k], 'fsdp', along[k])  9.88 us
    ppermute x6, starting transfers between devices, from_column(): return [shard] + [lax.ppermute(shard, 'fsdp', along[k]) for k in (1, 2, 3)]  8.31 us
    add x4, other arithmetic, added(): return sum((term.astype(f32) for term in terms))  6.05 us
  transfers between devices with their start and end apart: 39, of which 17 were waited for; matrix products, arithmetic and copies ran while one was open for 9% of the time, Pallas kernels for 25%

profile of v7, /device:TPU:0, one launch (start us, length us, event | category | flops | bytes accessed | tf_op | source)
XLA Modules:
  0.0 205.9 jit_solution(5579031744375442771)
XLA Ops:
  0.7 3.1 %collective-permute-start = (bf16[144,512]{1,0:T(8,128)(2,1)}, bf16[144,512]{1,0:T(8,128)(2,1)S(1)}, u32[]{:S(2)}, u32[]{:S(2)}) collective-permute-start(bf16[144,512]{1,0:T(8,128)(2,1)} %param.17), channel_id=1, source_target_pairs={{0,2},{1,3},{2,4},{3,5},{4,6},{5,7},{6,0},{7,1},{8,10},{9,11},{10,... | collective-permute-start | bytes 442376 | tf_op jit(solution)/shard_map/ppermute | solution.py:620
  3.7 2.1 %collective-permute-start.2 = (bf16[144,512]{1,0:T(8,128)(2,1)}, bf16[144,512]{1,0:T(8,128)(2,1)S(1)}, u32[]{:S(2)}, u32[]{:S(2)}) collective-permute-start(bf16[144,512]{1,0:T(8,128)(2,1)} %param.17), channel_id=1, source_target_pairs={{0,6},{1,7},{2,0},{3,1},{4,2},{5,3},{6,4},{7,5},{8,14},{9,15},{10,... | collective-permute-start | bytes 442376 | tf_op jit(solution)/shard_map/ppermute | solution.py:620
  12.0 4.6 %prep.1 = (bf16[2048,512]{1,0:T(8,128)(2,1)}, bf16[512,2048]{1,0:T(8,128)(2,1)}, f32[2048,128]{1,0:T(8,128)}) custom-call(bf16[2048,512]{1,0:T(8,128)(2,1)} %refs_16_.1, s32[4,4,128]{2,1,0:T(4,128)} %bitcast.60), custom_call_target="tpu_custom_call" | custom-call | bytes 786432 | tf_op jit(solution)/shard_map/prep/pallas_call | solution.py:112
  16.6 2.7 %collective-permute-done.1 = bf16[144,512]{1,0:T(8,128)(2,1)S(1)} collective-permute-done((bf16[144,512]{1,0:T(8,128)(2,1)}, bf16[144,512]{1,0:T(8,128)(2,1)S(1)}, u32[]{:S(2)}, u32[]{:S(2)}) %collective-permute-start.1) | collective-permute-done | bytes 147488 | tf_op jit(solution)/shard_map/ppermute | solution.py:620
  24.7 4.3 %collective-permute-done.7 = bf16[144,512]{1,0:T(8,128)(2,1)S(1)} collective-permute-done((bf16[144,512]{1,0:T(8,128)(2,1)S(1)}, bf16[144,512]{1,0:T(8,128)(2,1)S(1)}, u32[]{:S(2)}, u32[]{:S(2)}) %collective-permute-start.7) | collective-permute-done | bytes 147488 | tf_op jit(solution)/shard_map/ppermute | solution.py:620
  28.9 6.5 %collective-permute-done.6 = bf16[144,512]{1,0:T(8,128)(2,1)S(1)} collective-permute-done((bf16[144,512]{1,0:T(8,128)(2,1)S(1)}, bf16[144,512]{1,0:T(8,128)(2,1)S(1)}, u32[]{:S(2)}, u32[]{:S(2)}) %collective-permute-start.6) | collective-permute-done | bytes 147488 | tf_op jit(solution)/shard_map/ppermute | solution.py:620
  41.6 18.0 %conv_forward.1 = (f32[2048,512]{1,0:T(8,128)}, bf16[2048,1152]{1,0:T(8,128)(2,1)}, bf16[3456,512]{1,0:T(8,128)(2,1)}) custom-call(s32[1,4]{1,0:T(1,128)} %len_ref.5, s32[3]{0:T(128)} %pad_add_fusion.place_ref, bf16[4,144,512]{2,1,0:T(8,128)(2,1)} %copy-done.1, bf16[4,144,512]{2,1,0:T(8,128)(2,1)} %copy-done.4, bf16[4,144,512]{2,1,0:T(8,128)(2,1)} %copy-done.3, ...), custom_call_target="tpu_custom_call" | custom-call | flops 113246208 | bytes 786432 | tf_op jit(solution)/shard_map/conv_forward/pallas_call | solution.py:198
  64.5 4.8 %collective-permute-done.18.refs_8_ = bf16[2,144,512]{2,1,0:T(8,128)(2,1)S(1)} collective-permute-done((bf16[2,144,512]{2,1,0:T(8,128)(2,1)S(1)}, bf16[2,144,512]{2,1,0:T(8,128)(2,1)S(1)}, u32[]{:S(2)}, u32[]{:S(2)}) %collective-permute-start.18) | collective-permute-done | bytes 294944 | tf_op jit(solution)/shard_map/ppermute | solution.py:671
  71.6 1.8 collective-permute-done.23.refs_13_
  74.8 48.4 %feed.1 = (bf16[2048,512]{1,0:T(8,128)(2,1)}, f32[2048,512]{1,0:T(8,128)}, bf16[2048,512]{1,0:T(8,128)(2,1)}, f32[16,512]{1,0:T(8,128)}, bf16[1152,512]{1,0:T(8,...) custom-call(s32[3]{0:T(128)} %pad_add_fusion.place_ref, ...), custom_call_target="tpu_custom_call" | custom-call | flops 402653184 | bytes 1310720 | tf_op jit(solution)/shard_map/feed/pallas_call | solution.py:439
  125.5 2.0 add.176
  130.4 13.3 %conv_grad.1 = (bf16[16,144,512]{2,1,0:T(8,128)(2,1)}, bf16[16,144,512]{2,1,0:T(8,128)(2,1)}) custom-call(s32[1,4]{1,0:T(1,128)} %len_ref.5, s32[3]{0:T(128)} %pad_add_fusion.place_ref, bf16[512,2048]{1,0:T(8,128)(2,1)} %get-tuple-element.95.masked_ref, bf16[2048,512]{1,0:T(8,128)(2,1)} %get-tuple-element.106.d_conv_ref), custom_call_target="tpu_custom_call" | custom-call | flops 150994944 | bytes 393216 | tf_op jit(solution)/shard_map/conv_grad/pallas_call | solution.py:524
  149.7 2.2 %add.178 = bf16[16,144,512]{2,1,0:T(8,128)(2,1)} add(bf16[16,144,512]{2,1,0:T(8,128)(2,1)S(1)} %copy-done.2, bf16[16,144,512]{2,1,0:T(8,128)(2,1)S(1)} %collective-permute-done.29) | non-fusion elementwise | flops 1179648 | bytes 7077888 | tf_op jit(solution)/shard_map/add | solution.py:698
  151.9 4.1 %collective-permute-done.31 = bf16[2,144,512]{2,1,0:T(8,128)(2,1)S(1)} collective-permute-done((bf16[2,144,512]{2,1,0:T(8,128)(2,1)S(1)}, bf16[2,144,512]{2,1,0:T(8,128)(2,1)S(1)}, u32[]{:S(2)}, u32[]{:S(2)}) %collective-permute-start.31) | collective-permute-done | bytes 294944 | tf_op jit(solution)/shard_map/ppermute | solution.py:697
  156.7 4.6 %all-to-all-start = ((bf16[4,4,144,512]{3,2,1,0:T(8,128)(2,1)}), bf16[4,4,144,512]{3,2,1,0:T(8,128)(2,1)}, u32[]{:S(2)}, u32[]{:S(2)}) async-start(bf16[4,4,144,512]{3,2,1,0:T(8,128)(2,1)} %bitcast.22), calls=%async_computation | async-start | bytes 4718592 | tf_op jit(solution)/shard_map/all_to_all | solution.py:700
  161.4 2.3 %fusion.5 = (bf16[144,512]{1,0:T(8,128)(2,1)}, bf16[144,512]{1,0:T(8,128)(2,1)}, bf16[144,512]{1,0:T(8,128)(2,1)S(1)}, bf16[144,512]{1,0:T(8,128)(2,1)S(1)}) fusion(bf16[2,144,512]{2,1,0:T(8,128)(2,1)S(1)} %collective-permute-done.31, bf16[4,144,512]{2,1,0:T(8,128)(2,1)} %collective-permute-done.27, bf16[8,144,512]{2,1,0:T(8,128)(2,1)} %collective-permute-done.28, ...), kind=kLoop, calls=%fused_computation.19 | loop fusion | flops 2359296 | bytes 2949120 | tf_op jit(solution)/shard_map/add | solution.py:679
  166.1 2.0 collective-permute-start.32
  168.1 16.1 %token_grad.1 = f32[2048,512]{1,0:T(8,128)} custom-call(s32[1,4]{1,0:T(1,128)} %len_ref.5, s32[3]{0:T(128)} %pad_add_fusion.place_ref, bf16[3456,512]{1,0:T(8,128)(2,1)} %get-tuple-element.85.near_ref, bf16[1152,512]{1,0:T(8,128)(2,1)} %get-tuple-element.86.far_ref, bf16[2048,512]{1,0:T(8,128)(2,1)} %get-tuple-element.106.d_conv_ref, ...), custom_call_target="tpu_custom_call" | custom-call | flops 150994944 | bytes 393216 | tf_op jit(solution)/shard_map/token_grad/pallas_call | solution.py:578
  184.3 4.7 %all-to-all-done = bf16[4,4,144,512]{3,2,1,0:T(8,128)(2,1)} async-done(((bf16[4,4,144,512]{3,2,1,0:T(8,128)(2,1)}), bf16[4,4,144,512]{3,2,1,0:T(8,128)(2,1)}, u32[]{:S(2)}, u32[]{:S(2)}) %all-to-all-start) | async-done | bytes 2359328 | tf_op jit(solution)/shard_map/all_to_all | solution.py:700
  189.1 1.7 fusion.7
  191.4 2.0 collective-permute-start.36
  193.4 2.8 %collective-permute-start.37 = (bf16[144,512]{1,0:T(8,128)(2,1)S(1)}, bf16[144,512]{1,0:T(8,128)(2,1)S(1)}, u32[]{:S(2)}, u32[]{:S(2)}) collective-permute-start(bf16[144,512]{1,0:T(8,128)(2,1)S(1)} %get-tuple-element.124), channel_id=1, source_target_pairs={{0,6},{1,7},{2,0},{3,1},{4,2},{5,3},{6,4},{7,5},{8,14},{9,15},{10,... | collective-permute-start | bytes 442376 | tf_op jit(solution)/shard_map/ppermute | solution.py:682
  199.5 4.4 %collective-permute-done.36 = bf16[144,512]{1,0:T(8,128)(2,1)S(1)} collective-permute-done((bf16[144,512]{1,0:T(8,128)(2,1)S(1)}, bf16[144,512]{1,0:T(8,128)(2,1)S(1)}, u32[]{:S(2)}, u32[]{:S(2)}) %collective-permute-start.36) | collective-permute-done | bytes 147488 | tf_op jit(solution)/shard_map/ppermute | solution.py:682
  203.9 2.0 fusion.1
  (133 shorter events, 44.4 us)
Async XLA Ops:
  0.7 15.9 %collective-permute-start = (bf16[144,512]{1,0:T(8,128)(2,1)}, bf16[144,512]{1,0:T(8,128)(2,1)S(1)}, u32[]{:S(2)}, u32[]{:S(2)}) collective-permute-start(bf16[144,512]{1,0:T(8,128)(2,1)} %param.17), channel_id=1, source_target_pairs={{0,2},{1,3},{2,4},{3,5},{4,6},{5,7},{6,0},{7,1},{8,10},{9,11},{10,... | collective-permute-start | bytes 442376 | tf_op jit(solution)/shard_map/ppermute | solution.py:620
  3.7 12.9 %collective-permute-start.2 = (bf16[144,512]{1,0:T(8,128)(2,1)}, bf16[144,512]{1,0:T(8,128)(2,1)S(1)}, u32[]{:S(2)}, u32[]{:S(2)}) collective-permute-start(bf16[144,512]{1,0:T(8,128)(2,1)} %param.17), channel_id=1, source_target_pairs={{0,6},{1,7},{2,0},{3,1},{4,2},{5,3},{6,4},{7,5},{8,14},{9,15},{10,... | collective-permute-start | bytes 442376 | tf_op jit(solution)/shard_map/ppermute | solution.py:620
  5.8 13.5 %collective-permute-start.1 = (bf16[144,512]{1,0:T(8,128)(2,1)}, bf16[144,512]{1,0:T(8,128)(2,1)S(1)}, u32[]{:S(2)}, u32[]{:S(2)}) collective-permute-start(bf16[144,512]{1,0:T(8,128)(2,1)} %param.17), channel_id=1, source_target_pairs={{0,4},{1,5},{2,6},{3,7},{4,0},{5,1},{6,2},{7,3},{8,12},{9,13},{10,... | collective-permute-start | bytes 442376 | tf_op jit(solution)/shard_map/ppermute | solution.py:620
  19.4 16.2 %collective-permute-start.4 = (bf16[4,144,512]{2,1,0:T(8,128)(2,1)S(1)}, bf16[4,144,512]{2,1,0:T(8,128)(2,1)S(1)}, u32[]{:S(2)}, u32[]{:S(2)}) collective-permute-start(bf16[4,144,512]{2,1,0:T(8,128)(2,1)S(1)} %pad_maximum_fusion.refs_0_), channel_id=1, source_target_pairs={{0,16},{8,24},{16,0},{24,8},{1,17},{9,25},{17,1},{25,9},{2,18},{10... | collective-permute-start | bytes 1769480 | tf_op jit(solution)/shard_map/ppermute | solution.py:638
  21.0 15.0 %collective-permute-start.3 = (bf16[4,144,512]{2,1,0:T(8,128)(2,1)S(1)}, bf16[4,144,512]{2,1,0:T(8,128)(2,1)S(1)}, u32[]{:S(2)}, u32[]{:S(2)}) collective-permute-start(bf16[4,144,512]{2,1,0:T(8,128)(2,1)S(1)} %pad_maximum_fusion.refs_0_), channel_id=1, source_target_pairs={{0,8},{8,0},{16,24},{24,16},{1,9},{9,1},{17,25},{25,17},{2,10},{10... | collective-permute-start | bytes 1769480 | tf_op jit(solution)/shard_map/ppermute | solution.py:637
  24.1 11.4 %collective-permute-start.6 = (bf16[144,512]{1,0:T(8,128)(2,1)S(1)}, bf16[144,512]{1,0:T(8,128)(2,1)S(1)}, u32[]{:S(2)}, u32[]{:S(2)}) collective-permute-start(bf16[144,512]{1,0:T(8,128)(2,1)S(1)} %constant_dynamic-update-slice_fusion), channel_id=1, source_target_pairs={{0,4},{1,5},{2,6},{3,7},{4,0},{5,1},{6,2},{7,3},{8,12},{9,13},{10,... | collective-permute-start | bytes 442376 | tf_op jit(solution)/shard_map/ppermute | solution.py:620
  24.1 11.4 %collective-permute-start.5 = (bf16[144,512]{1,0:T(8,128)(2,1)S(1)}, bf16[144,512]{1,0:T(8,128)(2,1)S(1)}, u32[]{:S(2)}, u32[]{:S(2)}) collective-permute-start(bf16[144,512]{1,0:T(8,128)(2,1)S(1)} %constant_dynamic-update-slice_fusion), channel_id=1, source_target_pairs={{0,2},{1,3},{2,4},{3,5},{4,6},{5,7},{6,0},{7,1},{8,10},{9,11},{10,... | collective-permute-start | bytes 442376 | tf_op jit(solution)/shard_map/ppermute | solution.py:620
  36.5 23.2 %collective-permute-start.11 = (bf16[4,144,512]{2,1,0:T(8,128)(2,1)S(1)}, bf16[4,144,512]{2,1,0:T(8,128)(2,1)}, u32[]{:S(2)}, u32[]{:S(2)}) collective-permute-start(bf16[4,144,512]{2,1,0:T(8,128)(2,1)S(1)} %pad_maximum_fusion.1.refs_4_), channel_id=1, source_target_pairs={{0,16},{8,24},{16,0},{24,8},{1,17},{9,25},{17,1},{25,9},{2,18},{10... | collective-permute-start | bytes 1769480 | tf_op jit(solution)/shard_map/ppermute | solution.py:648
  37.0 22.7 %collective-permute-start.10 = (bf16[4,144,512]{2,1,0:T(8,128)(2,1)S(1)}, bf16[4,144,512]{2,1,0:T(8,128)(2,1)}, u32[]{:S(2)}, u32[]{:S(2)}) collective-permute-start(bf16[4,144,512]{2,1,0:T(8,128)(2,1)S(1)} %pad_maximum_fusion.1.refs_4_), channel_id=1, source_target_pairs={{0,8},{8,0},{16,24},{24,16},{1,9},{9,1},{17,25},{25,17},{2,10},{10... | collective-permute-start | bytes 1769480 | tf_op jit(solution)/shard_map/ppermute | solution.py:648
  39.2 20.4 %collective-permute-start.9 = (bf16[2,144,512]{2,1,0:T(8,128)(2,1)}, bf16[2,144,512]{2,1,0:T(8,128)(2,1)}, u32[]{:S(2)}, u32[]{:S(2)}) collective-permute-start(bf16[2,144,512]{2,1,0:T(8,128)(2,1)} %slice.164), channel_id=1, source_target_pairs={{0,8},{8,0},{16,24},{24,16},{1,9},{9,1},{17,25},{25,17},{2,10},{10... | collective-permute-start | bytes 884744 | tf_op jit(solution)/shard_map/ppermute | solution.py:646
  40.1 19.5 %collective-permute-start.8 = (bf16[2,144,512]{2,1,0:T(8,128)(2,1)S(1)}, bf16[2,144,512]{2,1,0:T(8,128)(2,1)}, u32[]{:S(2)}, u32[]{:S(2)}) collective-permute-start(bf16[2,144,512]{2,1,0:T(8,128)(2,1)S(1)} %slice.163), channel_id=1, source_target_pairs={{0,16},{8,24},{16,0},{24,8},{1,17},{9,25},{17,1},{25,9},{2,18},{10... | collective-permute-start | bytes 884744 | tf_op jit(solution)/shard_map/ppermute | solution.py:645
  64.0 10.7 %collective-permute-start.20 = (bf16[4,144,512]{2,1,0:T(8,128)(2,1)}, bf16[4,144,512]{2,1,0:T(8,128)(2,1)}, u32[]{:S(2)}, u32[]{:S(2)}) collective-permute-start(bf16[4,144,512]{2,1,0:T(8,128)(2,1)} %collective-permute-done.10.refs_5_), channel_id=1, source_target_pairs={{0,1},{1,0},{2,3},{3,2},{4,5},{5,4},{6,7},{7,6},{8,9},{9,8},{10,11... | collective-permute-start | bytes 1769480 | tf_op jit(solution)/shard_map/ppermute | solution.py:674
  123.8 19.9 %collective-permute-start.28 = (bf16[8,144,512]{2,1,0:T(8,128)(2,1)}, bf16[8,144,512]{2,1,0:T(8,128)(2,1)}, u32[]{:S(2)}, u32[]{:S(2)}) collective-permute-start(bf16[8,144,512]{2,1,0:T(8,128)(2,1)} %get-tuple-element.94), channel_id=1, source_target_pairs={{0,1},{1,0},{2,3},{3,2},{4,5},{5,4},{6,7},{7,6},{8,9},{9,8},{10,11... | collective-permute-start | bytes 3538952 | tf_op jit(solution)/shard_map/ppermute | solution.py:689
  128.5 15.6 %collective-permute-start.26 = (bf16[4,144,512]{2,1,0:T(8,128)(2,1)}, bf16[4,144,512]{2,1,0:T(8,128)(2,1)S(1)}, u32[]{:S(2)}, u32[]{:S(2)}) collective-permute-start(bf16[4,144,512]{2,1,0:T(8,128)(2,1)} %add.176), channel_id=1, source_target_pairs={{0,8},{8,0},{16,24},{24,16},{1,9},{9,1},{17,25},{25,17},{2,10},{10... | collective-permute-start | bytes 1769480 | tf_op jit(solution)/shard_map/ppermute | solution.py:691
  129.5 15.4 %collective-permute-start.27 = (bf16[4,144,512]{2,1,0:T(8,128)(2,1)}, bf16[4,144,512]{2,1,0:T(8,128)(2,1)}, u32[]{:S(2)}, u32[]{:S(2)}) collective-permute-start(bf16[4,144,512]{2,1,0:T(8,128)(2,1)} %add.177), channel_id=1, source_target_pairs={{0,16},{8,24},{16,0},{24,8},{1,17},{9,25},{17,1},{25,9},{2,18},{10... | collective-permute-start | bytes 1769480 | tf_op jit(solution)/shard_map/ppermute | solution.py:692
  146.5 9.5 %collective-permute-start.31 = (bf16[2,144,512]{2,1,0:T(8,128)(2,1)S(1)}, bf16[2,144,512]{2,1,0:T(8,128)(2,1)S(1)}, u32[]{:S(2)}, u32[]{:S(2)}) collective-permute-start(bf16[2,144,512]{2,1,0:T(8,128)(2,1)S(1)} %get-tuple-element.127), channel_id=1, source_target_pairs={{0,8},{8,0},{16,24},{24,16},{1,9},{9,1},{17,25},{25,17},{2,10},{10... | collective-permute-start | bytes 884744 | tf_op jit(solution)/shard_map/ppermute | solution.py:697
  147.6 9.1 %collective-permute-start.30 = (bf16[2,144,512]{2,1,0:T(8,128)(2,1)S(1)}, bf16[2,144,512]{2,1,0:T(8,128)(2,1)S(1)}, u32[]{:S(2)}, u32[]{:S(2)}) collective-permute-start(bf16[2,144,512]{2,1,0:T(8,128)(2,1)S(1)} %get-tuple-element.128), channel_id=1, source_target_pairs={{0,16},{8,24},{16,0},{24,8},{1,17},{9,25},{17,1},{25,9},{2,18},{10... | collective-permute-start | bytes 884744 | tf_op jit(solution)/shard_map/ppermute | solution.py:696
  156.7 32.2 %all-to-all-start = ((bf16[4,4,144,512]{3,2,1,0:T(8,128)(2,1)}), bf16[4,4,144,512]{3,2,1,0:T(8,128)(2,1)}, u32[]{:S(2)}, u32[]{:S(2)}) async-start(bf16[4,4,144,512]{3,2,1,0:T(8,128)(2,1)} %bitcast.22), calls=%async_computation | async-start | bytes 4718592 | tf_op jit(solution)/shard_map/all_to_all | solution.py:700
  163.6 20.6 %collective-permute-start.34 = (bf16[144,512]{1,0:T(8,128)(2,1)}, bf16[144,512]{1,0:T(8,128)(2,1)S(1)}, u32[]{:S(2)}, u32[]{:S(2)}) collective-permute-start(bf16[144,512]{1,0:T(8,128)(2,1)} %get-tuple-element.118), channel_id=1, source_target_pairs={{0,6},{1,7},{2,0},{3,1},{4,2},{5,3},{6,4},{7,5},{8,14},{9,15},{10,... | collective-permute-start | bytes 442376 | tf_op jit(solution)/shard_map/ppermute | solution.py:682
  164.5 19.8 %collective-permute-start.33 = (bf16[144,512]{1,0:T(8,128)(2,1)}, bf16[144,512]{1,0:T(8,128)(2,1)S(1)}, u32[]{:S(2)}, u32[]{:S(2)}) collective-permute-start(bf16[144,512]{1,0:T(8,128)(2,1)} %get-tuple-element.119), channel_id=1, source_target_pairs={{0,4},{1,5},{2,6},{3,7},{4,0},{5,1},{6,2},{7,3},{8,12},{9,13},{10,... | collective-permute-start | bytes 442376 | tf_op jit(solution)/shard_map/ppermute | solution.py:682
  166.1 18.2 %collective-permute-start.32 = (bf16[144,512]{1,0:T(8,128)(2,1)S(1)}, bf16[144,512]{1,0:T(8,128)(2,1)S(1)}, u32[]{:S(2)}, u32[]{:S(2)}) collective-permute-start(bf16[144,512]{1,0:T(8,128)(2,1)S(1)} %get-tuple-element.126), channel_id=1, source_target_pairs={{0,2},{1,3},{2,4},{3,5},{4,6},{5,7},{6,0},{7,1},{8,10},{9,11},{10,... | collective-permute-start | bytes 442376 | tf_op jit(solution)/shard_map/ppermute | solution.py:682
  190.8 8.7 %collective-permute-start.35 = (bf16[144,512]{1,0:T(8,128)(2,1)S(1)}, bf16[144,512]{1,0:T(8,128)(2,1)S(1)}, u32[]{:S(2)}, u32[]{:S(2)}) collective-permute-start(bf16[144,512]{1,0:T(8,128)(2,1)S(1)} %get-tuple-element.122), channel_id=1, source_target_pairs={{0,2},{1,3},{2,4},{3,5},{4,6},{5,7},{6,0},{7,1},{8,10},{9,11},{10,... | collective-permute-start | bytes 442376 | tf_op jit(solution)/shard_map/ppermute | solution.py:682
  191.4 12.5 %collective-permute-start.36 = (bf16[144,512]{1,0:T(8,128)(2,1)S(1)}, bf16[144,512]{1,0:T(8,128)(2,1)S(1)}, u32[]{:S(2)}, u32[]{:S(2)}) collective-permute-start(bf16[144,512]{1,0:T(8,128)(2,1)S(1)} %get-tuple-element.123), channel_id=1, source_target_pairs={{0,4},{1,5},{2,6},{3,7},{4,0},{5,1},{6,2},{7,3},{8,12},{9,13},{10,... | collective-permute-start | bytes 442376 | tf_op jit(solution)/shard_map/ppermute | solution.py:682
  193.4 10.5 %collective-permute-start.37 = (bf16[144,512]{1,0:T(8,128)(2,1)S(1)}, bf16[144,512]{1,0:T(8,128)(2,1)S(1)}, u32[]{:S(2)}, u32[]{:S(2)}) collective-permute-start(bf16[144,512]{1,0:T(8,128)(2,1)S(1)} %get-tuple-element.124), channel_id=1, source_target_pairs={{0,6},{1,7},{2,0},{3,1},{4,2},{5,3},{6,4},{7,5},{8,14},{9,15},{10,... | collective-permute-start | bytes 442376 | tf_op jit(solution)/shard_map/ppermute | solution.py:682
  (33 other events, 203.3 us)
